TPU v7x, 32 devices: a whole 2x2x4 slice. The times are simulated.
32 devices in a mesh: dp: 8 (over z, x), shard: 4 (over y, core).
Axes of the slice: x: 2, y: 2, z: 4, core: 2. Of those that a mesh axis runs over, the one named last changes fastest.
Arguments:
- tokens: bfloat16 [8192, 2048], P(('dp', 'shard')), may hold values from -6 to 6
- ctx_cotangent: bfloat16 [8192, 1024], P(('dp', 'shard')), may hold values from -0.59765625 to 0.59765625
- latent_cache: bfloat16 [1024, 128, 896], P('dp', 'shard'), may hold values from -300 to 300
- nbr_ids: int32 [128, 2], P(('dp', 'shard')), may hold values from 0 to 1023, as said below
- w_query: bfloat16 [2048, 1024], P('shard'), may hold values from -0.125 to 0.125
- w_key: bfloat16 [896, 1024], P('shard'), may hold values from -0.1875 to 0.1875
- w_value: bfloat16 [896, 1024], P('shard'), may hold values from -0.1875 to 0.1875
Outputs:
- context: bfloat16 [8192, 1024], P(('dp', 'shard'))
- grad_query: float32 [2048, 1024], P(('dp', 'shard'))
- grad_key: float32 [896, 1024], P(('dp', 'shard'))
- grad_value: float32 [896, 1024], P(('dp', 'shard'))
Inputs may be any that keep to these rules, and one draw needn't show every extreme that they name: Row r of latent_cache is owned by index r // 128 of dp. Within the 32 ids of one index of dp (its devices' nbr_ids in row-major order), at most 8 name rows of one owner, and in every draw one owner is named exactly 8 times by every index of dp. Ids may repeat.
All inputs are finite; a program needn't handle non-finite values.
Results may differ from a plain program's by a relative error of at most 0.0055.
The roundings to bfloat16 on the way count: a program that leaves them out, or rounds other values in their place, can miss the bound.
Values may be sent and summed in bfloat16 or wider, within the bound.
No kernel may reach another device: no remote copies, remote signals or barrier semaphores. Data moves between devices by JAX's collectives and lax.ppermute only.
A program may use at most 128 MiB of HBM per device.

v0:
```python
import jax
import jax.numpy as jnp
from jax import lax
from jax.sharding import PartitionSpec as P

LAT = 896
HEADS = 8
HEAD_DIM = 128
SPAN = 64
NBR = 2
NT = 128
CH_DEV = 4
INNER = 1024


def body(tokens, ctx_cotangent, latent_cache, nbr_ids, w_query, w_key, w_value):
    softmax_scale = HEAD_DIM ** (-0.5)
    owner_count = lax.axis_size("dp")
    shard_count = lax.axis_size("shard")
    owner_rows = latent_cache.shape[0]
    slice_tokens = latent_cache.shape[1]
    requests = nbr_ids.reshape(-1)
    gathered = lax.all_gather(requests, "shard", axis=0, tiled=True)
    slot_count = 2 * gathered.shape[0] // owner_count
    owner_of = gathered // owner_rows
    within_row = gathered % owner_rows
    onehot = (owner_of[:, None] == jnp.arange(owner_count, dtype=jnp.int32)[None, :]).astype(
        jnp.int32
    )
    earlier = jnp.cumsum(onehot, axis=0) - onehot
    position = jnp.sum(earlier * onehot, axis=1)
    slot_of = owner_of * slot_count + position
    outgoing = jnp.zeros((owner_count * slot_count,), jnp.int32).at[slot_of].set(within_row)
    outgoing = outgoing.reshape(owner_count, slot_count)
    asked_rows = lax.all_to_all(outgoing, "dp", split_axis=0, concat_axis=0, tiled=True)
    fetched = latent_cache[asked_rows.reshape(-1)]
    fetched = fetched.reshape(asked_rows.shape[0], asked_rows.shape[1], slice_tokens, LAT)
    replies = lax.all_to_all(fetched, "dp", split_axis=0, concat_axis=0, tiled=True)
    arrived = replies.reshape(owner_count * slot_count, slice_tokens, LAT)
    chosen = arrived[slot_of].reshape(shard_count, -1, slice_tokens, LAT)
    latents = lax.all_to_all(chosen, "shard", split_axis=0, concat_axis=2, tiled=True)
    latent_rows = latents.reshape(-1, LAT)
    columns = latent_rows
    key_sum = jnp.dot(
        columns,
        lax.all_gather(w_key, "shard", axis=0, tiled=True),
        preferred_element_type=jnp.float32,
    )
    value_sum = jnp.dot(
        columns,
        lax.all_gather(w_value, "shard", axis=0, tiled=True),
        preferred_element_type=jnp.float32,
    )
    key_rows = key_sum.astype(jnp.bfloat16)
    value_rows = value_sum.astype(jnp.bfloat16)
    as_float = tokens.astype(jnp.float32)
    normed = (
        as_float * lax.rsqrt(jnp.mean(as_float * as_float, axis=-1, keepdims=True) + 1e-06)
    ).astype(jnp.bfloat16)
    columns = normed
    query_sum = jnp.dot(
        columns,
        lax.all_gather(w_query, "shard", axis=0, tiled=True),
        preferred_element_type=jnp.float32,
    )
    queries = (query_sum * softmax_scale).astype(jnp.bfloat16)
    query_heads = queries.reshape(CH_DEV, SPAN, HEADS, HEAD_DIM)
    key_heads = key_rows.reshape(CH_DEV, NBR * NT, HEADS, HEAD_DIM)
    value_heads = value_rows.reshape(CH_DEV, NBR * NT, HEADS, HEAD_DIM)
    scores = jnp.einsum(
        "cmhd,cnhd->chmn", query_heads, key_heads, preferred_element_type=jnp.float32
    )
    highest = jnp.max(scores, axis=-1, keepdims=True)
    exp_scores = jnp.exp(scores - highest)
    attn_prob = exp_scores / jnp.sum(exp_scores, axis=-1, keepdims=True)
    prob_round = attn_prob.astype(jnp.bfloat16)
    context = jnp.einsum(
        "chmn,cnhd->cmhd", prob_round, value_heads, preferred_element_type=jnp.float32
    ).astype(jnp.bfloat16)
    grad_heads = ctx_cotangent.reshape(CH_DEV, SPAN, HEADS, HEAD_DIM)
    value_grad = jnp.einsum(
        "chmn,cmhd->cnhd", prob_round, grad_heads, preferred_element_type=jnp.float32
    ).astype(jnp.bfloat16)
    prob_grad = jnp.einsum(
        "cmhd,cnhd->chmn", grad_heads, value_heads, preferred_element_type=jnp.float32
    )
    score_grad = attn_prob * (prob_grad - jnp.sum(attn_prob * prob_grad, axis=-1, keepdims=True))
    score_grad = score_grad.astype(jnp.bfloat16)
    query_grad = (
        jnp.einsum("chmn,cnhd->cmhd", score_grad, key_heads, preferred_element_type=jnp.float32)
        * softmax_scale
    ).astype(jnp.bfloat16)
    key_grad = jnp.einsum(
        "chmn,cmhd->cnhd", score_grad, query_heads, preferred_element_type=jnp.float32
    ).astype(jnp.bfloat16)
    query_grad = query_grad.reshape(-1, INNER)
    key_grad = key_grad.reshape(-1, INNER)
    value_grad = value_grad.reshape(-1, INNER)
    term_query = jnp.einsum("td,te->de", normed, query_grad, preferred_element_type=jnp.float32)
    term_key = jnp.einsum("tl,te->le", latent_rows, key_grad, preferred_element_type=jnp.float32)
    term_value = jnp.einsum(
        "tl,te->le", latent_rows, value_grad, preferred_element_type=jnp.float32
    )
    grad_query, grad_key, grad_value = (
        lax.psum_scatter(term_query, ("dp", "shard"), scatter_dimension=0, tiled=True),
        lax.psum_scatter(term_key, ("dp", "shard"), scatter_dimension=0, tiled=True),
        lax.psum_scatter(term_value, ("dp", "shard"), scatter_dimension=0, tiled=True),
    )
    return (context.reshape(-1, INNER), grad_query, grad_key, grad_value)


def solution(mesh):
    return jax.shard_map(
        body,
        mesh=mesh,
        in_specs=(
            P(("dp", "shard"), None),
            P(("dp", "shard"), None),
            P("dp", "shard", None),
            P(("dp", "shard"), None),
            P("shard", None),
            P("shard", None),
            P("shard", None),
        ),
        out_specs=(
            P(("dp", "shard"), None),
            P(("dp", "shard"), None),
            P(("dp", "shard"), None),
            P(("dp", "shard"), None),
        ),
        check_vma=False,
    )
```

profile of v0, /device:TPU:0, one launch (start us, length us, event | category | flops | bytes accessed | tf_op | source)
XLA Modules:
  0.0 411.0 jit_solution(14408894791960943330)
XLA Ops:
  7.2 0.7 all-gather.6.cloned.1.call-update
  7.9 0.8 copy.47
  8.8 1.2 dynamic-slice
  10.9 6.4 %all-reduce = s32[32]{0:T(128)S(1)} all-reduce(s32[32]{0:T(128)S(1)} %dynamic-update-slice), channel_id=1, replica_groups=mesh['dp'=8,'shard'=4] {'shard'}, use_global_device_ids=true, to_apply=%add | all-reduce | flops 32 | bytes 256
  17.6 0.7 scatter_custom_fusion
  18.4 12.1 %all_to_all.29 = s32[8,1,8]{2,1,0:T(1,128)S(1)} all-to-all(s32[8,1,8]{2,1,0:T(1,128)S(1)} %bitcast.97), channel_id=1, replica_groups=mesh['dp'=8,'shard'=4] {'dp'}, dimensions={0} | all-to-all | bytes 512 | tf_op jit(solution)/shard_map/all_to_all | solution.py:35
  31.7 6.0 %gather_fusion = bf16[64,32,896]{2,1,0:T(8,128)(2,1)} fusion(bf16[128,32,896]{2,1,0:T(8,128)(2,1)} %param.9, s32[1024]{0:T(1024)S(1)} %pad_clamp_fusion.1), kind=kCustom, calls=%fused_computation | custom fusion | bytes 7340288 | tf_op jit(solution)/shard_map/gather | solution.py:36
  37.7 4.5 %all-to-all-start.1 = ((bf16[8,8,32,896]{3,2,1,0:T(8,128)(2,1)}), bf16[8,8,32,896]{3,2,1,0:T(8,128)(2,1)}, u32[]{:S(2)}, u32[]{:S(2)}) async-start(bf16[8,8,32,896]{3,2,1,0:T(8,128)(2,1)} %bitcast.76), calls=%async_computation.1 | async-start | bytes 7340032 | tf_op jit(solution)/shard_map/all_to_all | solution.py:38
  42.3 0.7 all-gather.8.cloned.1.call-update
  43.0 0.7 all-gather.4.cloned.1.call-update
  43.7 78.6 %all-to-all-done.1 = bf16[8,8,32,896]{3,2,1,0:T(8,128)(2,1)} async-done(((bf16[8,8,32,896]{3,2,1,0:T(8,128)(2,1)}), bf16[8,8,32,896]{3,2,1,0:T(8,128)(2,1)}, u32[]{:S(2)}, u32[]{:S(2)}) %all-to-all-start.1) | async-done | bytes 3670048 | tf_op jit(solution)/shard_map/all_to_all | solution.py:38
  122.3 4.1 %gather_fusion.1 = bf16[32,32,896]{2,1,0:T(8,128)(2,1)} fusion(bf16[64,32,896]{2,1,0:T(8,128)(2,1)} %bitcast.4, s32[1024]{0:T(1024)S(1)} %pad_clamp_fusion), kind=kCustom, calls=%fused_computation.1 | custom fusion | bytes 3670144 | tf_op jit(solution)/shard_map/gather | solution.py:40
  126.4 3.7 all-to-all-start.2
  130.2 0.9 copy.66
  131.5 3.5 fusion.38
  135.0 0.9 copy.62
  135.9 17.1 %all-to-all-done.2 = bf16[4,8,32,896]{3,2,1,0:T(8,128)(2,1)S(1)} async-done(((bf16[4,8,32,896]{3,2,1,0:T(8,128)(2,1)}), bf16[4,8,32,896]{3,2,1,0:T(8,128)(2,1)S(1)}, u32[]{:S(2)}, u32[]{:S(2)}) %all-to-all-start.2) | async-done | bytes 1835040 | tf_op jit(solution)/shard_map/all_to_all | solution.py:41
  153.0 1.5 copy.49
  154.5 4.4 %convert_bitcast_fusion.2 = bf16[128,8,8,128]{3,1,2,0:T(8,128)(2,1)S(1)} fusion(bf16[1024,896]{1,0:T(8,128)(2,1)} %bitcast.89, bf16[896,1024]{1,0:T(8,128)(2,1)} %all-gather.8.cloned.1.call-done), kind=kOutput, calls=%fused_computation.22 | convolution fusion | flops 1880096768 | bytes 5767168 | tf_op jit(solution)/shard_map/dot_general | solution.py:44
  158.9 1.9 copy.63
  160.9 3.8 convert_bitcast_fusion.3
  165.4 0.9 copy-done.1
  166.6 0.8 fusion.20
  167.5 5.7 %fusion.55 = (f32[4,8,64]{2,1,0:T(8,128)S(1)}, f32[4,8,64,256]{3,2,1,0:T(8,128)S(1)}) fusion(f32[4,8,64,256]{3,2,1,0:T(8,128)S(1)} %fusion.20), kind=kOutput, calls=%fused_computation.69 | output fusion | flops 1048831 | bytes 4202496 | tf_op jit(solution)/shard_map/sub | solution.py:74
  173.3 1.2 fusion.11
  174.5 0.7 fusion.13
  176.2 4.6 %fusion.39 = f32[2048,1024]{1,0:T(8,128)} fusion(bf16[32,8,8,128]{3,2,1,0:T(8,128)(2,1)S(1)} %bitcast.83, bf16[256,2048]{1,0:T(8,128)(2,1)S(1)} %copy-done.2, f32[256]{0:T(256)S(1)} %add_rsqrt_fusion), kind=kOutput, calls=%fused_computation.41 | convolution fusion | flops 1075314688 | bytes 9962496 | tf_op jit(solution)/shard_map/td,te->de/dot_general | solution.py:99
  180.9 1.0 copy-done.14
  181.9 5.6 %convert_bitcast_fusion = bf16[4,256,8,128]{3,1,2,0:T(8,128)(2,1)} fusion(bf16[4,64,8,128]{3,2,1,0:T(8,128)(2,1)S(1)} %bitcast.95, f32[4,8,64]{2,1,0:T(8,128)S(1)} %get-tuple-element.10, f32[4,8,64,256]{3,2,1,0:T(8,128)S(1)} %fusion.20), kind=kOutput, calls=%fused_computation.19 | convolution fusion | flops 136841472 | bytes 4726784 | tf_op jit(solution)/shard_map/chmn,cmhd->cnhd/dot_general | solution.py:81
  187.5 4.4 %copy.61 = bf16[4,256,8,128]{3,2,1,0:T(8,128)(2,1)} copy(bf16[4,256,8,128]{3,1,2,0:T(8,128)(2,1)} %convert_bitcast_fusion) | data formatting | bytes 4194304 | tf_op jit(solution)/shard_map/convert_element_type | solution.py:83
  191.9 0.8 convert_bitcast_fusion.1
  192.7 2.6 copy.59
  195.2 6.2 %fusion.8 = f32[896,1024]{1,0:T(8,128)} fusion(bf16[1024,896]{1,0:T(8,128)(2,1)} %bitcast.90, bf16[128,8,8,128]{3,2,1,0:T(8,128)(2,1)} %bitcast.87), kind=kOutput, calls=%fused_computation.11 | convolution fusion | flops 1879048192 | bytes 7602176 | tf_op jit(solution)/shard_map/tl,te->le/dot_general | solution.py:100
  201.4 3.9 fusion.5
  205.3 165.1 %fusion.54 = (f32[32,1024]{1,0:T(8,128)S(1)}, f32[32,1024]{1,0:T(8,128)S(1)}) fusion(f32[896,1024]{1,0:T(8,128)} %fusion.8, f32[896,1024]{1,0:T(8,128)} %fusion.5), kind=kCustom, calls=%all-reduce-scatter.2 | all-reduce-scatter fusion | flops 2097153 | bytes 7602176
  370.5 1.3 collective-permute-start.2
  371.8 3.4 collective-permute-start.1
  375.2 1.3 collective-permute-start.3
  376.5 3.2 collective-permute-start
  380.4 2.9 collective-permute-start.6
  383.3 2.0 collective-permute-start.5
  385.3 2.7 collective-permute-start.4
  387.9 4.1 collective-permute-start.7
  392.0 5.9 %fusion.35 = bf16[4,64,8,128]{3,1,2,0:T(8,128)(2,1)S(1)} fusion(bf16[4,256,8,128]{3,2,1,0:T(8,128)(2,1)S(1)} %bitcast.85, f32[4,8,64]{2,1,0:T(8,128)S(1)} %get-tuple-element.10, f32[4,8,64,256]{3,2,1,0:T(8,128)} %copy-done), kind=kOutput, calls=%fused_computation.38 | convolution fusion | flops 136055040 | bytes 4726784 | tf_op jit(solution)/shard_map/chmn,cnhd->cmhd/dot_general | solution.py:77
  398.3 0.9 copy.113
  399.2 1.5 concatenate
  400.7 2.4 concatenate.1
  403.1 0.7 constant_dynamic-slice_fusion.1
  (69 shorter events, 6.2 us)
Async XLA Ops:
  7.2 124.3 %all-gather.6.cloned.1.call-start = ((), (), s32[]{:S(2)}) async-start(), calls=%async_computation.5 | async-start | bytes 5242880 | tf_op jit(solution)/shard_map/all_gather | solution.py:63
  37.7 84.6 %all-to-all-start.1 = ((bf16[8,8,32,896]{3,2,1,0:T(8,128)(2,1)}), bf16[8,8,32,896]{3,2,1,0:T(8,128)(2,1)}, u32[]{:S(2)}, u32[]{:S(2)}) async-start(bf16[8,8,32,896]{3,2,1,0:T(8,128)(2,1)} %bitcast.76), calls=%async_computation.1 | async-start | bytes 7340032 | tf_op jit(solution)/shard_map/all_to_all | solution.py:38
  42.2 112.3 %all-gather.8.cloned.1.call-start = ((), (), s32[]{:S(2)}) async-start(), calls=%async_computation.6 | async-start | bytes 2293760 | tf_op jit(solution)/shard_map/all_gather | solution.py:46
  43.0 117.9 %all-gather.4.cloned.1.call-start = ((), (), s32[]{:S(2)}) async-start(), calls=%async_computation.4 | async-start | bytes 2293760 | tf_op jit(solution)/shard_map/all_gather | solution.py:51
  126.4 3.8 copy-start.12
  126.4 4.7 %copy-start.2 = (bf16[256,2048]{1,0:T(8,128)(2,1)S(1)}, bf16[256,2048]{1,0:T(8,128)(2,1)}, u32[]{:S(2)}) copy-start(bf16[256,2048]{1,0:T(8,128)(2,1)} %param.7) | copy-start | bytes 3145732
  126.4 26.6 %all-to-all-start.2 = ((bf16[4,8,32,896]{3,2,1,0:T(8,128)(2,1)}), bf16[4,8,32,896]{3,2,1,0:T(8,128)(2,1)S(1)}, u32[]{:S(2)}, u32[]{:S(2)}) async-start(bf16[4,8,32,896]{3,2,1,0:T(8,128)(2,1)} %bitcast.80), calls=%async_computation.2 | async-start | bytes 3670016 | tf_op jit(solution)/shard_map/all_to_all | solution.py:41
  130.2 274.3 %reduce-scatter.6.cloned.1.call-start = ((), (), s32[]{:S(2)}) async-start(), calls=%async_computation.7 | async-start | bytes 8650752 | tf_op jit(solution)/shard_map/reduce_scatter | solution.py:105
  158.9 2.0 copy-start.10
  164.7 1.6 copy-start.1
  164.7 1.9 copy-start.3
  165.3 7.9 %copy-start.7 = (bf16[128,8,8,128]{3,2,1,0:T(8,128)(2,1)}, bf16[128,8,8,128]{3,2,1,0:T(8,128)(2,1)S(1)}, u32[]{:S(2)}) copy-start(bf16[128,8,8,128]{3,2,1,0:T(8,128)(2,1)S(1)} %copy.64) | copy-start | bytes 6291460
  167.5 13.4 %copy-start = (f32[4,8,64,256]{3,2,1,0:T(8,128)}, f32[4,8,64,256]{3,2,1,0:T(8,128)S(1)}, u32[]{:S(2)}) copy-start(f32[4,8,64,256]{3,2,1,0:T(8,128)S(1)} %fusion.20) | copy-start | bytes 6291460
  167.5 5.8 %copy-start.13 = (bf16[32,8,8,128]{3,2,1,0:T(8,128)(2,1)S(1)}, bf16[32,8,8,128]{3,2,1,0:T(8,128)(2,1)}, u32[]{:S(2)}) copy-start(bf16[32,8,8,128]{3,2,1,0:T(8,128)(2,1)} %copy.66) | copy-start | bytes 1572868
  175.2 1.0 copy-start.5
  180.8 1.0 copy-start.14
  187.5 4.4 %copy-start.4 = (bf16[32,8,8,128]{3,2,1,0:T(8,128)(2,1)S(1)}, bf16[32,8,8,128]{3,2,1,0:T(8,128)(2,1)}, u32[]{:S(2)}) copy-start(bf16[32,8,8,128]{3,2,1,0:T(8,128)(2,1)} %copy.62) | copy-start | bytes 1572868
  187.5 4.4 %copy-start.6 = (bf16[4,8,64,256]{3,2,1,0:T(8,128)(2,1)S(1)}, bf16[4,8,64,256]{3,2,1,0:T(8,128)(2,1)}, u32[]{:S(2)}) copy-start(bf16[4,8,64,256]{3,2,1,0:T(8,128)(2,1)} %copy-done.5) | copy-start | bytes 3145732
  195.2 6.2 %copy-start.9 = (bf16[4,256,8,128]{3,2,1,0:T(8,128)(2,1)S(1)}, bf16[4,256,8,128]{3,2,1,0:T(8,128)(2,1)}, u32[]{:S(2)}) copy-start(bf16[4,256,8,128]{3,2,1,0:T(8,128)(2,1)} %copy.61) | copy-start | bytes 6291460
  195.2 6.2 %copy-start.11 = (bf16[1,8,4,32,896]{4,3,2,1,0:T(8,128)(2,1)S(1)}, bf16[1,8,4,32,896]{4,3,2,1,0:T(8,128)(2,1)}, u32[]{:S(2)}) copy-start(bf16[1,8,4,32,896]{4,3,2,1,0:T(8,128)(2,1)} %copy.49) | copy-start | bytes 5505028
  205.3 186.7 %copy-start.8 = (bf16[128,8,8,128]{3,2,1,0:T(8,128)(2,1)S(1)}, bf16[128,8,8,128]{3,2,1,0:T(8,128)(2,1)}, u32[]{:S(2)}) copy-start(bf16[128,8,8,128]{3,2,1,0:T(8,128)(2,1)} %copy-done.7) | copy-start | bytes 6291460
  370.5 14.8 %collective-permute-start.2 = (f32[32,1024]{1,0:T(8,128)S(1)}, f32[32,1024]{1,0:T(8,128)S(1)}, u32[]{:S(2)}, u32[]{:S(2)}) collective-permute-start(f32[32,1024]{1,0:T(8,128)S(1)} %get-tuple-element.6), channel_id=1, source_target_pairs={{0,3},{1,4},{2,5},{3,6},{4,7},{5,8},{6,9},{7,10},{8,11},{9,12},{10... | collective-permute-start | bytes 393224
  371.8 16.1 %collective-permute-start.1 = (f32[32,1024]{1,0:T(8,128)S(1)}, f32[32,1024]{1,0:T(8,128)S(1)}, u32[]{:S(2)}, u32[]{:S(2)}) collective-permute-start(f32[32,1024]{1,0:T(8,128)S(1)} %get-tuple-element.6), channel_id=1, source_target_pairs={{0,2},{1,3},{2,4},{3,5},{4,6},{5,7},{6,8},{7,9},{8,10},{9,11},{10,... | collective-permute-start | bytes 393224
  375.2 8.1 %collective-permute-start.3 = (f32[28,1024]{1,0:T(8,128)S(1)}, f32[28,1024]{1,0:T(8,128)S(1)}, u32[]{:S(2)}, u32[]{:S(2)}) collective-permute-start(f32[28,1024]{1,0:T(8,128)S(1)} %slice.4), channel_id=1, source_target_pairs={{0,4},{1,5},{2,6},{3,7},{4,8},{5,9},{6,10},{7,11},{8,12},{9,13},{1... | collective-permute-start | bytes 344072
  376.5 22.7 %collective-permute-start = (f32[32,1024]{1,0:T(8,128)S(1)}, f32[32,1024]{1,0:T(8,128)}, u32[]{:S(2)}, u32[]{:S(2)}) collective-permute-start(f32[32,1024]{1,0:T(8,128)S(1)} %get-tuple-element.6), channel_id=1, source_target_pairs={{0,1},{1,2},{2,3},{3,4},{4,5},{5,6},{6,7},{7,8},{8,9},{9,10},{10,1... | collective-permute-start | bytes 393224
  380.4 20.3 %collective-permute-start.6 = (f32[32,1024]{1,0:T(8,128)S(1)}, f32[32,1024]{1,0:T(8,128)S(1)}, u32[]{:S(2)}, u32[]{:S(2)}) collective-permute-start(f32[32,1024]{1,0:T(8,128)S(1)} %get-tuple-element.7), channel_id=1, source_target_pairs={{0,3},{1,4},{2,5},{3,6},{4,7},{5,8},{6,9},{7,10},{8,11},{9,12},{10... | collective-permute-start | bytes 393224
  383.3 17.4 %collective-permute-start.5 = (f32[32,1024]{1,0:T(8,128)S(1)}, f32[32,1024]{1,0:T(8,128)S(1)}, u32[]{:S(2)}, u32[]{:S(2)}) collective-permute-start(f32[32,1024]{1,0:T(8,128)S(1)} %get-tuple-element.7), channel_id=1, source_target_pairs={{0,2},{1,3},{2,4},{3,5},{4,6},{5,7},{6,8},{7,9},{8,10},{9,11},{10,... | collective-permute-start | bytes 393224
  385.3 15.4 %collective-permute-start.4 = (f32[32,1024]{1,0:T(8,128)S(1)}, f32[32,1024]{1,0:T(8,128)}, u32[]{:S(2)}, u32[]{:S(2)}) collective-permute-start(f32[32,1024]{1,0:T(8,128)S(1)} %get-tuple-element.7), channel_id=1, source_target_pairs={{0,1},{1,2},{2,3},{3,4},{4,5},{5,6},{6,7},{7,8},{8,9},{9,10},{10,1... | collective-permute-start | bytes 393224
  387.9 12.8 %collective-permute-start.7 = (f32[28,1024]{1,0:T(8,128)}, f32[28,1024]{1,0:T(8,128)}, u32[]{:S(2)}, u32[]{:S(2)}) collective-permute-start(f32[28,1024]{1,0:T(8,128)} %slice.5), channel_id=1, source_target_pairs={{0,4},{1,5},{2,6},{3,7},{4,8},{5,9},{6,10},{7,11},{8,12},{9,13},{1... | collective-permute-start | bytes 344072
Sparse Core Ops, SparseCore 0:
  9.6 37.1 all-gather.5
  48.3 21.1 all-gather.7
  71.1 21.1 all-gather.3
  181.0 176.0 reduce-scatter.5
where the time goes:
time: 413 us; the launch traced here: 411 us
  blocking collectives  184 us (45%)
  waiting for transfers between devices  97.9 us (24%)
  matrix products  41.2 us (10%)
  local copies, waits for them, and re-layouts  36.5 us (9%)
  starting transfers between devices  29.2 us (7%)
  between operations  14.8 us (4%)
  other arithmetic  7.79 us (2%)
    unnamed x2, blocking collectives  172 us
    all_to_all x1, waiting for transfers between devices, body(): lax.all_to_all(fetched, 'dp', split_axis=0, concat_axis=0, tiled=True)  78.6 us
    unnamed x8, starting transfers between devices  20.8 us
    all_to_all x1, waiting for transfers between devices, body(): lax.all_to_all(chosen, 'shard', split_axis=0, concat_axis=2, tiled=True)  17.1 us
    unnamed x45, local copies, waits for them, and re-layouts  15.9 us
    all_to_all x1, blocking collectives, body(): lax.all_to_all(outgoing, 'dp', split_axis=0, concat_axis=0, tiled=True)  12.1 us
  transfers between devices with their start and end apart: 14, of which 2 were waited for; matrix products, arithmetic and copies ran while one was open for 56% of the time, Pallas kernels for 0%

commit v1 on v0

v1 whole, which is shorter than its diff:
```python
import functools

import jax
import jax.numpy as jnp
from jax import lax
from jax.experimental import pallas as pl
from jax.experimental.pallas import tpu as pltpu
from jax.sharding import PartitionSpec as P

HEAD_DIM = 128
AXES = ("dp", "shard")
LANES = 128
ANY = pl.BlockSpec(memory_space=pl.ANY)
SMEM = pl.BlockSpec(memory_space=pltpu.SMEM)
VMEM = pl.BlockSpec(memory_space=pltpu.VMEM)
VMEM_LIMIT = 56 * 1024 * 1024
F32 = jnp.float32
BF16 = jnp.bfloat16


def lane_cuts(width, shares):
    tiles = width // LANES
    total = sum(shares)
    ends = [0]
    for k in range(1, len(shares) + 1):
        ends.append(round(tiles * sum(shares[:k]) / total) * LANES)
    return [(a, b - a) for a, b in zip(ends, ends[1:]) if b > a]


def serve_kernel(groups, group, slots, owned, cuts, ids, place, cache, *rest):
    outs, (table, sem) = rest[: len(cuts)], rest[len(cuts) :]
    me = place[0]

    def ask(g, carry):
        def scan(i, at):
            row = ids[g * group + i] - me * owned
            mine = jnp.logical_and(row >= 0, row < owned)
            table[at] = jnp.clip(row, 0, owned - 1)
            return jnp.where(mine, at + 1, at)

        at = lax.fori_loop(0, group, scan, g * slots, unroll=True)

        def fill(k, at):
            table[k] = jnp.where(k < at, table[k], 0)
            row = table[k]
            for (start, width), out in zip(cuts, outs):
                pltpu.make_async_copy(
                    cache.at[row, :, pl.ds(start, width)], out.at[k], sem
                ).start()
            return at

        lax.fori_loop(g * slots, g * slots + slots, fill, at)
        return carry

    lax.fori_loop(0, groups, ask, 0)
    for out in outs:
        pltpu.make_async_copy(out, out, sem).wait()


def pick_kernel(group, slots, owned, owners, shards, ids, place, arrived, *rest):
    outs, (count, sem) = rest[:shards], rest[shards:]
    me, shard = place[0], place[1]
    each = group // shards

    def clear(k, carry):
        count[k] = 0
        return carry

    lax.fori_loop(0, owners, clear, 0)

    def locate(i, carry):
        owner = ids[me * group + i] // owned
        at = count[owner]
        count[owner] = at + 1
        count[owners + i] = owner * slots + at
        return carry

    lax.fori_loop(0, group, locate, 0, unroll=8)
    for k in range(shards):
        peer = jnp.bitwise_xor(shard, k)
        for j in range(each):
            at = count[owners + peer * each + j]
            pltpu.make_async_copy(arrived.at[at], outs[k].at[j], sem).start()
    for k in range(shards):
        pltpu.make_async_copy(outs[k], outs[k], sem).wait()


def attend_kernel(parts, shards, heads, scale, *refs):
    pieces, refs = refs[: parts * shards], refs[parts * shards :]
    queries, cotangent, w_key, w_value = refs[:4]
    context, query_grad, key_grad, value_grad, latents = refs[4:9]
    key_rows, value_rows = refs[9:]
    nbr, tokens, _ = pieces[0].shape
    for k in range(shards):
        at = 0
        for j in range(parts):
            piece = pieces[j * shards + k]
            width = piece.shape[2]
            latents[k * nbr * tokens : (k + 1) * nbr * tokens, at : at + width] = piece[
                ...
            ].reshape(nbr * tokens, width)
            at += width
    rows = latents[...]
    key_rows[...] = jnp.dot(rows, w_key[...], preferred_element_type=F32).astype(BF16)
    value_rows[...] = jnp.dot(rows, w_value[...], preferred_element_type=F32).astype(
        BF16
    )
    dot = functools.partial(lax.dot_general, preferred_element_type=F32)
    nt = (((1,), (1,)), ((), ()))
    nn = (((1,), (0,)), ((), ()))
    tn = (((0,), (0,)), ((), ()))
    for h in range(heads):
        cols = slice(h * HEAD_DIM, (h + 1) * HEAD_DIM)
        query, grad = queries[:, cols], cotangent[:, cols]
        key, value = key_rows[:, cols], value_rows[:, cols]
        scores = dot(query, key, nt)
        raised = jnp.exp(scores - jnp.max(scores, axis=-1, keepdims=True))
        prob = raised * (1.0 / jnp.sum(raised, axis=-1, keepdims=True))
        rounded = prob.astype(BF16)
        context[:, cols] = dot(rounded, value, nn).astype(BF16)
        value_grad[:, cols] = dot(rounded, grad, tn).astype(BF16)
        prob_grad = dot(grad, value, nt)
        inner = jnp.sum(prob * prob_grad, axis=-1, keepdims=True)
        score_grad = (prob * (prob_grad - inner)).astype(BF16)
        query_grad[:, cols] = (dot(score_grad, key, nn) * scale).astype(BF16)
        key_grad[:, cols] = dot(score_grad, query, tn).astype(BF16)


def grad_kernel(devices, rows, padded, step, place, left, right, keep, send, total):
    me = place[2]
    odd = jnp.bitwise_and(me, 1) == 1
    half = me >> 1
    width = left.shape[1]
    for at in range(0, width, step):
        size = min(step, width - at)
        total[at : at + size, :] = lax.dot_general(
            left[:, at : at + size],
            right[...],
            (((0,), (0,)), ((), ())),
            preferred_element_type=F32,
        )
    if total.shape[0] > width:
        total[width:, :] = jnp.zeros((total.shape[0] - width, total.shape[1]), F32)
    for d in range(devices // 2):
        even_rows = total[2 * d * rows : 2 * d * rows + padded, :]
        odd_rows = total[(2 * d + 1) * rows : (2 * d + 1) * rows + padded, :]
        at = jnp.bitwise_xor(half, d)
        keep[at] = jnp.where(odd, odd_rows, even_rows)
        send[at] = jnp.where(odd, even_rows, odd_rows).astype(BF16)


def grad_blocks(place, left, right, devices, step):
    width, columns = left.shape[1], right.shape[1]
    rows = width // devices
    padded = -(-rows // 16) * 16
    body = functools.partial(grad_kernel, devices, rows, padded, step)
    return pl.pallas_call(
        body,
        out_shape=(
            jax.ShapeDtypeStruct((devices // 2, padded, columns), F32),
            jax.ShapeDtypeStruct((devices // 2, padded, columns), BF16),
        ),
        in_specs=[SMEM, VMEM, VMEM],
        out_specs=(VMEM, VMEM),
        scratch_shapes=[pltpu.VMEM((width + padded, columns), F32)],
        compiler_params=pltpu.CompilerParams(vmem_limit_bytes=VMEM_LIMIT),
        cost_estimate=pl.CostEstimate(
            flops=2 * width * columns * left.shape[0],
            bytes_accessed=2 * left.size + 2 * right.size + 6 * width * columns,
            transcendentals=0,
        ),
    )(place, left, right)


def swap(value, bit, devices):
    return lax.ppermute(value, AXES, [(i, i ^ bit) for i in range(devices)])


def body(tokens, ctx_cotangent, latent_cache, nbr_ids, w_query, w_key, w_value):
    owners, shards = lax.axis_size("dp"), lax.axis_size("shard")
    devices = owners * shards
    owned, slice_tokens, latent = latent_cache.shape
    spans, nbr = nbr_ids.shape
    each = spans * nbr
    group = each * shards
    slots = 2 * group // owners
    inner = w_query.shape[1]
    heads = inner // HEAD_DIM
    scale = HEAD_DIM**-0.5
    span = tokens.shape[0] // spans
    dp, shard = lax.axis_index("dp"), lax.axis_index("shard")
    place = jnp.stack([dp, shard, dp * shards + shard]).astype(jnp.int32)

    ids = lax.all_to_all(
        jnp.broadcast_to(nbr_ids.reshape(1, each), (devices, each)),
        AXES,
        split_axis=0,
        concat_axis=0,
        tiled=True,
    ).reshape(-1)

    key_full = lax.all_gather(w_key, "shard", axis=0, tiled=True)
    value_full = lax.all_gather(w_value, "shard", axis=0, tiled=True)
    query_full = lax.all_gather(w_query, "shard", axis=0, tiled=True)

    cuts = lane_cuts(latent, (3, 3, 1))
    served = pl.pallas_call(
        functools.partial(serve_kernel, owners, group, slots, owned, cuts),
        out_shape=[
            jax.ShapeDtypeStruct((owners * slots, slice_tokens, width), BF16)
            for _, width in cuts
        ],
        in_specs=[SMEM, SMEM, ANY],
        out_specs=[ANY] * len(cuts),
        scratch_shapes=[
            pltpu.SMEM((owners * slots + 1,), jnp.int32),
            pltpu.SemaphoreType.DMA,
        ],
    )(ids, place, latent_cache)

    pieces = []
    for (_, width), rows in zip(cuts, served):
        arrived = lax.all_to_all(rows, "dp", split_axis=0, concat_axis=0, tiled=True)
        picked = pl.pallas_call(
            functools.partial(pick_kernel, group, slots, owned, owners, shards),
            out_shape=[
                jax.ShapeDtypeStruct((each, slice_tokens, width), BF16)
                for _ in range(shards)
            ],
            in_specs=[SMEM, SMEM, ANY],
            out_specs=[ANY] * shards,
            scratch_shapes=[
                pltpu.SMEM((owners + group,), jnp.int32),
                pltpu.SemaphoreType.DMA,
            ],
        )(ids, place, arrived)
        pieces += [
            piece if k == 0 else swap(piece, k, devices)
            for k, piece in enumerate(picked)
        ]

    as_float = tokens.astype(F32)
    normed = (
        as_float
        * lax.rsqrt(jnp.mean(as_float * as_float, axis=-1, keepdims=True) + 1e-06)
    ).astype(BF16)
    query_sum = jnp.dot(normed, query_full, preferred_element_type=F32)
    queries = (query_sum * scale).astype(BF16)

    keys = nbr * shards * slice_tokens
    piece_specs = [
        pl.BlockSpec((nbr, slice_tokens, piece.shape[2]), lambda c: (c, 0, 0))
        for piece in pieces
    ]
    by_span = pl.BlockSpec((span, inner), lambda c: (c, 0))
    by_keys = pl.BlockSpec((keys, inner), lambda c: (c, 0))
    whole = pl.BlockSpec((latent, inner), lambda c: (0, 0))
    context, query_grad, key_grad, value_grad, latents = pl.pallas_call(
        functools.partial(attend_kernel, len(cuts), shards, heads, scale),
        grid=(spans,),
        out_shape=(
            jax.ShapeDtypeStruct((spans * span, inner), BF16),
            jax.ShapeDtypeStruct((spans * span, inner), BF16),
            jax.ShapeDtypeStruct((spans * keys, inner), BF16),
            jax.ShapeDtypeStruct((spans * keys, inner), BF16),
            jax.ShapeDtypeStruct((spans * keys, latent), BF16),
        ),
        in_specs=piece_specs + [by_span, by_span, whole, whole],
        out_specs=(
            by_span,
            by_span,
            by_keys,
            by_keys,
            pl.BlockSpec((keys, latent), lambda c: (c, 0)),
        ),
        scratch_shapes=[pltpu.VMEM((keys, inner), BF16)] * 2,
        compiler_params=pltpu.CompilerParams(vmem_limit_bytes=VMEM_LIMIT),
        cost_estimate=pl.CostEstimate(
            flops=4 * spans * keys * inner * (latent + 3 * span),
            bytes_accessed=2 * spans * keys * (2 * inner + 2 * latent),
            transcendentals=spans * span * keys * heads,
        ),
    )(*pieces, queries, ctx_cotangent, key_full, value_full)

    low = 1 << (owners.bit_length() - 1) // 2
    lengths = dict(z=owners // low, x=low, y=shards // 2)
    bits = dict(z=low * shards, x=shards, y=2)

    def scatter_sum(left, right, order):
        keep, send = grad_blocks(place, left, right, devices, 512)
        total = keep + swap(send, 1, devices).astype(F32)
        total = total.reshape(lengths["z"], lengths["x"], lengths["y"], *keep.shape[1:])
        for name in order:
            axis = "zxy".index(name)
            cut = lambda k: lax.slice_in_dim(total, k, k + 1, axis=axis)
            came = [
                swap(cut(k).astype(BF16), k * bits[name], devices)
                for k in range(1, lengths[name])
            ]
            total = sum((part.astype(F32) for part in came), cut(0))
        return total.reshape(keep.shape[1:])[: left.shape[1] // devices]

    grad_value = scatter_sum(latents, value_grad, "zyx")
    grad_query = scatter_sum(normed, query_grad, "xyz")
    grad_key = scatter_sum(latents, key_grad, "yxz")
    return context, grad_query, grad_key, grad_value


def solution(mesh):
    rows = P(AXES, None)
    by_shard = P("shard", None)
    return jax.shard_map(
        body,
        mesh=mesh,
        in_specs=(rows, rows, P("dp", "shard", None), rows)
        + (by_shard, by_shard, by_shard),
        out_specs=(rows, rows, rows, rows),
        check_vma=False,
    )
```

time: 413 us -> 404 us (0.978)
  Pallas kernels: 0 us -> 222 us
  blocking collectives: 184 us -> 18.9 us
  matrix products: 41.2 us -> 4.6 us
  local copies, waits for them, and re-layouts: 36.5 us -> 5.07 us
  starting transfers between devices: 29.2 us -> 41.8 us
  waiting for transfers between devices: 97.9 us -> 88.2 us
    pallas_call x0 -> x8, Pallas kernels: none -> 222 us  [the longest x1 113 us: body(): pl.pallas_call(functools.partial(serve_kernel, owners, group, slots, owne...]
    unnamed x2 -> x0, blocking collectives: 172 us -> none
    all_to_all x2 -> x3, waiting for transfers between devices: 95.8 us -> 42.4 us  [the longest x2 35.9 us: body(): lax.all_to_all(rows, 'dp', split_axis=0, concat_axis=0, tiled=True)]
    ppermute x0 -> x27, waiting for transfers between devices: none -> 43.8 us  [swap(): return lax.ppermute(value, AXES, [(i, i ^ bit) for i in range(devices)])]
    dot_general x12 -> x1, matrix products: 41.2 us -> 4.6 us  [body(): query_sum = jnp.dot(normed, query_full, preferred_element_type=F32)]
    ppermute x0 -> x27, starting transfers between devices: none -> 27.1 us  [swap(): return lax.ppermute(value, AXES, [(i, i ^ bit) for i in range(devices)])]
    unnamed x8 -> x0, starting transfers between devices: 20.8 us -> none
    unnamed x45 -> x35, local copies, waits for them, and re-layouts: 15.9 us -> 2.7 us
  transfers between devices with their start and end apart: 14 -> 33, of which waited for: 2 -> 14; matrix products, arithmetic and copies ran while one was open for 56% -> 4% of each run, Pallas kernels for 0% -> 47%
where the time goes in v1:
time: 404 us
  Pallas kernels  222 us (55%)
  waiting for transfers between devices  88.2 us (22%)
  starting transfers between devices  41.8 us (10%)
  blocking collectives  18.9 us (5%)
  between operations  14.2 us (4%)
  other arithmetic  9.08 us (2%)
  local copies, waits for them, and re-layouts  5.07 us (1%)
  matrix products  4.6 us (1%)
    pallas_call x1, Pallas kernels, body(): pl.pallas_call(functools.partial(serve_kernel, owners, group, slots, owne...  113 us
    pallas_call x3, Pallas kernels, body(): pl.pallas_call(functools.partial(pick_kernel, group, slots, owned, owners...  62 us
    ppermute x27, waiting for transfers between devices, swap(): return lax.ppermute(value, AXES, [(i, i ^ bit) for i in range(devices)])  43.8 us
    all_to_all x2, waiting for transfers between devices, body(): lax.all_to_all(rows, 'dp', split_axis=0, concat_axis=0, tiled=True)  35.9 us
    pallas_call x1, Pallas kernels, body(): pl.pallas_call(functools.partial(attend_kernel, len(cuts), shards, heads,...  28.3 us
    ppermute x27, starting transfers between devices, swap(): return lax.ppermute(value, AXES, [(i, i ^ bit) for i in range(devices)])  27.1 us
    all_to_all x1, blocking collectives, body(): lax.all_to_all(rows, 'dp', split_axis=0, concat_axis=0, tiled=True)  18.9 us
    pallas_call x3, Pallas kernels, grad_blocks(): pl.pallas_call(body, out_shape=(jax.ShapeDtypeStruct((devices // 2, padde...  18.5 us
  transfers between devices with their start and end apart: 33, of which 14 were waited for; matrix products, arithmetic and copies ran while one was open for 4% of the time, Pallas kernels for 47%

profile of v1, /device:TPU:0, one launch (start us, length us, event | category | flops | bytes accessed | tf_op | source)
XLA Modules:
  0.0 403.8 jit_solution(10576184473169486671)
XLA Ops:
  7.9 0.8 copy.13
  9.4 7.3 %all-to-all-start = ((s32[32,1,8]{2,1,0:T(1,128)}), s32[32,1,8]{2,1,0:T(1,128)S(1)}, u32[]{:S(2)}, u32[]{:S(2)}) async-start(s32[32,1,8]{2,1,0:T(1,128)} %broadcast_in_dim.9), calls=%async_computation | async-start | bytes 32768 | tf_op jit(solution)/shard_map/all_to_all | solution.py:194
  17.3 6.4 %all-to-all-done = s32[32,1,8]{2,1,0:T(1,128)S(1)} async-done(((s32[32,1,8]{2,1,0:T(1,128)}), s32[32,1,8]{2,1,0:T(1,128)S(1)}, u32[]{:S(2)}, u32[]{:S(2)}) %all-to-all-start) | async-done | bytes 1056 | tf_op jit(solution)/shard_map/all_to_all | solution.py:194
  24.3 0.7 reduce.3
  25.6 113.2 %shard_map.102 = (bf16[64,32,384]{2,1,0:T(8,128)(2,1)}, bf16[64,32,384]{2,1,0:T(8,128)(2,1)}, bf16[64,32,128]{2,1,0:T(8,128)(2,1)}) custom-call(s32[256]{0:T(256)} %reshape.86.ids, s32[3]{0:T(128)} %pad_add_fusion.place, bf16[128,32,896]{2,1,0:T(8,128)(2,1)} %cache.1), custom_call_target="tpu_custom_call" | custom-call | tf_op jit(solution)/shard_map/pallas_call | solution.py:207
  138.7 18.9 %all_to_all.21.arrived = bf16[64,32,128]{2,1,0:T(8,128)(2,1)} all-to-all(bf16[64,32,128]{2,1,0:T(8,128)(2,1)} %get-tuple-element.40), channel_id=1, replica_groups=mesh['dp'=8,'shard'=4] {'dp'}, dimensions={0} | all-to-all | bytes 1048576 | tf_op jit(solution)/shard_map/all_to_all | solution.py:223
  157.7 3.6 all-to-all-start.2
  161.4 0.7 all-gather.6.cloned.1.call-update
  162.1 35.9 %all-to-all-done.2.arrived = bf16[64,32,384]{2,1,0:T(8,128)(2,1)S(1)} async-done(((bf16[64,32,384]{2,1,0:T(8,128)(2,1)}), bf16[64,32,384]{2,1,0:T(8,128)(2,1)S(1)}, u32[]{:S(2)}, u32[]{:S(2)}) %all-to-all-start.2) | async-done | bytes 1572896 | tf_op jit(solution)/shard_map/all_to_all | solution.py:223
  198.0 3.6 all-to-all-start.1
  202.4 1.5 fusion
  203.9 10.2 %shard_map.105 = (bf16[8,32,128]{2,1,0:T(8,128)(2,1)}, bf16[8,32,128]{2,1,0:T(8,128)(2,1)}, bf16[8,32,128]{2,1,0:T(8,128)(2,1)}, bf16[8,32,128]{2,1,0:T(8,128)(2,1)}) custom-call(s32[256]{0:T(256)} %reshape.86.ids, s32[3]{0:T(128)} %pad_add_fusion.place, bf16[64,32,128]{2,1,0:T(8,128)(2,1)} %all_to_all.21.arrived), custom_call_target="tpu_custom_call" | custom-call | tf_op jit(solution)/shard_map/pallas_call | solution.py:224
  214.8 1.3 collective-permute-start.8
  216.0 25.9 %shard_map.104 = (bf16[8,32,384]{2,1,0:T(8,128)(2,1)}, bf16[8,32,384]{2,1,0:T(8,128)(2,1)}, bf16[8,32,384]{2,1,0:T(8,128)(2,1)}, bf16[8,32,384]{2,1,0:T(8,128)(2,1)}) custom-call(s32[256]{0:T(256)} %reshape.86.ids, s32[3]{0:T(128)} %pad_add_fusion.place, bf16[64,32,384]{2,1,0:T(8,128)(2,1)} %copy-done.1), custom_call_target="tpu_custom_call" | custom-call | tf_op jit(solution)/shard_map/pallas_call | solution.py:224
  242.4 1.2 fusion.1.left
  244.2 1.2 copy-done
  245.4 25.9 %shard_map.103 = (bf16[8,32,384]{2,1,0:T(8,128)(2,1)}, bf16[8,32,384]{2,1,0:T(8,128)(2,1)}, bf16[8,32,384]{2,1,0:T(8,128)(2,1)}, bf16[8,32,384]{2,1,0:T(8,128)(2,1)}) custom-call(s32[256]{0:T(256)} %reshape.86.ids, s32[3]{0:T(128)} %pad_add_fusion.place, bf16[64,32,384]{2,1,0:T(8,128)(2,1)} %copy-done), custom_call_target="tpu_custom_call" | custom-call | tf_op jit(solution)/shard_map/pallas_call | solution.py:224
  271.4 1.0 collective-permute-start.5
  273.6 0.9 collective-permute-start.2
  274.5 4.6 %fusion.2.refs_12_ = bf16[256,1024]{1,0:T(8,128)(2,1)} fusion(bf16[256,2048]{1,0:T(8,128)(2,1)} %fusion.1.left, bf16[2048,1024]{1,0:T(8,128)(2,1)} %all-gather.4.cloned.1.call-done), kind=kOutput, calls=%fused_computation.10 | convolution fusion | flops 1074266112 | bytes 5767168 | tf_op jit(solution)/shard_map/dot_general | solution.py:247
  279.2 3.7 collective-permute-done.1.refs_2_
  282.9 4.1 %collective-permute-done.2.refs_3_ = bf16[8,32,384]{2,1,0:T(8,128)(2,1)S(1)} collective-permute-done((bf16[8,32,384]{2,1,0:T(8,128)(2,1)}, bf16[8,32,384]{2,1,0:T(8,128)(2,1)S(1)}, u32[]{:S(2)}, u32[]{:S(2)}) %collective-permute-start.2) | collective-permute-done | bytes 196640 | tf_op jit(solution)/shard_map/ppermute | solution.py:176
  287.7 28.3 %shard_map.106 = (bf16[256,1024]{1,0:T(8,128)(2,1)}, bf16[256,1024]{1,0:T(8,128)(2,1)}, bf16[1024,1024]{1,0:T(8,128)(2,1)}, bf16[1024,1024]{1,0:T(8,128)(2,1)}, bf16[1024,896]{1,0:T(8,128)(2,1)}) custom-call(bf16[8,32,384]{2,1,0:T(8,128)(2,1)} %get-tuple-element.31.refs_0_, bf16[8,32,384]{2,1,0:T(8,128)(2,1)} %copy-done.11, bf16[8,32,384]{2,1,0:T(8,128)(2,1)} %copy-done.12, ...), custom_call_target="tpu_custom_call" | custom-call | flops 4563402752 | bytes 7864320 | tf_op jit(solution)/shard_map/pallas_call | solution.py:258
  316.0 5.4 %shard_map.107 = (f32[16,64,1024]{2,1,0:T(8,128)}, bf16[16,64,1024]{2,1,0:T(8,128)(2,1)}) custom-call(s32[3]{0:T(128)} %pad_add_fusion.place, bf16[256,2048]{1,0:T(8,128)(2,1)} %fusion.1.left, bf16[256,1024]{1,0:T(8,128)(2,1)} %get-tuple-element.46.right), custom_call_target="tpu_custom_call" | custom-call | flops 1073741824 | bytes 14155776 | tf_op jit(solution)/shard_map/pallas_call | solution.py:157
  321.5 6.5 %shard_map.109 = (f32[16,32,1024]{2,1,0:T(8,128)}, bf16[16,32,1024]{2,1,0:T(8,128)(2,1)}) custom-call(s32[3]{0:T(128)} %pad_add_fusion.place, bf16[1024,896]{1,0:T(8,128)(2,1)} %get-tuple-element.49.left, bf16[1024,1024]{1,0:T(8,128)(2,1)} %get-tuple-element.53.right), custom_call_target="tpu_custom_call" | custom-call | flops 1879048192 | bytes 9437184 | tf_op jit(solution)/shard_map/pallas_call | solution.py:157
  328.4 6.6 %shard_map.108 = (f32[16,32,1024]{2,1,0:T(8,128)}, bf16[16,32,1024]{2,1,0:T(8,128)(2,1)}) custom-call(s32[3]{0:T(128)} %pad_add_fusion.place, bf16[1024,896]{1,0:T(8,128)(2,1)} %get-tuple-element.49.left, bf16[1024,1024]{1,0:T(8,128)(2,1)} %get-tuple-element.50.right), custom_call_target="tpu_custom_call" | custom-call | flops 1879048192 | bytes 9437184 | tf_op jit(solution)/shard_map/pallas_call | solution.py:157
  335.6 3.9 collective-permute-start.24
  340.2 1.1 convert_add_fusion
  341.4 2.0 collective-permute-start.10
  344.0 1.6 collective-permute-start.16
  345.6 1.2 collective-permute-done.24
  346.8 6.1 %collective-permute-done.22 = bf16[1,2,2,32,1024]{4,3,2,1,0:T(8,128)(2,1)S(1)} collective-permute-done((bf16[1,2,2,32,1024]{4,3,2,1,0:T(8,128)(2,1)S(1)}, bf16[1,2,2,32,1024]{4,3,2,1,0:T(8,128)(2,1)S(1)}, u32[]{:S(2)}, u32[]{:S(2)}) %collective-permute-start.22) | collective-permute-done | bytes 262176 | tf_op jit(solution)/shard_map/ppermute | solution.py:176
  352.9 9.7 %collective-permute-done.23 = bf16[1,2,2,32,1024]{4,3,2,1,0:T(8,128)(2,1)S(1)} collective-permute-done((bf16[1,2,2,32,1024]{4,3,2,1,0:T(8,128)(2,1)S(1)}, bf16[1,2,2,32,1024]{4,3,2,1,0:T(8,128)(2,1)S(1)}, u32[]{:S(2)}, u32[]{:S(2)}) %collective-permute-start.23) | collective-permute-done | bytes 262176 | tf_op jit(solution)/shard_map/ppermute | solution.py:176
  362.8 1.6 collective-permute-start.25
  364.3 3.5 collective-permute-done.25
  367.9 1.5 collective-permute-start.26
  370.7 1.6 collective-permute-start.11
  373.5 3.5 collective-permute-done.17
  377.2 2.4 collective-permute-start.20
  379.6 1.1 collective-permute-start.19
  380.7 2.0 collective-permute-done.11
  383.0 2.5 collective-permute-start.14
  385.5 1.0 collective-permute-start.13
  386.5 1.7 collective-permute-done.19
  388.2 0.7 fusion.9
  388.9 2.4 collective-permute-done.14
  391.3 5.3 %collective-permute-done.13 = bf16[1,1,1,64,1024]{4,3,2,1,0:T(8,128)(2,1)S(1)} collective-permute-done((bf16[1,1,1,64,1024]{4,3,2,1,0:T(8,128)(2,1)S(1)}, bf16[1,1,1,64,1024]{4,3,2,1,0:T(8,128)(2,1)S(1)}, u32[]{:S(2)}, u32[]{:S(2)}) %collective-permute-start.13) | collective-permute-done | bytes 131104 | tf_op jit(solution)/shard_map/ppermute | solution.py:176
  396.5 0.8 fusion.5
  (99 shorter events, 13.2 us)
Async XLA Ops:
  7.2 267.3 %all-gather.4.cloned.1.call-start = ((), (), s32[]{:S(2)}) async-start(), calls=%async_computation.4 | async-start | bytes 5242880 | tf_op jit(solution)/shard_map/all_gather | solution.py:204
  9.4 14.4 %all-to-all-start = ((s32[32,1,8]{2,1,0:T(1,128)}), s32[32,1,8]{2,1,0:T(1,128)S(1)}, u32[]{:S(2)}, u32[]{:S(2)}) async-start(s32[32,1,8]{2,1,0:T(1,128)} %broadcast_in_dim.9), calls=%async_computation | async-start | bytes 32768 | tf_op jit(solution)/shard_map/all_to_all | solution.py:194
  157.7 40.3 %all-to-all-start.2 = ((bf16[64,32,384]{2,1,0:T(8,128)(2,1)}), bf16[64,32,384]{2,1,0:T(8,128)(2,1)S(1)}, u32[]{:S(2)}, u32[]{:S(2)}) async-start(bf16[64,32,384]{2,1,0:T(8,128)(2,1)} %get-tuple-element.35), calls=%async_computation.2 | async-start | bytes 3145728 | tf_op jit(solution)/shard_map/all_to_all | solution.py:223
  161.3 117.8 %all-gather.6.cloned.1.call-start = ((), (), s32[]{:S(2)}) async-start(), calls=%async_computation.5 | async-start | bytes 2293760 | tf_op jit(solution)/shard_map/all_gather | solution.py:202
  198.0 5.9 %copy-start.1 = (bf16[64,32,384]{2,1,0:T(8,128)(2,1)}, bf16[64,32,384]{2,1,0:T(8,128)(2,1)S(1)}, u32[]{:S(2)}) copy-start(bf16[64,32,384]{2,1,0:T(8,128)(2,1)S(1)} %all-to-all-done.2.arrived) | copy-start | bytes 4718596
  198.0 46.2 %all-to-all-start.1 = ((bf16[64,32,384]{2,1,0:T(8,128)(2,1)}), bf16[64,32,384]{2,1,0:T(8,128)(2,1)S(1)}, u32[]{:S(2)}, u32[]{:S(2)}) async-start(bf16[64,32,384]{2,1,0:T(8,128)(2,1)} %get-tuple-element.30), calls=%async_computation.1 | async-start | bytes 3145728 | tf_op jit(solution)/shard_map/all_to_all | solution.py:223
  201.6 77.5 %all-gather.8.cloned.1.call-start = ((), (), s32[]{:S(2)}) async-start(), calls=%async_computation.6 | async-start | bytes 2293760 | tf_op jit(solution)/shard_map/all_gather | solution.py:203
  203.9 38.5 %copy-start.3 = (bf16[256,2048]{1,0:T(8,128)(2,1)S(1)}, bf16[256,2048]{1,0:T(8,128)(2,1)}, u32[]{:S(2)}) copy-start(bf16[256,2048]{1,0:T(8,128)(2,1)} %param.7) | copy-start | bytes 3145732
  214.1 57.2 %collective-permute-start.6 = (bf16[8,32,128]{2,1,0:T(8,128)(2,1)}, bf16[8,32,128]{2,1,0:T(8,128)(2,1)S(1)}, u32[]{:S(2)}, u32[]{:S(2)}) collective-permute-start(bf16[8,32,128]{2,1,0:T(8,128)(2,1)} %get-tuple-element.42), channel_id=1, source_target_pairs={{0,1},{1,0},{2,3},{3,2},{4,5},{5,4},{6,7},{7,6},{8,9},{9,8},{10,11... | collective-permute-start | bytes 196616 | tf_op jit(solution)/shard_map/ppermute | solution.py:176
  214.2 58.2 %collective-permute-start.7 = (bf16[8,32,128]{2,1,0:T(8,128)(2,1)}, bf16[8,32,128]{2,1,0:T(8,128)(2,1)S(1)}, u32[]{:S(2)}, u32[]{:S(2)}) collective-permute-start(bf16[8,32,128]{2,1,0:T(8,128)(2,1)} %get-tuple-element.43), channel_id=1, source_target_pairs={{0,2},{1,3},{2,0},{3,1},{4,6},{5,7},{6,4},{7,5},{8,10},{9,11},{10,... | collective-permute-start | bytes 196616 | tf_op jit(solution)/shard_map/ppermute | solution.py:176
  214.8 58.3 %collective-permute-start.8 = (bf16[8,32,128]{2,1,0:T(8,128)(2,1)}, bf16[8,32,128]{2,1,0:T(8,128)(2,1)S(1)}, u32[]{:S(2)}, u32[]{:S(2)}) collective-permute-start(bf16[8,32,128]{2,1,0:T(8,128)(2,1)} %get-tuple-element.44), channel_id=1, source_target_pairs={{0,3},{1,2},{2,1},{3,0},{4,7},{5,6},{6,5},{7,4},{8,11},{9,10},{10,... | collective-permute-start | bytes 196616 | tf_op jit(solution)/shard_map/ppermute | solution.py:176
  242.0 1.7 copy-start.10
  242.0 29.4 %copy-start.9 = (bf16[8,32,384]{2,1,0:T(8,128)(2,1)S(1)}, bf16[8,32,384]{2,1,0:T(8,128)(2,1)}, u32[]{:S(2)}) copy-start(bf16[8,32,384]{2,1,0:T(8,128)(2,1)} %get-tuple-element.39) | copy-start | bytes 589828
  242.0 31.6 %collective-permute-start.3 = (bf16[8,32,384]{2,1,0:T(8,128)(2,1)}, bf16[8,32,384]{2,1,0:T(8,128)(2,1)S(1)}, u32[]{:S(2)}, u32[]{:S(2)}) collective-permute-start(bf16[8,32,384]{2,1,0:T(8,128)(2,1)} %get-tuple-element.37), channel_id=1, source_target_pairs={{0,1},{1,0},{2,3},{3,2},{4,5},{5,4},{6,7},{7,6},{8,9},{9,8},{10,11... | collective-permute-start | bytes 589832 | tf_op jit(solution)/shard_map/ppermute | solution.py:176
  243.7 35.5 %collective-permute-start.4 = (bf16[8,32,384]{2,1,0:T(8,128)(2,1)S(1)}, bf16[8,32,384]{2,1,0:T(8,128)(2,1)S(1)}, u32[]{:S(2)}, u32[]{:S(2)}) collective-permute-start(bf16[8,32,384]{2,1,0:T(8,128)(2,1)S(1)} %copy-done.10), channel_id=1, source_target_pairs={{0,2},{1,3},{2,0},{3,1},{4,6},{5,7},{6,4},{7,5},{8,10},{9,11},{10,... | collective-permute-start | bytes 589832 | tf_op jit(solution)/shard_map/ppermute | solution.py:176
  271.3 7.8 %copy-start.14 = (bf16[8,32,128]{2,1,0:T(8,128)(2,1)}, bf16[8,32,128]{2,1,0:T(8,128)(2,1)S(1)}, u32[]{:S(2)}) copy-start(bf16[8,32,128]{2,1,0:T(8,128)(2,1)S(1)} %collective-permute-done.6.refs_9_) | copy-start | bytes 196612
  271.4 7.8 %collective-permute-start.5 = (bf16[8,32,384]{2,1,0:T(8,128)(2,1)S(1)}, bf16[8,32,384]{2,1,0:T(8,128)(2,1)S(1)}, u32[]{:S(2)}, u32[]{:S(2)}) collective-permute-start(bf16[8,32,384]{2,1,0:T(8,128)(2,1)S(1)} %copy-done.9), channel_id=1, source_target_pairs={{0,3},{1,2},{2,1},{3,0},{4,7},{5,6},{6,5},{7,4},{8,11},{9,10},{10,... | collective-permute-start | bytes 589832 | tf_op jit(solution)/shard_map/ppermute | solution.py:176
  272.4 6.7 %copy-start.15 = (bf16[8,32,128]{2,1,0:T(8,128)(2,1)}, bf16[8,32,128]{2,1,0:T(8,128)(2,1)S(1)}, u32[]{:S(2)}) copy-start(bf16[8,32,128]{2,1,0:T(8,128)(2,1)S(1)} %collective-permute-done.7.refs_10_) | copy-start | bytes 196612
  272.4 6.8 %collective-permute-start = (bf16[8,32,384]{2,1,0:T(8,128)(2,1)}, bf16[8,32,384]{2,1,0:T(8,128)(2,1)S(1)}, u32[]{:S(2)}, u32[]{:S(2)}) collective-permute-start(bf16[8,32,384]{2,1,0:T(8,128)(2,1)} %get-tuple-element.32), channel_id=1, source_target_pairs={{0,1},{1,0},{2,3},{3,2},{4,5},{5,4},{6,7},{7,6},{8,9},{9,8},{10,11... | collective-permute-start | bytes 589832 | tf_op jit(solution)/shard_map/ppermute | solution.py:176
  273.0 6.1 %copy-start.16 = (bf16[8,32,128]{2,1,0:T(8,128)(2,1)}, bf16[8,32,128]{2,1,0:T(8,128)(2,1)S(1)}, u32[]{:S(2)}) copy-start(bf16[8,32,128]{2,1,0:T(8,128)(2,1)S(1)} %collective-permute-done.8.refs_11_) | copy-start | bytes 196612
  273.0 9.9 %collective-permute-start.1 = (bf16[8,32,384]{2,1,0:T(8,128)(2,1)}, bf16[8,32,384]{2,1,0:T(8,128)(2,1)S(1)}, u32[]{:S(2)}, u32[]{:S(2)}) collective-permute-start(bf16[8,32,384]{2,1,0:T(8,128)(2,1)} %get-tuple-element.33), channel_id=1, source_target_pairs={{0,2},{1,3},{2,0},{3,1},{4,6},{5,7},{6,4},{7,5},{8,10},{9,11},{10,... | collective-permute-start | bytes 589832 | tf_op jit(solution)/shard_map/ppermute | solution.py:176
  273.6 5.5 %copy-start.6 = (bf16[8,32,384]{2,1,0:T(8,128)(2,1)}, bf16[8,32,384]{2,1,0:T(8,128)(2,1)S(1)}, u32[]{:S(2)}) copy-start(bf16[8,32,384]{2,1,0:T(8,128)(2,1)S(1)} %collective-permute-done.3.refs_5_) | copy-start | bytes 589828
  273.6 13.4 %collective-permute-start.2 = (bf16[8,32,384]{2,1,0:T(8,128)(2,1)}, bf16[8,32,384]{2,1,0:T(8,128)(2,1)S(1)}, u32[]{:S(2)}, u32[]{:S(2)}) collective-permute-start(bf16[8,32,384]{2,1,0:T(8,128)(2,1)} %get-tuple-element.34), channel_id=1, source_target_pairs={{0,3},{1,2},{2,1},{3,0},{4,7},{5,6},{6,5},{7,4},{8,11},{9,10},{10,... | collective-permute-start | bytes 589832 | tf_op jit(solution)/shard_map/ppermute | solution.py:176
  279.2 7.8 %copy-start.7 = (bf16[8,32,384]{2,1,0:T(8,128)(2,1)}, bf16[8,32,384]{2,1,0:T(8,128)(2,1)S(1)}, u32[]{:S(2)}) copy-start(bf16[8,32,384]{2,1,0:T(8,128)(2,1)S(1)} %collective-permute-done.4.refs_6_) | copy-start | bytes 589828
  279.2 7.8 %copy-start.8 = (bf16[8,32,384]{2,1,0:T(8,128)(2,1)}, bf16[8,32,384]{2,1,0:T(8,128)(2,1)S(1)}, u32[]{:S(2)}) copy-start(bf16[8,32,384]{2,1,0:T(8,128)(2,1)S(1)} %collective-permute-done.5.refs_7_) | copy-start | bytes 589828
  279.2 7.8 %copy-start.11 = (bf16[8,32,384]{2,1,0:T(8,128)(2,1)}, bf16[8,32,384]{2,1,0:T(8,128)(2,1)S(1)}, u32[]{:S(2)}) copy-start(bf16[8,32,384]{2,1,0:T(8,128)(2,1)S(1)} %collective-permute-done.refs_1_) | copy-start | bytes 589828
  282.9 4.1 %copy-start.12 = (bf16[8,32,384]{2,1,0:T(8,128)(2,1)}, bf16[8,32,384]{2,1,0:T(8,128)(2,1)S(1)}, u32[]{:S(2)}) copy-start(bf16[8,32,384]{2,1,0:T(8,128)(2,1)S(1)} %collective-permute-done.1.refs_2_) | copy-start | bytes 589828
  321.4 18.8 %collective-permute-start.9 = (bf16[16,64,1024]{2,1,0:T(8,128)(2,1)}, bf16[16,64,1024]{2,1,0:T(8,128)(2,1)S(1)}, u32[]{:S(2)}, u32[]{:S(2)}) collective-permute-start(bf16[16,64,1024]{2,1,0:T(8,128)(2,1)} %get-tuple-element.48), channel_id=1, source_target_pairs={{0,1},{1,0},{2,3},{3,2},{4,5},{5,4},{6,7},{7,6},{8,9},{9,8},{10,11... | collective-permute-start | bytes 6291464 | tf_op jit(solution)/shard_map/ppermute | solution.py:176
  328.0 7.1 %collective-permute-start.21 = (bf16[16,32,1024]{2,1,0:T(8,128)(2,1)}, bf16[16,32,1024]{2,1,0:T(8,128)(2,1)S(1)}, u32[]{:S(2)}, u32[]{:S(2)}) collective-permute-start(bf16[16,32,1024]{2,1,0:T(8,128)(2,1)} %get-tuple-element.55), channel_id=1, source_target_pairs={{0,1},{1,0},{2,3},{3,2},{4,5},{5,4},{6,7},{7,6},{8,9},{9,8},{10,11... | collective-permute-start | bytes 3145736 | tf_op jit(solution)/shard_map/ppermute | solution.py:176
  328.4 6.7 %copy-start.4 = (f32[16,32,1024]{2,1,0:T(8,128)S(1)}, f32[16,32,1024]{2,1,0:T(8,128)}, u32[]{:S(2)}) copy-start(f32[16,32,1024]{2,1,0:T(8,128)} %get-tuple-element.54) | copy-start | bytes 6291460
  335.0 8.4 %collective-permute-start.15 = (bf16[16,32,1024]{2,1,0:T(8,128)(2,1)}, bf16[16,32,1024]{2,1,0:T(8,128)(2,1)S(1)}, u32[]{:S(2)}, u32[]{:S(2)}) collective-permute-start(bf16[16,32,1024]{2,1,0:T(8,128)(2,1)} %get-tuple-element.52), channel_id=1, source_target_pairs={{0,1},{1,0},{2,3},{3,2},{4,5},{5,4},{6,7},{7,6},{8,9},{9,8},{10,11... | collective-permute-start | bytes 3145736 | tf_op jit(solution)/shard_map/ppermute | solution.py:176
  335.1 5.1 %copy-start.2 = (f32[16,64,1024]{2,1,0:T(8,128)S(1)}, f32[16,64,1024]{2,1,0:T(8,128)}, u32[]{:S(2)}) copy-start(f32[16,64,1024]{2,1,0:T(8,128)} %get-tuple-element.47) | copy-start | bytes 12582916
  335.6 11.2 %collective-permute-start.24 = (bf16[1,2,2,32,1024]{4,3,2,1,0:T(8,128)(2,1)S(1)}, bf16[1,2,2,32,1024]{4,3,2,1,0:T(8,128)(2,1)S(1)}, u32[]{:S(2)}, u32[]{:S(2)}) collective-permute-start(bf16[1,2,2,32,1024]{4,3,2,1,0:T(8,128)(2,1)S(1)} %bitcast.24), channel_id=1, source_target_pairs={{0,24},{1,25},{2,26},{3,27},{4,28},{5,29},{6,30},{7,31},{8,16},{9,... | collective-permute-start | bytes 786440 | tf_op jit(solution)/shard_map/ppermute | solution.py:176
  339.5 13.4 %collective-permute-start.22 = (bf16[1,2,2,32,1024]{4,3,2,1,0:T(8,128)(2,1)S(1)}, bf16[1,2,2,32,1024]{4,3,2,1,0:T(8,128)(2,1)S(1)}, u32[]{:S(2)}, u32[]{:S(2)}) collective-permute-start(bf16[1,2,2,32,1024]{4,3,2,1,0:T(8,128)(2,1)S(1)} %bitcast.23), channel_id=1, source_target_pairs={{0,8},{1,9},{2,10},{3,11},{4,12},{5,13},{6,14},{7,15},{8,0},{9,1},... | collective-permute-start | bytes 786440 | tf_op jit(solution)/shard_map/ppermute | solution.py:176
  339.5 23.1 %collective-permute-start.23 = (bf16[1,2,2,32,1024]{4,3,2,1,0:T(8,128)(2,1)S(1)}, bf16[1,2,2,32,1024]{4,3,2,1,0:T(8,128)(2,1)S(1)}, u32[]{:S(2)}, u32[]{:S(2)}) collective-permute-start(bf16[1,2,2,32,1024]{4,3,2,1,0:T(8,128)(2,1)S(1)} %bitcast.22), channel_id=1, source_target_pairs={{0,16},{1,17},{2,18},{3,19},{4,20},{5,21},{6,22},{7,23},{8,24},{9,... | collective-permute-start | bytes 786440 | tf_op jit(solution)/shard_map/ppermute | solution.py:176
  341.2 2.2 copy-start.5
  341.4 28.9 %collective-permute-start.10 = (bf16[4,1,2,64,1024]{4,3,2,1,0:T(8,128)(2,1)S(1)}, bf16[4,1,2,64,1024]{4,3,2,1,0:T(8,128)(2,1)S(1)}, u32[]{:S(2)}, u32[]{:S(2)}) collective-permute-start(bf16[4,1,2,64,1024]{4,3,2,1,0:T(8,128)(2,1)S(1)} %slice.196), channel_id=1, source_target_pairs={{0,4},{1,5},{2,6},{3,7},{4,0},{5,1},{6,2},{7,3},{8,12},{9,13},{10,... | collective-permute-start | bytes 3145736 | tf_op jit(solution)/shard_map/ppermute | solution.py:176
  344.0 25.4 %collective-permute-start.16 = (bf16[4,2,1,32,1024]{4,3,2,1,0:T(8,128)(2,1)S(1)}, bf16[4,2,1,32,1024]{4,3,2,1,0:T(8,128)(2,1)S(1)}, u32[]{:S(2)}, u32[]{:S(2)}) collective-permute-start(bf16[4,2,1,32,1024]{4,3,2,1,0:T(8,128)(2,1)S(1)} %slice.197), channel_id=1, source_target_pairs={{0,2},{1,3},{2,0},{3,1},{4,6},{5,7},{6,4},{7,5},{8,10},{9,11},{10,... | collective-permute-start | bytes 1572872 | tf_op jit(solution)/shard_map/ppermute | solution.py:176
  362.8 5.0 %collective-permute-start.25 = (bf16[1,2,1,32,1024]{4,3,2,1,0:T(8,128)(2,1)S(1)}, bf16[1,2,1,32,1024]{4,3,2,1,0:T(8,128)(2,1)S(1)}, u32[]{:S(2)}, u32[]{:S(2)}) collective-permute-start(bf16[1,2,1,32,1024]{4,3,2,1,0:T(8,128)(2,1)S(1)} %slice.200), channel_id=1, source_target_pairs={{0,2},{1,3},{2,0},{3,1},{4,6},{5,7},{6,4},{7,5},{8,10},{9,11},{10,... | collective-permute-start | bytes 393224 | tf_op jit(solution)/shard_map/ppermute | solution.py:176
  367.9 5.0 %collective-permute-start.26 = (bf16[1,1,1,32,1024]{4,3,2,1,0:T(8,128)(2,1)S(1)}, bf16[1,1,1,32,1024]{4,3,2,1,0:T(8,128)(2,1)S(1)}, u32[]{:S(2)}, u32[]{:S(2)}) collective-permute-start(bf16[1,1,1,32,1024]{4,3,2,1,0:T(8,128)(2,1)S(1)} %slice.201), channel_id=1, source_target_pairs={{0,4},{1,5},{2,6},{3,7},{4,0},{5,1},{6,2},{7,3},{8,12},{9,13},{10,... | collective-permute-start | bytes 196616 | tf_op jit(solution)/shard_map/ppermute | solution.py:176
  369.6 7.4 %collective-permute-start.17 = (bf16[4,1,1,32,1024]{4,3,2,1,0:T(8,128)(2,1)S(1)}, bf16[4,1,1,32,1024]{4,3,2,1,0:T(8,128)(2,1)S(1)}, u32[]{:S(2)}, u32[]{:S(2)}) collective-permute-start(bf16[4,1,1,32,1024]{4,3,2,1,0:T(8,128)(2,1)S(1)} %slice.199), channel_id=1, source_target_pairs={{0,4},{1,5},{2,6},{3,7},{4,0},{5,1},{6,2},{7,3},{8,12},{9,13},{10,... | collective-permute-start | bytes 786440 | tf_op jit(solution)/shard_map/ppermute | solution.py:176
  370.7 12.0 %collective-permute-start.11 = (bf16[4,1,1,64,1024]{4,3,2,1,0:T(8,128)(2,1)S(1)}, bf16[4,1,1,64,1024]{4,3,2,1,0:T(8,128)(2,1)S(1)}, u32[]{:S(2)}, u32[]{:S(2)}) collective-permute-start(bf16[4,1,1,64,1024]{4,3,2,1,0:T(8,128)(2,1)S(1)} %slice.198), channel_id=1, source_target_pairs={{0,2},{1,3},{2,0},{3,1},{4,6},{5,7},{6,4},{7,5},{8,10},{9,11},{10,... | collective-permute-start | bytes 1572872 | tf_op jit(solution)/shard_map/ppermute | solution.py:176
  377.1 8.3 %collective-permute-start.18 = (bf16[1,1,1,32,1024]{4,3,2,1,0:T(8,128)(2,1)S(1)}, bf16[1,1,1,32,1024]{4,3,2,1,0:T(8,128)(2,1)S(1)}, u32[]{:S(2)}, u32[]{:S(2)}) collective-permute-start(bf16[1,1,1,32,1024]{4,3,2,1,0:T(8,128)(2,1)S(1)} %get-tuple-element.68), channel_id=1, source_target_pairs={{0,8},{1,9},{2,10},{3,11},{4,12},{5,13},{6,14},{7,15},{8,0},{9,1},... | collective-permute-start | bytes 196616 | tf_op jit(solution)/shard_map/ppermute | solution.py:176
  377.2 9.2 %collective-permute-start.20 = (bf16[1,1,1,32,1024]{4,3,2,1,0:T(8,128)(2,1)S(1)}, bf16[1,1,1,32,1024]{4,3,2,1,0:T(8,128)(2,1)S(1)}, u32[]{:S(2)}, u32[]{:S(2)}) collective-permute-start(bf16[1,1,1,32,1024]{4,3,2,1,0:T(8,128)(2,1)S(1)} %get-tuple-element.69), channel_id=1, source_target_pairs={{0,24},{1,25},{2,26},{3,27},{4,28},{5,29},{6,30},{7,31},{8,16},{9,... | collective-permute-start | bytes 196616 | tf_op jit(solution)/shard_map/ppermute | solution.py:176
  379.6 8.5 %collective-permute-start.19 = (bf16[1,1,1,32,1024]{4,3,2,1,0:T(8,128)(2,1)S(1)}, bf16[1,1,1,32,1024]{4,3,2,1,0:T(8,128)(2,1)S(1)}, u32[]{:S(2)}, u32[]{:S(2)}) collective-permute-start(bf16[1,1,1,32,1024]{4,3,2,1,0:T(8,128)(2,1)S(1)} %get-tuple-element.70), channel_id=1, source_target_pairs={{0,16},{1,17},{2,18},{3,19},{4,20},{5,21},{6,22},{7,23},{8,24},{9,... | collective-permute-start | bytes 196616 | tf_op jit(solution)/shard_map/ppermute | solution.py:176
  382.9 6.0 %collective-permute-start.12 = (bf16[1,1,1,64,1024]{4,3,2,1,0:T(8,128)(2,1)S(1)}, bf16[1,1,1,64,1024]{4,3,2,1,0:T(8,128)(2,1)S(1)}, u32[]{:S(2)}, u32[]{:S(2)}) collective-permute-start(bf16[1,1,1,64,1024]{4,3,2,1,0:T(8,128)(2,1)S(1)} %get-tuple-element.65), channel_id=1, source_target_pairs={{0,8},{1,9},{2,10},{3,11},{4,12},{5,13},{6,14},{7,15},{8,0},{9,1},... | collective-permute-start | bytes 393224 | tf_op jit(solution)/shard_map/ppermute | solution.py:176
  383.0 8.3 %collective-permute-start.14 = (bf16[1,1,1,64,1024]{4,3,2,1,0:T(8,128)(2,1)S(1)}, bf16[1,1,1,64,1024]{4,3,2,1,0:T(8,128)(2,1)S(1)}, u32[]{:S(2)}, u32[]{:S(2)}) collective-permute-start(bf16[1,1,1,64,1024]{4,3,2,1,0:T(8,128)(2,1)S(1)} %get-tuple-element.66), channel_id=1, source_target_pairs={{0,24},{1,25},{2,26},{3,27},{4,28},{5,29},{6,30},{7,31},{8,16},{9,... | collective-permute-start | bytes 393224 | tf_op jit(solution)/shard_map/ppermute | solution.py:176
  385.5 11.1 %collective-permute-start.13 = (bf16[1,1,1,64,1024]{4,3,2,1,0:T(8,128)(2,1)S(1)}, bf16[1,1,1,64,1024]{4,3,2,1,0:T(8,128)(2,1)S(1)}, u32[]{:S(2)}, u32[]{:S(2)}) collective-permute-start(bf16[1,1,1,64,1024]{4,3,2,1,0:T(8,128)(2,1)S(1)} %get-tuple-element.67), channel_id=1, source_target_pairs={{0,16},{1,17},{2,18},{3,19},{4,20},{5,21},{6,22},{7,23},{8,24},{9,... | collective-permute-start | bytes 393224 | tf_op jit(solution)/shard_map/ppermute | solution.py:176
  (2 other events, 1.9 us)
Sparse Core Ops, SparseCore 0:
  9.6 37.2 all-gather.3
  163.7 21.5 all-gather.5
  204.0 24.4 all-gather.7

commit v2 on v1

v2 whole, which is shorter than its diff:
```python
import functools

import jax
import jax.numpy as jnp
from jax import lax
from jax.experimental import pallas as pl
from jax.experimental.pallas import tpu as pltpu
from jax.sharding import PartitionSpec as P

HEAD_DIM = 128
AXES = ("dp", "shard")
LANES = 128
ANY = pl.BlockSpec(memory_space=pl.ANY)
SMEM = pl.BlockSpec(memory_space=pltpu.SMEM)
VMEM = pl.BlockSpec(memory_space=pltpu.VMEM)
VMEM_LIMIT = 56 * 1024 * 1024
F32 = jnp.float32
BF16 = jnp.bfloat16


def lane_cuts(width, shares):
    tiles = width // LANES
    total = sum(shares)
    ends = [0]
    for k in range(1, len(shares) + 1):
        ends.append(round(tiles * sum(shares[:k]) / total) * LANES)
    return [(a, b - a) for a, b in zip(ends, ends[1:]) if b > a]


def serve_kernel(owners, slots, owned, start, after, ids, place, cache, *rest):
    rest = rest[after:]
    outs, (table, sem) = rest[:owners], rest[owners:]
    me = place[0]
    shards, each = ids.shape[0] // owners, ids.shape[1]
    width = outs[0].shape[2]
    for k in range(owners):
        asking = jnp.bitwise_xor(me, k)
        base = k * slots

        def scan(s, at):
            for i in range(each):
                row = ids[asking * shards + s, i] - me * owned
                mine = jnp.logical_and(row >= 0, row < owned)
                table[at] = jnp.clip(row, 0, owned - 1)
                at = jnp.where(mine, at + 1, at)
            return at

        at = lax.fori_loop(0, shards, scan, base)
        for j in range(slots):
            row = jnp.where(base + j < at, table[base + j], 0)
            pltpu.make_async_copy(
                cache.at[row, :, pl.ds(start, width)], outs[k].at[j], sem
            ).start()
    for out in outs:
        pltpu.make_async_copy(out, out, sem).wait()


def pick_kernel(owners, shards, owned, after, ids, place, *rest):
    arrived, rest = rest[:owners], rest[after:]
    outs = rest[owners : owners + shards]
    count, sem = rest[owners + shards :]
    me, shard = place[0], place[1]
    each = ids.shape[1]
    for k in range(owners):
        count[k] = 0

    def locate(s, carry):
        for i in range(each):
            owner = ids[me * shards + s, i] // owned
            at = count[owner]
            count[owner] = at + 1
            count[owners + s * each + i] = at
        return carry

    lax.fori_loop(0, shards, locate, 0)
    for k in range(shards):
        peer = jnp.bitwise_xor(shard, k)
        for j in range(each):
            source = jnp.bitwise_xor(ids[me * shards + peer, j] // owned, me)
            at = count[owners + peer * each + j]
            for n in range(owners):

                @pl.when(source == n)
                def _(n=n, k=k, j=j, at=at):
                    pltpu.make_async_copy(
                        arrived[n].at[at], outs[k].at[j], sem
                    ).start()

    for out in outs:
        pltpu.make_async_copy(out, out, sem).wait()


def concat_kernel(after, *refs):
    out, at = refs[-1], 0
    for ref in refs[: len(refs) - 1 - after]:
        out[at : at + ref.shape[0], :] = ref[...]
        at += ref.shape[0]


def place_blocks(total, rows, place, turn, first, targets):
    me = place[2]
    odd = jnp.bitwise_and(me, 1) == 1
    half = me >> 1
    for d in range(first):
        rel = jnp.bitwise_xor(half, d)
        for order, keep, send, source, into, size in targets:
            even_at = 2 * d * rows + source
            odd_at = even_at + rows
            even_rows = total[even_at : even_at + size, :]
            odd_rows = total[odd_at : odd_at + size, :]
            at = turn(rel, order)
            keep[at, into : into + size, :] = jnp.where(odd, odd_rows, even_rows)
            send[at, into : into + size, :] = jnp.where(odd, even_rows, odd_rows).astype(
                BF16
            )


def combine_kernel(counts, split, after, *refs):
    inputs, outs = [], refs[sum(counts) + after :]
    for count in counts:
        inputs.append(refs[:count])
        refs = refs[count:]
    each = inputs[0][0].shape[0] // split
    for k in range(split):
        at = 0
        for parts in inputs:
            rows = parts[0].shape[1]

            def one(i, carry, k=k, at=at, rows=rows, parts=parts):
                total = parts[0][k * each + i]
                for part in parts[1:]:
                    total = total + part[k * each + i].astype(F32)
                outs[k][i, at : at + rows, :] = total.astype(outs[k].dtype)
                return carry

            lax.fori_loop(0, each, one, 0)
            at += rows


def combine(groups, split, after=()):
    lead, _, columns = groups[0][0].shape
    rows = sum(group[0].shape[1] for group in groups)
    shape = (lead // split, rows, columns)
    flat = [array for group in groups for array in group]
    body = functools.partial(
        combine_kernel, [len(group) for group in groups], split, len(after)
    )
    moved = sum(array.size * array.dtype.itemsize for array in flat)
    keep, *sends = pl.pallas_call(
        body,
        out_shape=[jax.ShapeDtypeStruct(shape, F32)]
        + [jax.ShapeDtypeStruct(shape, BF16)] * (split - 1),
        in_specs=[VMEM] * len(flat) + [ANY] * len(after),
        out_specs=[VMEM] * split,
        compiler_params=pltpu.CompilerParams(vmem_limit_bytes=2 * moved + (4 << 20)),
    )(*flat, *after)
    return keep, sends


def attend_kernel(parts, shards, heads, scale, devices, spans, turn, *refs):
    pieces, refs = refs[: parts * shards], refs[parts * shards :]
    place, queries, cotangent, normed_t, w_key, w_value = refs[:6]
    context, keep_v, send_v, keep_p, send_p, keep_r, send_r = refs[6:13]
    key_rows, value_rows, scores, prob_grads, prob_rounds, score_grads = refs[13:19]
    latents_t, query_grad, key_grad, value_grad, total_v, total_k, total_q = refs[19:]
    nbr, tokens, _ = pieces[0].shape
    step = pl.program_id(0)
    rows = jnp.concatenate(
        [
            jnp.concatenate(
                [
                    pieces[j * shards + k][...].reshape(nbr * tokens, -1)
                    for j in range(parts)
                ],
                axis=1,
            )
            for k in range(shards)
        ],
        axis=0,
    )
    keys, latent = rows.shape
    span, inner = queries.shape
    latents_t[step] = rows.T
    key_rows[...] = jnp.dot(rows, w_key[...], preferred_element_type=F32).astype(BF16)
    value_rows[...] = jnp.dot(rows, w_value[...], preferred_element_type=F32).astype(
        BF16
    )
    dot = functools.partial(lax.dot_general, preferred_element_type=F32)
    nt = (((1,), (1,)), ((), ()))
    nn = (((1,), (0,)), ((), ()))
    tn = (((0,), (0,)), ((), ()))
    of_keys = pl.ds(pl.multiple_of(step * keys, keys), keys)
    of_span = pl.ds(pl.multiple_of(step * span, span), span)

    def at_head(h):
        return slice(h * span, (h + 1) * span), slice(h * HEAD_DIM, (h + 1) * HEAD_DIM)

    for h in range(heads):
        stacked, cols = at_head(h)
        scores[stacked, :] = dot(queries[:, cols], key_rows[:, cols], nt)
        prob_grads[stacked, :] = dot(cotangent[:, cols], value_rows[:, cols], nt)
    for h in range(heads):
        stacked, _ = at_head(h)
        score = scores[stacked, :]
        raised = jnp.exp(score - jnp.max(score, axis=-1, keepdims=True))
        prob = raised * (1.0 / jnp.sum(raised, axis=-1, keepdims=True))
        prob_rounds[stacked, :] = prob.astype(BF16)
        prob_grad = prob_grads[stacked, :]
        inner_sum = jnp.sum(prob * prob_grad, axis=-1, keepdims=True)
        score_grads[stacked, :] = (prob * (prob_grad - inner_sum)).astype(BF16)
    for h in range(heads):
        stacked, cols = at_head(h)
        prob, score_grad = prob_rounds[stacked, :], score_grads[stacked, :]
        context[:, cols] = dot(prob, value_rows[:, cols], nn).astype(BF16)
        value_grad[of_keys, cols] = dot(prob, cotangent[:, cols], tn).astype(BF16)
        query_grad[of_span, cols] = (
            dot(score_grad, key_rows[:, cols], nn) * scale
        ).astype(BF16)
        key_grad[of_keys, cols] = dot(score_grad, queries[:, cols], tn).astype(BF16)

    @pl.when(step == spans - 1)
    def _():
        across = jnp.concatenate([latents_t[c] for c in range(spans)], axis=1)
        of_v, of_p, of_r = (0, keep_v, send_v), (1, keep_p, send_p), (2, keep_r, send_r)
        rows_k, rows_q = keep_v.shape[1], total_q.shape[0] // devices
        shared = keep_p.shape[1] - rows_k
        for total, grad, target in ((total_v, value_grad, of_v), (total_k, key_grad, of_p)):
            total[:latent, :] = dot(across, grad[...], nn)
            total[latent:, :] = jnp.zeros((total.shape[0] - latent, inner), F32)
            place_blocks(
                total, latent // devices, place, turn, devices // 2, [target + (0, 0, rows_k)]
            )
        total_q[...] = dot(normed_t[...], query_grad[...], nn)
        targets = [of_r + (shared, 0, rows_q - shared)]
        if shared:
            targets.append(of_p + (0, rows_k, shared))
        place_blocks(total_q, rows_q, place, turn, devices // 2, targets)


def swap(value, bit, devices):
    return lax.ppermute(value, AXES, [(i, i ^ bit) for i in range(devices)])


def body(tokens, ctx_cotangent, latent_cache, nbr_ids, w_query, w_key, w_value):
    owners, shards = lax.axis_size("dp"), lax.axis_size("shard")
    devices = owners * shards
    owned, slice_tokens, latent = latent_cache.shape
    spans, nbr = nbr_ids.shape
    each = spans * nbr
    group = each * shards
    slots = 2 * group // owners
    inner = w_query.shape[1]
    heads = inner // HEAD_DIM
    scale = HEAD_DIM**-0.5
    span = tokens.shape[0] // spans
    dp, shard = lax.axis_index("dp"), lax.axis_index("shard")
    place = jnp.stack([dp, shard, dp * shards + shard]).astype(jnp.int32)

    ids = lax.all_to_all(
        jnp.broadcast_to(nbr_ids.reshape(1, each), (devices, each)),
        AXES,
        split_axis=0,
        concat_axis=0,
        tiled=True,
    )
    as_float = tokens.astype(F32)
    normed = (
        as_float
        * lax.rsqrt(jnp.mean(as_float * as_float, axis=-1, keepdims=True) + 1e-06)
    ).astype(BF16)

    pieces = []
    cuts = lane_cuts(latent, (3, 3, 1))
    before = []
    for turn_at, (start, width) in enumerate(cuts):
        served = pl.pallas_call(
            functools.partial(serve_kernel, owners, slots, owned, start, len(before)),
            out_shape=[jax.ShapeDtypeStruct((slots, slice_tokens, width), BF16)]
            * owners,
            in_specs=[SMEM, SMEM, ANY] + [ANY] * len(before),
            out_specs=[VMEM] * owners,
            scratch_shapes=[
                pltpu.SMEM((owners * slots + 1,), jnp.int32),
                pltpu.SemaphoreType.DMA,
            ],
            compiler_params=pltpu.CompilerParams(vmem_limit_bytes=16 << 20),
        )(ids, place, latent_cache, *before)
        arrived = [
            part if k == 0 else swap(part, k * shards, devices)
            for k, part in enumerate(served)
        ]
        if turn_at == 0:
            heights = [w.shape[0] for w in (w_query, w_key, w_value)]
            weights = pl.pallas_call(
                functools.partial(concat_kernel, 1),
                out_shape=jax.ShapeDtypeStruct((sum(heights), inner), BF16),
                in_specs=[VMEM] * 3 + [ANY],
                out_specs=VMEM,
                compiler_params=pltpu.CompilerParams(vmem_limit_bytes=16 << 20),
            )(w_query, w_key, w_value, served[0])
            before = [weights]
            weights = lax.all_gather(weights, "shard", axis=0)
            a, b = heights[0], heights[0] + heights[1]
            query_full = weights[:, :a].reshape(-1, inner)
            key_full = weights[:, a:b].reshape(-1, inner)
            value_full = weights[:, b:].reshape(-1, inner)
            query_sum = jnp.dot(normed, query_full, preferred_element_type=F32)
            queries = (query_sum * scale).astype(BF16)
            normed_t = normed.T
        else:
            before = [served[0]]
        ready = []
        if turn_at == len(cuts) - 1:
            ready = [queries, key_full, value_full, normed_t]
        picked = pl.pallas_call(
            functools.partial(pick_kernel, owners, shards, owned, len(ready)),
            out_shape=[jax.ShapeDtypeStruct((each, slice_tokens, width), BF16)]
            * shards,
            in_specs=[SMEM, SMEM] + [ANY] * (owners + len(ready)),
            out_specs=[VMEM] * shards,
            scratch_shapes=[
                pltpu.SMEM((owners + group,), jnp.int32),
                pltpu.SemaphoreType.DMA,
            ],
            compiler_params=pltpu.CompilerParams(vmem_limit_bytes=16 << 20),
        )(ids, place, *arrived, *ready)
        pieces += [
            piece if k == 0 else swap(piece, k, devices)
            for k, piece in enumerate(picked)
        ]

    keys = nbr * shards * slice_tokens
    width_q = tokens.shape[1]
    by_span = pl.BlockSpec((span, inner), lambda c: (c, 0))

    def fixed(*shape):
        return pl.BlockSpec(
            shape, lambda c: (0,) * len(shape), pipeline_mode=pl.Buffered(1)
        )

    low = 1 << (owners.bit_length() - 1) // 2
    length = dict(z=owners // low, x=low, y=shards // 2)
    bit = dict(z=low * shards, x=shards, y=2)
    orders = ("zyx", "yxz", "xyz")

    def turn(rel, which):
        at = dict(
            y=rel % length["y"],
            x=rel // length["y"] % length["x"],
            z=rel // (length["y"] * length["x"]),
        )
        first, second, third = orders[which]
        return (at[first] * length[second] + at[second]) * length[third] + at[third]

    rows_k = -(-latent // devices // 16) * 16
    rows_q = width_q // devices
    shared = max(0, (rows_k + rows_q) // 32 * 16 - rows_k)
    blocks, block_specs = [], []
    for rows in (rows_k, rows_k + shared, rows_q - shared):
        for kind in (F32, BF16):
            shape = (devices // 2, rows, inner)
            blocks.append(jax.ShapeDtypeStruct(shape, kind))
            block_specs.append(fixed(*shape))
    spare = rows_k
    context, *blocks = pl.pallas_call(
        functools.partial(
            attend_kernel,
            len(pieces) // shards,
            shards,
            heads,
            scale,
            devices,
            spans,
            turn,
        ),
        grid=(spans,),
        out_shape=[jax.ShapeDtypeStruct((spans * span, inner), BF16)] + blocks,
        in_specs=[
            pl.BlockSpec((nbr, slice_tokens, piece.shape[2]), lambda c: (c, 0, 0))
            for piece in pieces
        ]
        + [SMEM, by_span, by_span, fixed(width_q, spans * span)]
        + [fixed(latent, inner)] * 2,
        out_specs=[by_span] + block_specs,
        scratch_shapes=[pltpu.VMEM((keys, inner), BF16)] * 2
        + [pltpu.VMEM((heads * span, keys), F32)] * 2
        + [pltpu.VMEM((heads * span, keys), BF16)] * 2
        + [
            pltpu.VMEM((spans, latent, keys), BF16),
            pltpu.VMEM((spans * span, inner), BF16),
        ]
        + [pltpu.VMEM((spans * keys, inner), BF16)] * 2
        + [pltpu.VMEM((latent + spare, inner), F32)] * 2
        + [pltpu.VMEM((width_q, inner), F32)],
        compiler_params=pltpu.CompilerParams(vmem_limit_bytes=VMEM_LIMIT),
        cost_estimate=pl.CostEstimate(
            flops=2 * inner * (4 * spans * keys * (latent + 2 * span) + tokens.size),
            bytes_accessed=12 * (2 * latent + width_q) * inner,
            transcendentals=spans * span * keys * heads,
        ),
    )(*pieces, place, queries, ctx_cotangent, normed_t, key_full, value_full)

    def travel(sends, axis):
        return [swap(part, k * bit[axis], devices) for k, part in enumerate(sends, 1)]

    keep_v, send_v, keep_p, send_p, keep_r, send_r = blocks
    came_v, came_p, came_r = (swap(s, 1, devices) for s in (send_v, send_p, send_r))
    keep_v, sends = combine([[keep_v, came_v]], length["z"])
    came_v = travel(sends, "z")
    keep_p, sends = combine([[keep_p, came_p]], length["y"], sends[:1])
    came_p = travel(sends, "y")
    keep_r, sends = combine([[keep_r, came_r]], length["x"], sends[:1])
    came_r = travel(sends, "x")
    keep_p, sends = combine([[keep_p, *came_p]], length["x"], sends[:1])
    came_p = travel(sends, "x")
    keep_r, sends = combine([[keep_r, *came_r]], length["y"], sends[:1])
    came_r = travel(sends, "y")
    keep_v, sends = combine([[keep_v, *came_v]], length["y"], sends[:1])
    came_v = travel(sends, "y")
    keep, sends = combine(
        [[keep_p, *came_p], [keep_r, *came_r]], length["z"], sends[:1]
    )
    came = travel(sends, "z")
    keep_v, sends = combine([[keep_v, *came_v]], length["x"], sends[:1])
    came_v = travel(sends, "x")

    def whole_sum(parts):
        return sum((part[0].astype(F32) for part in parts[1:]), parts[0][0])

    grad_value = whole_sum([keep_v, *came_v])[: latent // devices]
    rest = whole_sum([keep, *came])
    grad_key, grad_query = rest[: latent // devices], rest[rows_k:]
    return context, grad_query, grad_key, grad_value


def solution(mesh):
    rows = P(AXES, None)
    by_shard = P("shard", None)
    return jax.shard_map(
        body,
        mesh=mesh,
        in_specs=(rows, rows, P("dp", "shard", None), rows)
        + (by_shard, by_shard, by_shard),
        out_specs=(rows, rows, rows, rows),
        check_vma=False,
    )
```

time: 404 us -> 237 us (0.59)
  Pallas kernels: 222 us -> 45 us
  starting transfers between devices: 41.8 us -> 73.3 us
  blocking collectives: 18.9 us -> 0 us
  local copies, waits for them, and re-layouts: 5.07 us -> 22.3 us
  waiting for transfers between devices: 88.2 us -> 78 us
  other arithmetic: 9.08 us -> 2.57 us
    pallas_call x8 -> x16, Pallas kernels: 222 us -> 45 us  [the longest x1 22.8 us: body(): pl.pallas_call(functools.partial(attend_kernel, len(pieces) // shards, sh...]
    ppermute x27 -> x45, starting transfers between devices: 27.1 us -> 65.9 us  [swap(): return lax.ppermute(value, AXES, [(i, i ^ bit) for i in range(devices)])]
    all_to_all x2 -> x0, waiting for transfers between devices: 35.9 us -> none  [body(): lax.all_to_all(rows, 'dp', split_axis=0, concat_axis=0, tiled=True)]
    ppermute x27 -> x45, waiting for transfers between devices: 43.8 us -> 71.1 us  [swap(): return lax.ppermute(value, AXES, [(i, i ^ bit) for i in range(devices)])]
    all_to_all x1 -> x0, blocking collectives: 18.9 us -> none  [body(): lax.all_to_all(rows, 'dp', split_axis=0, concat_axis=0, tiled=True)]
    unnamed x35 -> x64, local copies, waits for them, and re-layouts: 2.7 us -> 14.9 us
    all_to_all x2 -> x0, starting transfers between devices: 7.27 us -> none  [body(): lax.all_to_all(rows, 'dp', split_axis=0, concat_axis=0, tiled=True)]
    slice x12 -> x4, local copies, waits for them, and re-layouts: 0.53 us -> 6.62 us  [the longest x1 2.73 us: body(): query_full = weights[:, :a].reshape(-1, inner)]
  transfers between devices with their start and end apart: 33 -> 47, of which waited for: 14 -> 19; matrix products, arithmetic and copies ran while one was open for 4% -> 5% of each run, Pallas kernels for 47% -> 8%
where the time goes in v2:
time: 237 us
  waiting for transfers between devices  78 us (33%)
  starting transfers between devices  73.3 us (31%)
  Pallas kernels  45 us (19%)
  local copies, waits for them, and re-layouts  22.3 us (9%)
  between operations  14.5 us (6%)
  other arithmetic  2.57 us (1%)
    ppermute x45, waiting for transfers between devices, swap(): return lax.ppermute(value, AXES, [(i, i ^ bit) for i in range(devices)])  71.1 us
    ppermute x45, starting transfers between devices, swap(): return lax.ppermute(value, AXES, [(i, i ^ bit) for i in range(devices)])  65.9 us
    pallas_call x1, Pallas kernels, body(): pl.pallas_call(functools.partial(attend_kernel, len(pieces) // shards, sh...  22.8 us
    unnamed x64, local copies, waits for them, and re-layouts  14.9 us
    pallas_call x3, Pallas kernels, body(): pl.pallas_call(functools.partial(pick_kernel, owners, shards, owned, len(...  10.9 us
    pallas_call x3, Pallas kernels, body(): pl.pallas_call(functools.partial(serve_kernel, owners, slots, owned, star...  8.29 us
    all_to_all x1, starting transfers between devices, body(): lax.all_to_all(jnp.broadcast_to(nbr_ids.reshape(1, each), (devices, each)...  7.3 us
    all_to_all x1, waiting for transfers between devices, body(): lax.all_to_all(jnp.broadcast_to(nbr_ids.reshape(1, each), (devices, each)...  6.94 us
  transfers between devices with their start and end apart: 47, of which 19 were waited for; matrix products, arithmetic and copies ran while one was open for 5% of the time, Pallas kernels for 8%

profile of v2, /device:TPU:0, one launch (start us, length us, event | category | flops | bytes accessed | tf_op | source)
XLA Modules:
  0.0 236.9 jit_solution(15202321412041574988)
XLA Ops:
  8.6 7.3 %all-to-all-start = ((s32[32,1,8]{2,1,0:T(1,128)}), s32[32,1,8]{2,1,0:T(1,128)S(1)}, u32[]{:S(2)}, u32[]{:S(2)}) async-start(s32[32,1,8]{2,1,0:T(1,128)} %broadcast_in_dim.9), calls=%async_computation | async-start | bytes 32768 | tf_op jit(solution)/shard_map/all_to_all | solution.py:259
  16.1 6.9 %all-to-all-done = s32[32,1,8]{2,1,0:T(1,128)S(1)} async-done(((s32[32,1,8]{2,1,0:T(1,128)}), s32[32,1,8]{2,1,0:T(1,128)S(1)}, u32[]{:S(2)}, u32[]{:S(2)}) %all-to-all-start) | async-done | bytes 1056 | tf_op jit(solution)/shard_map/all_to_all | solution.py:259
  23.0 3.1 %copy-done = bf16[128,32,896]{2,1,0:T(8,128)(2,1)S(1)} copy-done((bf16[128,32,896]{2,1,0:T(8,128)(2,1)S(1)}, bf16[128,32,896]{2,1,0:T(8,128)(2,1)}, u32[]{:S(2)}) %copy-start) | copy-done | bytes 7340056
  26.1 2.6 %shard_map.102 = (bf16[8,32,384]{2,1,0:T(8,128)(2,1)S(1)}, bf16[8,32,384]{2,1,0:T(8,128)(2,1)S(1)}, bf16[8,32,384]{2,1,0:T(8,128)(2,1)S(1)}, bf16[8,32,384]{2,1,...) custom-call(s32[32,8]{1,0:T(8,128)S(1)} %bitcast.21, ...), custom_call_target="tpu_custom_call" | custom-call | tf_op jit(solution)/shard_map/pallas_call | solution.py:276
  28.7 1.4 shard_map.104.rest_0_
  31.4 2.3 collective-permute-start.2
  34.3 2.3 collective-permute-start.4
  37.4 6.4 %collective-permute-done.1.rest_2_ = bf16[8,32,384]{2,1,0:T(8,128)(2,1)S(1)} collective-permute-done((bf16[8,32,384]{2,1,0:T(8,128)(2,1)S(1)}, bf16[8,32,384]{2,1,0:T(8,128)(2,1)S(1)}, u32[]{:S(2)}, u32[]{:S(2)}) %collective-permute-start.1) | collective-permute-done | bytes 196640 | tf_op jit(solution)/shard_map/ppermute | solution.py:241
  43.8 3.7 %collective-permute-start.6 = (bf16[8,32,384]{2,1,0:T(8,128)(2,1)S(1)}, bf16[8,32,384]{2,1,0:T(8,128)(2,1)S(1)}, u32[]{:S(2)}, u32[]{:S(2)}) collective-permute-start(bf16[8,32,384]{2,1,0:T(8,128)(2,1)S(1)} %get-tuple-element.74), channel_id=1, source_target_pairs={{0,28},{1,29},{2,30},{3,31},{4,24},{5,25},{6,26},{7,27},{8,20},{9,... | collective-permute-start | bytes 589832 | tf_op jit(solution)/shard_map/ppermute | solution.py:241
  47.5 2.3 copy.16
  49.8 1.5 fusion
  51.3 3.1 %copy-done.1 = bf16[128,32,896]{2,1,0:T(8,128)(2,1)S(1)} copy-done((bf16[128,32,896]{2,1,0:T(8,128)(2,1)S(1)}, bf16[128,32,896]{2,1,0:T(8,128)(2,1)}, u32[]{:S(2)}) %copy-start.1) | copy-done | bytes 7340056
  54.4 2.6 %shard_map.105 = (bf16[8,32,384]{2,1,0:T(8,128)(2,1)S(1)}, bf16[8,32,384]{2,1,0:T(8,128)(2,1)S(1)}, bf16[8,32,384]{2,1,0:T(8,128)(2,1)S(1)}, bf16[8,32,384]{2,1,...) custom-call(s32[32,8]{1,0:T(8,128)S(1)} %bitcast.22, ...), custom_call_target="tpu_custom_call" | custom-call | tf_op jit(solution)/shard_map/pallas_call | solution.py:276
  57.1 1.9 collective-permute-done.3.rest_4_
  59.0 4.5 %collective-permute-done.4.rest_5_ = bf16[8,32,384]{2,1,0:T(8,128)(2,1)S(1)} collective-permute-done((bf16[8,32,384]{2,1,0:T(8,128)(2,1)S(1)}, bf16[8,32,384]{2,1,0:T(8,128)(2,1)S(1)}, u32[]{:S(2)}, u32[]{:S(2)}) %collective-permute-start.4) | collective-permute-done | bytes 196640 | tf_op jit(solution)/shard_map/ppermute | solution.py:241
  63.5 5.2 %collective-permute-start.13 = (bf16[8,32,384]{2,1,0:T(8,128)(2,1)S(1)}, bf16[8,32,384]{2,1,0:T(8,128)(2,1)S(1)}, u32[]{:S(2)}, u32[]{:S(2)}) collective-permute-start(bf16[8,32,384]{2,1,0:T(8,128)(2,1)S(1)} %get-tuple-element.83), channel_id=1, source_target_pairs={{0,16},{1,17},{2,18},{3,19},{4,20},{5,21},{6,22},{7,23},{8,24},{9,... | collective-permute-start | bytes 589832 | tf_op jit(solution)/shard_map/ppermute | solution.py:241
  68.8 10.1 %collective-permute-start.14 = (bf16[8,32,384]{2,1,0:T(8,128)(2,1)S(1)}, bf16[8,32,384]{2,1,0:T(8,128)(2,1)S(1)}, u32[]{:S(2)}, u32[]{:S(2)}) collective-permute-start(bf16[8,32,384]{2,1,0:T(8,128)(2,1)S(1)} %get-tuple-element.84), channel_id=1, source_target_pairs={{0,20},{1,21},{2,22},{3,23},{4,16},{5,17},{6,18},{7,19},{8,28},{9,... | collective-permute-start | bytes 589832 | tf_op jit(solution)/shard_map/ppermute | solution.py:241
  78.9 3.1 %shard_map.107 = (bf16[8,32,128]{2,1,0:T(8,128)(2,1)S(1)}, bf16[8,32,128]{2,1,0:T(8,128)(2,1)}, bf16[8,32,128]{2,1,0:T(8,128)(2,1)}, bf16[8,32,128]{2,1,0:T(8,12...) custom-call(s32[32,8]{1,0:T(8,128)S(1)} %bitcast.23, ...), custom_call_target="tpu_custom_call" | custom-call | tf_op jit(solution)/shard_map/pallas_call | solution.py:276
  82.6 7.5 %collective-permute-start.15 = (bf16[8,32,384]{2,1,0:T(8,128)(2,1)S(1)}, bf16[8,32,384]{2,1,0:T(8,128)(2,1)S(1)}, u32[]{:S(2)}, u32[]{:S(2)}) collective-permute-start(bf16[8,32,384]{2,1,0:T(8,128)(2,1)S(1)} %get-tuple-element.85), channel_id=1, source_target_pairs={{0,24},{1,25},{2,26},{3,27},{4,28},{5,29},{6,30},{7,31},{8,16},{9,... | collective-permute-start | bytes 589832 | tf_op jit(solution)/shard_map/ppermute | solution.py:241
  90.4 1.2 collective-permute-start.20
  91.6 3.7 %collective-permute-done.14.rest_5_ = bf16[8,32,384]{2,1,0:T(8,128)(2,1)S(1)} collective-permute-done((bf16[8,32,384]{2,1,0:T(8,128)(2,1)S(1)}, bf16[8,32,384]{2,1,0:T(8,128)(2,1)S(1)}, u32[]{:S(2)}, u32[]{:S(2)}) %collective-permute-start.14) | collective-permute-done | bytes 196640 | tf_op jit(solution)/shard_map/ppermute | solution.py:241
  95.5 3.8 %shard_map.103 = (bf16[8,32,384]{2,1,0:T(8,128)(2,1)S(1)}, bf16[8,32,384]{2,1,0:T(8,128)(2,1)S(1)}, bf16[8,32,384]{2,1,0:T(8,128)(2,1)S(1)}, bf16[8,32,384]{2,1,0:T(8,128)(2,1)S(1)}) custom-call(s32[32,8]{1,0:T(8,128)S(1)} %bitcast.24, s32[3]{0:T(128)S(1)} %pad_add_fusion.place.refs_12_, bf16[8,32,384]{2,1,0:T(8,128)(2,1)S(1)} %get-tuple-element.67.rest_0_.refs_3_, ...), custom_call_target="tpu_custom_call" | custom-call | tf_op jit(solution)/shard_map/pallas_call | solution.py:315
  100.1 1.8 collective-permute-start.23
  101.9 4.0 %collective-permute-start.24 = (bf16[8,32,128]{2,1,0:T(8,128)(2,1)}, bf16[8,32,128]{2,1,0:T(8,128)(2,1)S(1)}, u32[]{:S(2)}, u32[]{:S(2)}) collective-permute-start(bf16[8,32,128]{2,1,0:T(8,128)(2,1)} %get-tuple-element.96), channel_id=1, source_target_pairs={{0,20},{1,21},{2,22},{3,23},{4,16},{5,17},{6,18},{7,19},{8,28},{9,... | collective-permute-start | bytes 196616 | tf_op jit(solution)/shard_map/ppermute | solution.py:241
  105.9 4.0 %shard_map.106 = (bf16[8,32,384]{2,1,0:T(8,128)(2,1)S(1)}, bf16[8,32,384]{2,1,0:T(8,128)(2,1)S(1)}, bf16[8,32,384]{2,1,0:T(8,128)(2,1)S(1)}, bf16[8,32,384]{2,1,0:T(8,128)(2,1)S(1)}) custom-call(s32[32,8]{1,0:T(8,128)S(1)} %bitcast.25, s32[3]{0:T(128)S(1)} %pad_add_fusion.place.refs_12_, bf16[8,32,384]{2,1,0:T(8,128)(2,1)S(1)} %get-tuple-element.79.rest_0_, ...), custom_call_target="tpu_custom_call" | custom-call | tf_op jit(solution)/shard_map/pallas_call | solution.py:315
  110.6 2.7 %slice.36 = bf16[4,512,1024]{2,1,0:T(8,128)(2,1)S(1)} slice(bf16[4,960,1024]{2,1,0:T(8,128)(2,1)} %bitcast.27), slice={[0:4], [0:512], [0:1024]} | slice | bytes 8388608 | tf_op jit(solution)/shard_map/slice | solution.py:304
  113.3 3.9 %collective-permute-start.25 = (bf16[8,32,128]{2,1,0:T(8,128)(2,1)S(1)}, bf16[8,32,128]{2,1,0:T(8,128)(2,1)S(1)}, u32[]{:S(2)}, u32[]{:S(2)}) collective-permute-start(bf16[8,32,128]{2,1,0:T(8,128)(2,1)S(1)} %copy-done.18), channel_id=1, source_target_pairs={{0,24},{1,25},{2,26},{3,27},{4,28},{5,29},{6,30},{7,31},{8,16},{9,... | collective-permute-start | bytes 196616 | tf_op jit(solution)/shard_map/ppermute | solution.py:241
  117.7 1.3 fusion.2.rest_8_.refs_13_
  119.6 1.3 collective-permute-start.9
  121.2 3.0 %collective-permute-done.26.rest_7_ = bf16[8,32,128]{2,1,0:T(8,128)(2,1)S(1)} collective-permute-done((bf16[8,32,128]{2,1,0:T(8,128)(2,1)S(1)}, bf16[8,32,128]{2,1,0:T(8,128)(2,1)S(1)}, u32[]{:S(2)}, u32[]{:S(2)}) %collective-permute-start.26) | collective-permute-done | bytes 65568 | tf_op jit(solution)/shard_map/ppermute | solution.py:241
  124.7 2.5 %fusion.6 = (bf16[4,224,1024]{2,1,0:T(8,128)(2,1)S(1)}, bf16[4,224,1024]{2,1,0:T(8,128)(2,1)S(1)}) fusion(bf16[4,960,1024]{2,1,0:T(8,128)(2,1)} %bitcast.28), kind=kLoop, calls=%fused_computation.14 | loop fusion | bytes 7340032 | tf_op jit(solution)/shard_map/slice | solution.py:306
  127.3 3.1 %shard_map.108 = (bf16[8,32,128]{2,1,0:T(8,128)(2,1)S(1)}, bf16[8,32,128]{2,1,0:T(8,128)(2,1)S(1)}, bf16[8,32,128]{2,1,0:T(8,128)(2,1)S(1)}, bf16[8,32,128]{2,1,0:T(8,128)(2,1)S(1)}) custom-call(s32[32,8]{1,0:T(8,128)S(1)} %bitcast.26, s32[3]{0:T(128)S(1)} %pad_add_fusion.place.refs_12_, bf16[8,32,128]{2,1,0:T(8,128)(2,1)S(1)} %get-tuple-element.91.rest_0_, ...), custom_call_target="tpu_custom_call" | custom-call | tf_op jit(solution)/shard_map/pallas_call | solution.py:315
  131.0 1.5 collective-permute-start.27
  135.2 3.4 %collective-permute-done.19.refs_7_ = bf16[8,32,384]{2,1,0:T(8,128)(2,1)S(1)} collective-permute-done((bf16[8,32,384]{2,1,0:T(8,128)(2,1)S(1)}, bf16[8,32,384]{2,1,0:T(8,128)(2,1)S(1)}, u32[]{:S(2)}, u32[]{:S(2)}) %collective-permute-start.19) | collective-permute-done | bytes 196640 | tf_op jit(solution)/shard_map/ppermute | solution.py:241
  138.6 2.2 collective-permute-done.28.refs_10_
  142.0 22.8 %shard_map.109 = (bf16[256,1024]{1,0:T(8,128)(2,1)}, f32[16,32,1024]{2,1,0:T(8,128)}, bf16[16,32,1024]{2,1,0:T(8,128)(2,1)}, f32[16,48,1024]{2,1,0:T(8,128)}, bf...) custom-call(bf16[8,32,384]{2,1,0:T(8,128)(2,1)} %copy-done.13, ...), custom_call_target="tpu_custom_call" | custom-call | flops 9663676416 | bytes 47185920 | tf_op jit(solution)/shard_map/pallas_call | solution.py:365
  165.7 6.6 %collective-permute-done.31.refs_1_ = bf16[16,32,1024]{2,1,0:T(8,128)(2,1)S(1)} collective-permute-done((bf16[16,32,1024]{2,1,0:T(8,128)(2,1)}, bf16[16,32,1024]{2,1,0:T(8,128)(2,1)S(1)}, u32[]{:S(2)}, u32[]{:S(2)}) %collective-permute-start.31) | collective-permute-done | bytes 1048608 | tf_op jit(solution)/shard_map/ppermute | solution.py:241
  172.3 1.6 copy-done.7
  176.4 1.2 collective-permute-start.35
  177.6 4.3 %collective-permute-start.38 = (bf16[4,32,1024]{2,1,0:T(8,128)(2,1)S(1)}, bf16[4,32,1024]{2,1,0:T(8,128)(2,1)S(1)}, u32[]{:S(2)}, u32[]{:S(2)}) collective-permute-start(bf16[4,32,1024]{2,1,0:T(8,128)(2,1)S(1)} %get-tuple-element.120), channel_id=1, source_target_pairs={{0,16},{1,17},{2,18},{3,19},{4,20},{5,21},{6,22},{7,23},{8,24},{9,... | collective-permute-start | bytes 786440 | tf_op jit(solution)/shard_map/ppermute | solution.py:241
  182.0 12.3 %collective-permute-done.32.refs_1_ = bf16[8,48,1024]{2,1,0:T(8,128)(2,1)S(1)} collective-permute-done((bf16[8,48,1024]{2,1,0:T(8,128)(2,1)S(1)}, bf16[8,48,1024]{2,1,0:T(8,128)(2,1)S(1)}, u32[]{:S(2)}, u32[]{:S(2)}) %collective-permute-start.32) | collective-permute-done | bytes 786464 | tf_op jit(solution)/shard_map/ppermute | solution.py:241
  194.4 1.2 collective-permute-start.34
  196.9 3.4 %collective-permute-done.38.refs_2_ = bf16[4,32,1024]{2,1,0:T(8,128)(2,1)S(1)} collective-permute-done((bf16[4,32,1024]{2,1,0:T(8,128)(2,1)S(1)}, bf16[4,32,1024]{2,1,0:T(8,128)(2,1)S(1)}, u32[]{:S(2)}, u32[]{:S(2)}) %collective-permute-start.38) | collective-permute-done | bytes 262176 | tf_op jit(solution)/shard_map/ppermute | solution.py:241
  201.0 3.9 %collective-permute-done.34.refs_1_ = bf16[4,48,1024]{2,1,0:T(8,128)(2,1)S(1)} collective-permute-done((bf16[4,48,1024]{2,1,0:T(8,128)(2,1)S(1)}, bf16[4,48,1024]{2,1,0:T(8,128)(2,1)S(1)}, u32[]{:S(2)}, u32[]{:S(2)}) %collective-permute-start.34) | collective-permute-done | bytes 393248 | tf_op jit(solution)/shard_map/ppermute | solution.py:241
  204.9 3.3 %collective-permute-done.36.refs_3_ = bf16[4,48,1024]{2,1,0:T(8,128)(2,1)S(1)} collective-permute-done((bf16[4,48,1024]{2,1,0:T(8,128)(2,1)S(1)}, bf16[4,48,1024]{2,1,0:T(8,128)(2,1)S(1)}, u32[]{:S(2)}, u32[]{:S(2)}) %collective-permute-start.36) | collective-permute-done | bytes 393248 | tf_op jit(solution)/shard_map/ppermute | solution.py:241
  208.4 1.2 collective-permute-done.43.refs_1_
  211.2 3.8 %collective-permute-start.41 = (bf16[1,96,1024]{2,1,0:T(8,128)(2,1)S(1)}, bf16[1,96,1024]{2,1,0:T(8,128)(2,1)S(1)}, u32[]{:S(2)}, u32[]{:S(2)}) collective-permute-start(bf16[1,96,1024]{2,1,0:T(8,128)(2,1)S(1)} %get-tuple-element.125), channel_id=1, source_target_pairs={{0,16},{1,17},{2,18},{3,19},{4,20},{5,21},{6,22},{7,23},{8,24},{9,... | collective-permute-start | bytes 589832 | tf_op jit(solution)/shard_map/ppermute | solution.py:241
  215.9 12.7 %collective-permute-done.41 = bf16[1,96,1024]{2,1,0:T(8,128)(2,1)S(1)} collective-permute-done((bf16[1,96,1024]{2,1,0:T(8,128)(2,1)S(1)}, bf16[1,96,1024]{2,1,0:T(8,128)(2,1)S(1)}, u32[]{:S(2)}, u32[]{:S(2)}) %collective-permute-start.41) | collective-permute-done | bytes 196640 | tf_op jit(solution)/shard_map/ppermute | solution.py:241
  (140 shorter events, 22.8 us)
Async XLA Ops:
  8.6 14.4 %all-to-all-start = ((s32[32,1,8]{2,1,0:T(1,128)}), s32[32,1,8]{2,1,0:T(1,128)S(1)}, u32[]{:S(2)}, u32[]{:S(2)}) async-start(s32[32,1,8]{2,1,0:T(1,128)} %broadcast_in_dim.9), calls=%async_computation | async-start | bytes 32768 | tf_op jit(solution)/shard_map/all_to_all | solution.py:259
  15.9 94.6 %all-gather.3.cloned.1.call-start = ((), (), s32[]{:S(2)}) async-start(), calls=%async_computation.1 | async-start | bytes 9830400 | tf_op jit(solution)/shard_map/all_gather | solution.py:302
  16.1 111.2 %copy-start.12 = (s32[3]{0:T(128)}, s32[3]{0:T(128)S(1)}, u32[]{:S(2)}) copy-start(s32[3]{0:T(128)S(1)} %pad_add_fusion.place.refs_12_) | copy-start | bytes 40
  30.2 6.7 %collective-permute-start = (bf16[8,32,384]{2,1,0:T(8,128)(2,1)S(1)}, bf16[8,32,384]{2,1,0:T(8,128)(2,1)S(1)}, u32[]{:S(2)}, u32[]{:S(2)}) collective-permute-start(bf16[8,32,384]{2,1,0:T(8,128)(2,1)S(1)} %get-tuple-element.68), channel_id=1, source_target_pairs={{0,4},{1,5},{2,6},{3,7},{4,0},{5,1},{6,2},{7,3},{8,12},{9,13},{10,... | collective-permute-start | bytes 589832 | tf_op jit(solution)/shard_map/ppermute | solution.py:241
  30.8 13.0 %collective-permute-start.1 = (bf16[8,32,384]{2,1,0:T(8,128)(2,1)S(1)}, bf16[8,32,384]{2,1,0:T(8,128)(2,1)S(1)}, u32[]{:S(2)}, u32[]{:S(2)}) collective-permute-start(bf16[8,32,384]{2,1,0:T(8,128)(2,1)S(1)} %get-tuple-element.69), channel_id=1, source_target_pairs={{0,8},{1,9},{2,10},{3,11},{4,12},{5,13},{6,14},{7,15},{8,0},{9,1},... | collective-permute-start | bytes 589832 | tf_op jit(solution)/shard_map/ppermute | solution.py:241
  31.4 25.7 %collective-permute-start.2 = (bf16[8,32,384]{2,1,0:T(8,128)(2,1)S(1)}, bf16[8,32,384]{2,1,0:T(8,128)(2,1)S(1)}, u32[]{:S(2)}, u32[]{:S(2)}) collective-permute-start(bf16[8,32,384]{2,1,0:T(8,128)(2,1)S(1)} %get-tuple-element.70), channel_id=1, source_target_pairs={{0,12},{1,13},{2,14},{3,15},{4,8},{5,9},{6,10},{7,11},{8,4},{9,5},... | collective-permute-start | bytes 589832 | tf_op jit(solution)/shard_map/ppermute | solution.py:241
  33.7 25.3 %collective-permute-start.3 = (bf16[8,32,384]{2,1,0:T(8,128)(2,1)S(1)}, bf16[8,32,384]{2,1,0:T(8,128)(2,1)S(1)}, u32[]{:S(2)}, u32[]{:S(2)}) collective-permute-start(bf16[8,32,384]{2,1,0:T(8,128)(2,1)S(1)} %get-tuple-element.71), channel_id=1, source_target_pairs={{0,16},{1,17},{2,18},{3,19},{4,20},{5,21},{6,22},{7,23},{8,24},{9,... | collective-permute-start | bytes 589832 | tf_op jit(solution)/shard_map/ppermute | solution.py:241
  34.3 29.2 %collective-permute-start.4 = (bf16[8,32,384]{2,1,0:T(8,128)(2,1)S(1)}, bf16[8,32,384]{2,1,0:T(8,128)(2,1)S(1)}, u32[]{:S(2)}, u32[]{:S(2)}) collective-permute-start(bf16[8,32,384]{2,1,0:T(8,128)(2,1)S(1)} %get-tuple-element.72), channel_id=1, source_target_pairs={{0,20},{1,21},{2,22},{3,23},{4,16},{5,17},{6,18},{7,19},{8,28},{9,... | collective-permute-start | bytes 589832 | tf_op jit(solution)/shard_map/ppermute | solution.py:241
  36.9 26.6 %collective-permute-start.5 = (bf16[8,32,384]{2,1,0:T(8,128)(2,1)S(1)}, bf16[8,32,384]{2,1,0:T(8,128)(2,1)S(1)}, u32[]{:S(2)}, u32[]{:S(2)}) collective-permute-start(bf16[8,32,384]{2,1,0:T(8,128)(2,1)S(1)} %get-tuple-element.73), channel_id=1, source_target_pairs={{0,24},{1,25},{2,26},{3,27},{4,28},{5,29},{6,30},{7,31},{8,16},{9,... | collective-permute-start | bytes 589832 | tf_op jit(solution)/shard_map/ppermute | solution.py:241
  43.8 24.9 %collective-permute-start.6 = (bf16[8,32,384]{2,1,0:T(8,128)(2,1)S(1)}, bf16[8,32,384]{2,1,0:T(8,128)(2,1)S(1)}, u32[]{:S(2)}, u32[]{:S(2)}) collective-permute-start(bf16[8,32,384]{2,1,0:T(8,128)(2,1)S(1)} %get-tuple-element.74), channel_id=1, source_target_pairs={{0,28},{1,29},{2,30},{3,31},{4,24},{5,25},{6,26},{7,27},{8,20},{9,... | collective-permute-start | bytes 589832 | tf_op jit(solution)/shard_map/ppermute | solution.py:241
  57.0 25.6 %collective-permute-start.10 = (bf16[8,32,384]{2,1,0:T(8,128)(2,1)S(1)}, bf16[8,32,384]{2,1,0:T(8,128)(2,1)S(1)}, u32[]{:S(2)}, u32[]{:S(2)}) collective-permute-start(bf16[8,32,384]{2,1,0:T(8,128)(2,1)S(1)} %get-tuple-element.80), channel_id=1, source_target_pairs={{0,4},{1,5},{2,6},{3,7},{4,0},{5,1},{6,2},{7,3},{8,12},{9,13},{10,... | collective-permute-start | bytes 589832 | tf_op jit(solution)/shard_map/ppermute | solution.py:241
  59.0 31.1 %collective-permute-start.11 = (bf16[8,32,384]{2,1,0:T(8,128)(2,1)S(1)}, bf16[8,32,384]{2,1,0:T(8,128)(2,1)S(1)}, u32[]{:S(2)}, u32[]{:S(2)}) collective-permute-start(bf16[8,32,384]{2,1,0:T(8,128)(2,1)S(1)} %get-tuple-element.81), channel_id=1, source_target_pairs={{0,8},{1,9},{2,10},{3,11},{4,12},{5,13},{6,14},{7,15},{8,0},{9,1},... | collective-permute-start | bytes 589832 | tf_op jit(solution)/shard_map/ppermute | solution.py:241
  63.5 26.9 %collective-permute-start.12 = (bf16[8,32,384]{2,1,0:T(8,128)(2,1)S(1)}, bf16[8,32,384]{2,1,0:T(8,128)(2,1)S(1)}, u32[]{:S(2)}, u32[]{:S(2)}) collective-permute-start(bf16[8,32,384]{2,1,0:T(8,128)(2,1)S(1)} %get-tuple-element.82), channel_id=1, source_target_pairs={{0,12},{1,13},{2,14},{3,15},{4,8},{5,9},{6,10},{7,11},{8,4},{9,5},... | collective-permute-start | bytes 589832 | tf_op jit(solution)/shard_map/ppermute | solution.py:241
  63.5 28.1 %collective-permute-start.13 = (bf16[8,32,384]{2,1,0:T(8,128)(2,1)S(1)}, bf16[8,32,384]{2,1,0:T(8,128)(2,1)S(1)}, u32[]{:S(2)}, u32[]{:S(2)}) collective-permute-start(bf16[8,32,384]{2,1,0:T(8,128)(2,1)S(1)} %get-tuple-element.83), channel_id=1, source_target_pairs={{0,16},{1,17},{2,18},{3,19},{4,20},{5,21},{6,22},{7,23},{8,24},{9,... | collective-permute-start | bytes 589832 | tf_op jit(solution)/shard_map/ppermute | solution.py:241
  68.8 26.5 %collective-permute-start.14 = (bf16[8,32,384]{2,1,0:T(8,128)(2,1)S(1)}, bf16[8,32,384]{2,1,0:T(8,128)(2,1)S(1)}, u32[]{:S(2)}, u32[]{:S(2)}) collective-permute-start(bf16[8,32,384]{2,1,0:T(8,128)(2,1)S(1)} %get-tuple-element.84), channel_id=1, source_target_pairs={{0,20},{1,21},{2,22},{3,23},{4,16},{5,17},{6,18},{7,19},{8,28},{9,... | collective-permute-start | bytes 589832 | tf_op jit(solution)/shard_map/ppermute | solution.py:241
  82.6 17.5 %collective-permute-start.15 = (bf16[8,32,384]{2,1,0:T(8,128)(2,1)S(1)}, bf16[8,32,384]{2,1,0:T(8,128)(2,1)S(1)}, u32[]{:S(2)}, u32[]{:S(2)}) collective-permute-start(bf16[8,32,384]{2,1,0:T(8,128)(2,1)S(1)} %get-tuple-element.85), channel_id=1, source_target_pairs={{0,24},{1,25},{2,26},{3,27},{4,28},{5,29},{6,30},{7,31},{8,16},{9,... | collective-permute-start | bytes 589832 | tf_op jit(solution)/shard_map/ppermute | solution.py:241
  90.1 11.8 %collective-permute-start.16 = (bf16[8,32,384]{2,1,0:T(8,128)(2,1)S(1)}, bf16[8,32,384]{2,1,0:T(8,128)(2,1)S(1)}, u32[]{:S(2)}, u32[]{:S(2)}) collective-permute-start(bf16[8,32,384]{2,1,0:T(8,128)(2,1)S(1)} %get-tuple-element.86), channel_id=1, source_target_pairs={{0,28},{1,29},{2,30},{3,31},{4,24},{5,25},{6,26},{7,27},{8,20},{9,... | collective-permute-start | bytes 589832 | tf_op jit(solution)/shard_map/ppermute | solution.py:241
  90.4 22.9 %collective-permute-start.20 = (bf16[8,32,128]{2,1,0:T(8,128)(2,1)}, bf16[8,32,128]{2,1,0:T(8,128)(2,1)S(1)}, u32[]{:S(2)}, u32[]{:S(2)}) collective-permute-start(bf16[8,32,128]{2,1,0:T(8,128)(2,1)} %get-tuple-element.92), channel_id=1, source_target_pairs={{0,4},{1,5},{2,6},{3,7},{4,0},{5,1},{6,2},{7,3},{8,12},{9,13},{10,... | collective-permute-start | bytes 196616 | tf_op jit(solution)/shard_map/ppermute | solution.py:241
  91.6 25.6 %collective-permute-start.21 = (bf16[8,32,128]{2,1,0:T(8,128)(2,1)}, bf16[8,32,128]{2,1,0:T(8,128)(2,1)S(1)}, u32[]{:S(2)}, u32[]{:S(2)}) collective-permute-start(bf16[8,32,128]{2,1,0:T(8,128)(2,1)} %get-tuple-element.93), channel_id=1, source_target_pairs={{0,8},{1,9},{2,10},{3,11},{4,12},{5,13},{6,14},{7,15},{8,0},{9,1},... | collective-permute-start | bytes 196616 | tf_op jit(solution)/shard_map/ppermute | solution.py:241
  95.3 22.4 %collective-permute-start.22 = (bf16[8,32,128]{2,1,0:T(8,128)(2,1)}, bf16[8,32,128]{2,1,0:T(8,128)(2,1)S(1)}, u32[]{:S(2)}, u32[]{:S(2)}) collective-permute-start(bf16[8,32,128]{2,1,0:T(8,128)(2,1)} %get-tuple-element.94), channel_id=1, source_target_pairs={{0,12},{1,13},{2,14},{3,15},{4,8},{5,9},{6,10},{7,11},{8,4},{9,5},... | collective-permute-start | bytes 196616 | tf_op jit(solution)/shard_map/ppermute | solution.py:241
  100.1 18.9 %collective-permute-start.23 = (bf16[8,32,128]{2,1,0:T(8,128)(2,1)}, bf16[8,32,128]{2,1,0:T(8,128)(2,1)S(1)}, u32[]{:S(2)}, u32[]{:S(2)}) collective-permute-start(bf16[8,32,128]{2,1,0:T(8,128)(2,1)} %get-tuple-element.95), channel_id=1, source_target_pairs={{0,16},{1,17},{2,18},{3,19},{4,20},{5,21},{6,22},{7,23},{8,24},{9,... | collective-permute-start | bytes 196616 | tf_op jit(solution)/shard_map/ppermute | solution.py:241
  101.9 17.7 %collective-permute-start.24 = (bf16[8,32,128]{2,1,0:T(8,128)(2,1)}, bf16[8,32,128]{2,1,0:T(8,128)(2,1)S(1)}, u32[]{:S(2)}, u32[]{:S(2)}) collective-permute-start(bf16[8,32,128]{2,1,0:T(8,128)(2,1)} %get-tuple-element.96), channel_id=1, source_target_pairs={{0,20},{1,21},{2,22},{3,23},{4,16},{5,17},{6,18},{7,19},{8,28},{9,... | collective-permute-start | bytes 196616 | tf_op jit(solution)/shard_map/ppermute | solution.py:241
  113.3 7.6 %collective-permute-start.25 = (bf16[8,32,128]{2,1,0:T(8,128)(2,1)S(1)}, bf16[8,32,128]{2,1,0:T(8,128)(2,1)S(1)}, u32[]{:S(2)}, u32[]{:S(2)}) collective-permute-start(bf16[8,32,128]{2,1,0:T(8,128)(2,1)S(1)} %copy-done.18), channel_id=1, source_target_pairs={{0,24},{1,25},{2,26},{3,27},{4,28},{5,29},{6,30},{7,31},{8,16},{9,... | collective-permute-start | bytes 196616 | tf_op jit(solution)/shard_map/ppermute | solution.py:241
  117.2 7.0 %collective-permute-start.26 = (bf16[8,32,128]{2,1,0:T(8,128)(2,1)S(1)}, bf16[8,32,128]{2,1,0:T(8,128)(2,1)S(1)}, u32[]{:S(2)}, u32[]{:S(2)}) collective-permute-start(bf16[8,32,128]{2,1,0:T(8,128)(2,1)S(1)} %copy-done.16), channel_id=1, source_target_pairs={{0,28},{1,29},{2,30},{3,31},{4,24},{5,25},{6,26},{7,27},{8,20},{9,... | collective-permute-start | bytes 196616 | tf_op jit(solution)/shard_map/ppermute | solution.py:241
  117.7 7.1 %collective-permute-start.7 = (bf16[8,32,384]{2,1,0:T(8,128)(2,1)S(1)}, bf16[8,32,384]{2,1,0:T(8,128)(2,1)S(1)}, u32[]{:S(2)}, u32[]{:S(2)}) collective-permute-start(bf16[8,32,384]{2,1,0:T(8,128)(2,1)S(1)} %get-tuple-element.76), channel_id=1, source_target_pairs={{0,1},{1,0},{2,3},{3,2},{4,5},{5,4},{6,7},{7,6},{8,9},{9,8},{10,11... | collective-permute-start | bytes 589832 | tf_op jit(solution)/shard_map/ppermute | solution.py:241
  119.0 12.1 %collective-permute-start.8 = (bf16[8,32,384]{2,1,0:T(8,128)(2,1)S(1)}, bf16[8,32,384]{2,1,0:T(8,128)(2,1)S(1)}, u32[]{:S(2)}, u32[]{:S(2)}) collective-permute-start(bf16[8,32,384]{2,1,0:T(8,128)(2,1)S(1)} %get-tuple-element.77), channel_id=1, source_target_pairs={{0,2},{1,3},{2,0},{3,1},{4,6},{5,7},{6,4},{7,5},{8,10},{9,11},{10,... | collective-permute-start | bytes 589832 | tf_op jit(solution)/shard_map/ppermute | solution.py:241
  119.6 13.0 %collective-permute-start.9 = (bf16[8,32,384]{2,1,0:T(8,128)(2,1)S(1)}, bf16[8,32,384]{2,1,0:T(8,128)(2,1)S(1)}, u32[]{:S(2)}, u32[]{:S(2)}) collective-permute-start(bf16[8,32,384]{2,1,0:T(8,128)(2,1)S(1)} %get-tuple-element.78), channel_id=1, source_target_pairs={{0,3},{1,2},{2,1},{3,0},{4,7},{5,6},{6,5},{7,4},{8,11},{9,10},{10,... | collective-permute-start | bytes 589832 | tf_op jit(solution)/shard_map/ppermute | solution.py:241
  120.9 12.2 %collective-permute-start.17 = (bf16[8,32,384]{2,1,0:T(8,128)(2,1)S(1)}, bf16[8,32,384]{2,1,0:T(8,128)(2,1)S(1)}, u32[]{:S(2)}, u32[]{:S(2)}) collective-permute-start(bf16[8,32,384]{2,1,0:T(8,128)(2,1)S(1)} %get-tuple-element.88), channel_id=1, source_target_pairs={{0,1},{1,0},{2,3},{3,2},{4,5},{5,4},{6,7},{7,6},{8,9},{9,8},{10,11... | collective-permute-start | bytes 589832 | tf_op jit(solution)/shard_map/ppermute | solution.py:241
  124.2 11.0 %collective-permute-start.18 = (bf16[8,32,384]{2,1,0:T(8,128)(2,1)S(1)}, bf16[8,32,384]{2,1,0:T(8,128)(2,1)S(1)}, u32[]{:S(2)}, u32[]{:S(2)}) collective-permute-start(bf16[8,32,384]{2,1,0:T(8,128)(2,1)S(1)} %get-tuple-element.89), channel_id=1, source_target_pairs={{0,2},{1,3},{2,0},{3,1},{4,6},{5,7},{6,4},{7,5},{8,10},{9,11},{10,... | collective-permute-start | bytes 589832 | tf_op jit(solution)/shard_map/ppermute | solution.py:241
  124.7 13.9 %collective-permute-start.19 = (bf16[8,32,384]{2,1,0:T(8,128)(2,1)S(1)}, bf16[8,32,384]{2,1,0:T(8,128)(2,1)S(1)}, u32[]{:S(2)}, u32[]{:S(2)}) collective-permute-start(bf16[8,32,384]{2,1,0:T(8,128)(2,1)S(1)} %get-tuple-element.90), channel_id=1, source_target_pairs={{0,3},{1,2},{2,1},{3,0},{4,7},{5,6},{6,5},{7,4},{8,11},{9,10},{10,... | collective-permute-start | bytes 589832 | tf_op jit(solution)/shard_map/ppermute | solution.py:241
  131.0 7.6 %collective-permute-start.27 = (bf16[8,32,128]{2,1,0:T(8,128)(2,1)S(1)}, bf16[8,32,128]{2,1,0:T(8,128)(2,1)S(1)}, u32[]{:S(2)}, u32[]{:S(2)}) collective-permute-start(bf16[8,32,128]{2,1,0:T(8,128)(2,1)S(1)} %get-tuple-element.100), channel_id=1, source_target_pairs={{0,1},{1,0},{2,3},{3,2},{4,5},{5,4},{6,7},{7,6},{8,9},{9,8},{10,11... | collective-permute-start | bytes 196616 | tf_op jit(solution)/shard_map/ppermute | solution.py:241
  132.5 8.2 %collective-permute-start.28 = (bf16[8,32,128]{2,1,0:T(8,128)(2,1)S(1)}, bf16[8,32,128]{2,1,0:T(8,128)(2,1)S(1)}, u32[]{:S(2)}, u32[]{:S(2)}) collective-permute-start(bf16[8,32,128]{2,1,0:T(8,128)(2,1)S(1)} %get-tuple-element.101), channel_id=1, source_target_pairs={{0,2},{1,3},{2,0},{3,1},{4,6},{5,7},{6,4},{7,5},{8,10},{9,11},{10,... | collective-permute-start | bytes 196616 | tf_op jit(solution)/shard_map/ppermute | solution.py:241
  133.1 8.3 %collective-permute-start.29 = (bf16[8,32,128]{2,1,0:T(8,128)(2,1)S(1)}, bf16[8,32,128]{2,1,0:T(8,128)(2,1)S(1)}, u32[]{:S(2)}, u32[]{:S(2)}) collective-permute-start(bf16[8,32,128]{2,1,0:T(8,128)(2,1)S(1)} %get-tuple-element.102), channel_id=1, source_target_pairs={{0,3},{1,2},{2,1},{3,0},{4,7},{5,6},{6,5},{7,4},{8,11},{9,10},{10,... | collective-permute-start | bytes 196616 | tf_op jit(solution)/shard_map/ppermute | solution.py:241
  164.9 9.3 %collective-permute-start.30 = (bf16[16,48,1024]{2,1,0:T(8,128)(2,1)}, bf16[16,48,1024]{2,1,0:T(8,128)(2,1)S(1)}, u32[]{:S(2)}, u32[]{:S(2)}) collective-permute-start(bf16[16,48,1024]{2,1,0:T(8,128)(2,1)} %get-tuple-element.105), channel_id=1, source_target_pairs={{0,1},{1,0},{2,3},{3,2},{4,5},{5,4},{6,7},{7,6},{8,9},{9,8},{10,11... | collective-permute-start | bytes 4718600 | tf_op jit(solution)/shard_map/ppermute | solution.py:241
  165.2 10.0 %collective-permute-start.33 = (bf16[16,48,1024]{2,1,0:T(8,128)(2,1)}, bf16[16,48,1024]{2,1,0:T(8,128)(2,1)S(1)}, u32[]{:S(2)}, u32[]{:S(2)}) collective-permute-start(bf16[16,48,1024]{2,1,0:T(8,128)(2,1)} %get-tuple-element.112), channel_id=1, source_target_pairs={{0,1},{1,0},{2,3},{3,2},{4,5},{5,4},{6,7},{7,6},{8,9},{9,8},{10,11... | collective-permute-start | bytes 4718600 | tf_op jit(solution)/shard_map/ppermute | solution.py:241
  165.5 6.9 %collective-permute-start.31 = (bf16[16,32,1024]{2,1,0:T(8,128)(2,1)}, bf16[16,32,1024]{2,1,0:T(8,128)(2,1)S(1)}, u32[]{:S(2)}, u32[]{:S(2)}) collective-permute-start(bf16[16,32,1024]{2,1,0:T(8,128)(2,1)} %get-tuple-element.107), channel_id=1, source_target_pairs={{0,1},{1,0},{2,3},{3,2},{4,5},{5,4},{6,7},{7,6},{8,9},{9,8},{10,11... | collective-permute-start | bytes 3145736 | tf_op jit(solution)/shard_map/ppermute | solution.py:241
  174.5 19.7 %collective-permute-start.32 = (bf16[8,48,1024]{2,1,0:T(8,128)(2,1)S(1)}, bf16[8,48,1024]{2,1,0:T(8,128)(2,1)S(1)}, u32[]{:S(2)}, u32[]{:S(2)}) collective-permute-start(bf16[8,48,1024]{2,1,0:T(8,128)(2,1)S(1)} %get-tuple-element.110.refs_2_), channel_id=1, source_target_pairs={{0,2},{1,3},{2,0},{3,1},{4,6},{5,7},{6,4},{7,5},{8,10},{9,11},{10,... | collective-permute-start | bytes 2359304 | tf_op jit(solution)/shard_map/ppermute | solution.py:241
  176.4 19.7 %collective-permute-start.35 = (bf16[8,48,1024]{2,1,0:T(8,128)(2,1)S(1)}, bf16[8,48,1024]{2,1,0:T(8,128)(2,1)S(1)}, u32[]{:S(2)}, u32[]{:S(2)}) collective-permute-start(bf16[8,48,1024]{2,1,0:T(8,128)(2,1)S(1)} %get-tuple-element.113.refs_2_), channel_id=1, source_target_pairs={{0,4},{1,5},{2,6},{3,7},{4,0},{5,1},{6,2},{7,3},{8,12},{9,13},{10,... | collective-permute-start | bytes 2359304 | tf_op jit(solution)/shard_map/ppermute | solution.py:241
  177.6 22.7 %collective-permute-start.37 = (bf16[4,32,1024]{2,1,0:T(8,128)(2,1)S(1)}, bf16[4,32,1024]{2,1,0:T(8,128)(2,1)S(1)}, u32[]{:S(2)}, u32[]{:S(2)}) collective-permute-start(bf16[4,32,1024]{2,1,0:T(8,128)(2,1)S(1)} %get-tuple-element.108.refs_2_), channel_id=1, source_target_pairs={{0,8},{1,9},{2,10},{3,11},{4,12},{5,13},{6,14},{7,15},{8,0},{9,1},... | collective-permute-start | bytes 786440 | tf_op jit(solution)/shard_map/ppermute | solution.py:241
  177.6 22.7 %collective-permute-start.38 = (bf16[4,32,1024]{2,1,0:T(8,128)(2,1)S(1)}, bf16[4,32,1024]{2,1,0:T(8,128)(2,1)S(1)}, u32[]{:S(2)}, u32[]{:S(2)}) collective-permute-start(bf16[4,32,1024]{2,1,0:T(8,128)(2,1)S(1)} %get-tuple-element.120), channel_id=1, source_target_pairs={{0,16},{1,17},{2,18},{3,19},{4,20},{5,21},{6,22},{7,23},{8,24},{9,... | collective-permute-start | bytes 786440 | tf_op jit(solution)/shard_map/ppermute | solution.py:241
  181.9 18.4 %collective-permute-start.39 = (bf16[4,32,1024]{2,1,0:T(8,128)(2,1)S(1)}, bf16[4,32,1024]{2,1,0:T(8,128)(2,1)S(1)}, u32[]{:S(2)}, u32[]{:S(2)}) collective-permute-start(bf16[4,32,1024]{2,1,0:T(8,128)(2,1)S(1)} %get-tuple-element.121), channel_id=1, source_target_pairs={{0,24},{1,25},{2,26},{3,27},{4,28},{5,29},{6,30},{7,31},{8,16},{9,... | collective-permute-start | bytes 786440 | tf_op jit(solution)/shard_map/ppermute | solution.py:241
  194.4 10.5 %collective-permute-start.34 = (bf16[4,48,1024]{2,1,0:T(8,128)(2,1)S(1)}, bf16[4,48,1024]{2,1,0:T(8,128)(2,1)S(1)}, u32[]{:S(2)}, u32[]{:S(2)}) collective-permute-start(bf16[4,48,1024]{2,1,0:T(8,128)(2,1)S(1)} %get-tuple-element.115.refs_2_), channel_id=1, source_target_pairs={{0,4},{1,5},{2,6},{3,7},{4,0},{5,1},{6,2},{7,3},{8,12},{9,13},{10,... | collective-permute-start | bytes 1179656 | tf_op jit(solution)/shard_map/ppermute | solution.py:241
  196.3 11.9 %collective-permute-start.36 = (bf16[4,48,1024]{2,1,0:T(8,128)(2,1)S(1)}, bf16[4,48,1024]{2,1,0:T(8,128)(2,1)S(1)}, u32[]{:S(2)}, u32[]{:S(2)}) collective-permute-start(bf16[4,48,1024]{2,1,0:T(8,128)(2,1)S(1)} %get-tuple-element.118.refs_4_), channel_id=1, source_target_pairs={{0,2},{1,3},{2,0},{3,1},{4,6},{5,7},{6,4},{7,5},{8,10},{9,11},{10,... | collective-permute-start | bytes 1179656 | tf_op jit(solution)/shard_map/ppermute | solution.py:241
  200.4 9.2 %collective-permute-start.43 = (bf16[2,32,1024]{2,1,0:T(8,128)(2,1)S(1)}, bf16[2,32,1024]{2,1,0:T(8,128)(2,1)S(1)}, u32[]{:S(2)}, u32[]{:S(2)}) collective-permute-start(bf16[2,32,1024]{2,1,0:T(8,128)(2,1)S(1)} %get-tuple-element.122.refs_4_), channel_id=1, source_target_pairs={{0,2},{1,3},{2,0},{3,1},{4,6},{5,7},{6,4},{7,5},{8,10},{9,11},{10,... | collective-permute-start | bytes 393224 | tf_op jit(solution)/shard_map/ppermute | solution.py:241
  209.6 5.6 %collective-permute-start.44 = (bf16[1,32,1024]{2,1,0:T(8,128)(2,1)S(1)}, bf16[1,32,1024]{2,1,0:T(8,128)(2,1)S(1)}, u32[]{:S(2)}, u32[]{:S(2)}) collective-permute-start(bf16[1,32,1024]{2,1,0:T(8,128)(2,1)S(1)} %get-tuple-element.129), channel_id=1, source_target_pairs={{0,4},{1,5},{2,6},{3,7},{4,0},{5,1},{6,2},{7,3},{8,12},{9,13},{10,... | collective-permute-start | bytes 196616 | tf_op jit(solution)/shard_map/ppermute | solution.py:241
  210.8 17.8 %collective-permute-start.40 = (bf16[1,96,1024]{2,1,0:T(8,128)(2,1)S(1)}, bf16[1,96,1024]{2,1,0:T(8,128)(2,1)S(1)}, u32[]{:S(2)}, u32[]{:S(2)}) collective-permute-start(bf16[1,96,1024]{2,1,0:T(8,128)(2,1)S(1)} %get-tuple-element.124.refs_2_), channel_id=1, source_target_pairs={{0,8},{1,9},{2,10},{3,11},{4,12},{5,13},{6,14},{7,15},{8,0},{9,1},... | collective-permute-start | bytes 589832 | tf_op jit(solution)/shard_map/ppermute | solution.py:241
  211.2 17.3 %collective-permute-start.41 = (bf16[1,96,1024]{2,1,0:T(8,128)(2,1)S(1)}, bf16[1,96,1024]{2,1,0:T(8,128)(2,1)S(1)}, u32[]{:S(2)}, u32[]{:S(2)}) collective-permute-start(bf16[1,96,1024]{2,1,0:T(8,128)(2,1)S(1)} %get-tuple-element.125), channel_id=1, source_target_pairs={{0,16},{1,17},{2,18},{3,19},{4,20},{5,21},{6,22},{7,23},{8,24},{9,... | collective-permute-start | bytes 589832 | tf_op jit(solution)/shard_map/ppermute | solution.py:241
  215.1 13.5 %collective-permute-start.42 = (bf16[1,96,1024]{2,1,0:T(8,128)(2,1)S(1)}, bf16[1,96,1024]{2,1,0:T(8,128)(2,1)S(1)}, u32[]{:S(2)}, u32[]{:S(2)}) collective-permute-start(bf16[1,96,1024]{2,1,0:T(8,128)(2,1)S(1)} %get-tuple-element.126), channel_id=1, source_target_pairs={{0,24},{1,25},{2,26},{3,27},{4,28},{5,29},{6,30},{7,31},{8,16},{9,... | collective-permute-start | bytes 589832 | tf_op jit(solution)/shard_map/ppermute | solution.py:241
  (30 other events, 171.3 us)
Sparse Core Ops, SparseCore 0:
  30.3 51.6 all-gather.2

commit v3 on v2

--- a/solution.py
+++ b/solution.py
@@ -11,9 +11,9 @@
 AXES = ("dp", "shard")
 LANES = 128
 ANY = pl.BlockSpec(memory_space=pl.ANY)
+HBM = pl.BlockSpec(memory_space=pltpu.HBM)
 SMEM = pl.BlockSpec(memory_space=pltpu.SMEM)
 VMEM = pl.BlockSpec(memory_space=pltpu.VMEM)
-VMEM_LIMIT = 56 * 1024 * 1024
 F32 = jnp.float32
 BF16 = jnp.bfloat16
 
@@ -27,9 +27,15 @@
     return [(a, b - a) for a, b in zip(ends, ends[1:]) if b > a]
 
 
-def serve_kernel(owners, slots, owned, start, after, ids, place, cache, *rest):
-    rest = rest[after:]
-    outs, (table, sem) = rest[:owners], rest[owners:]
+def serve_kernel(owners, slots, owned, start, lay, after, ids, place, cache, *rest):
+    parts, (*outs, table, sem) = rest[:lay], rest[lay + after :]
+    if lay:
+        *outs, joined = outs
+        at = 0
+        for part in parts:
+            size = part.shape[0]
+            pltpu.make_async_copy(part, joined.at[pl.ds(at, size)], sem).start()
+            at += size
     me = place[0]
     shards, each = ids.shape[0] // owners, ids.shape[1]
     width = outs[0].shape[2]
@@ -48,17 +54,18 @@
         at = lax.fori_loop(0, shards, scan, base)
         for j in range(slots):
             row = jnp.where(base + j < at, table[base + j], 0)
+            into = outs[0].at[asking * slots + j] if len(outs) == 1 else outs[k].at[j]
             pltpu.make_async_copy(
-                cache.at[row, :, pl.ds(start, width)], outs[k].at[j], sem
+                cache.at[row, :, pl.ds(start, width)], into, sem
             ).start()
-    for out in outs:
+    for out in outs + [joined] if lay else outs:
         pltpu.make_async_copy(out, out, sem).wait()
 
 
-def pick_kernel(owners, shards, owned, after, ids, place, *rest):
-    arrived, rest = rest[:owners], rest[after:]
-    outs = rest[owners : owners + shards]
-    count, sem = rest[owners + shards :]
+def pick_kernel(owners, slots, shards, owned, lanes, after, ids, place, *rest):
+    arrived, rest = rest[:lanes], rest[lanes + after :]
+    outs = rest[:shards]
+    count, sem = rest[shards:]
     me, shard = place[0], place[1]
     each = ids.shape[1]
     for k in range(owners):
@@ -76,11 +83,16 @@
     for k in range(shards):
         peer = jnp.bitwise_xor(shard, k)
         for j in range(each):
-            source = jnp.bitwise_xor(ids[me * shards + peer, j] // owned, me)
+            owner = ids[me * shards + peer, j] // owned
             at = count[owners + peer * each + j]
+            if lanes == 1:
+                pltpu.make_async_copy(
+                    arrived[0].at[owner * slots + at], outs[k].at[j], sem
+                ).start()
+                continue
             for n in range(owners):
 
-                @pl.when(source == n)
+                @pl.when(jnp.bitwise_xor(owner, me) == n)
                 def _(n=n, k=k, j=j, at=at):
                     pltpu.make_async_copy(
                         arrived[n].at[at], outs[k].at[j], sem
@@ -90,26 +102,21 @@
         pltpu.make_async_copy(out, out, sem).wait()
 
 
-def concat_kernel(after, *refs):
-    out, at = refs[-1], 0
-    for ref in refs[: len(refs) - 1 - after]:
-        out[at : at + ref.shape[0], :] = ref[...]
-        at += ref.shape[0]
-
-
-def place_blocks(total, rows, place, turn, first, targets):
+def place_blocks(total, rows, place, turn, pairs, targets):
     me = place[2]
     odd = jnp.bitwise_and(me, 1) == 1
     half = me >> 1
-    for d in range(first):
+    for d in pairs:
         rel = jnp.bitwise_xor(half, d)
         for order, keep, send, source, into, size in targets:
-            even_at = 2 * d * rows + source
+            even_at = 2 * (d - pairs[0]) * rows + source
             odd_at = even_at + rows
             even_rows = total[even_at : even_at + size, :]
             odd_rows = total[odd_at : odd_at + size, :]
             at = turn(rel, order)
-            keep[at, into : into + size, :] = jnp.where(odd, odd_rows, even_rows)
+            keep[at, into : into + size, :] = jnp.where(odd, odd_rows, even_rows).astype(
+                BF16
+            )
             send[at, into : into + size, :] = jnp.where(odd, even_rows, odd_rows).astype(
                 BF16
             )
@@ -127,7 +134,7 @@
             rows = parts[0].shape[1]
 
             def one(i, carry, k=k, at=at, rows=rows, parts=parts):
-                total = parts[0][k * each + i]
+                total = parts[0][k * each + i].astype(F32)
                 for part in parts[1:]:
                     total = total + part[k * each + i].astype(F32)
                 outs[k][i, at : at + rows, :] = total.astype(outs[k].dtype)
@@ -135,6 +142,21 @@
 
             lax.fori_loop(0, each, one, 0)
             at += rows
+
+
+def finish_kernel(first, rows_k, *refs):
+    ends, (grad_query, grad_key, grad_value) = refs[:-3], refs[-3:]
+
+    def total(parts, at, size):
+        result = parts[0][0, at : at + size, :]
+        for part in parts[1:]:
+            result = result + part[0, at : at + size, :].astype(F32)
+        return result
+
+    exact = grad_key.shape[0]
+    grad_value[...] = total(ends[:first], 0, rows_k)[:exact]
+    grad_key[...] = total(ends[first:], 0, rows_k)[:exact]
+    grad_query[...] = total(ends[first:], rows_k, grad_query.shape[0])
 
 
 def combine(groups, split, after=()):
@@ -159,10 +181,12 @@
 
 def attend_kernel(parts, shards, heads, scale, devices, spans, turn, *refs):
     pieces, refs = refs[: parts * shards], refs[parts * shards :]
-    place, queries, cotangent, normed_t, w_key, w_value = refs[:6]
-    context, keep_v, send_v, keep_p, send_p, keep_r, send_r = refs[6:13]
-    key_rows, value_rows, scores, prob_grads, prob_rounds, score_grads = refs[13:19]
-    latents_t, query_grad, key_grad, value_grad, total_v, total_k, total_q = refs[19:]
+    place, queries, cotangent, normed_hbm, weights, context = refs[:6]
+    results, refs = refs[6:12], refs[12:]
+    key_rows, value_rows, scores, prob_grads, prob_rounds, score_grads = refs[:6]
+    latents_t, query_grad, key_grad, value_grad, total_v, total_k, total_q = refs[6:13]
+    keep_v, send_v, keep_p, send_p, keep_r, send_r = staged = refs[13:19]
+    w_key, w_value, normed_t, weight_sem, normed_sem, out_sem = refs[19:]
     nbr, tokens, _ = pieces[0].shape
     step = pl.program_id(0)
     rows = jnp.concatenate(
@@ -181,6 +205,24 @@
     keys, latent = rows.shape
     span, inner = queries.shape
     latents_t[step] = rows.T
+    each = w_key.shape[0] // shards
+    skipped = weights.shape[1] - 2 * each
+
+    @pl.when(step == 0)
+    def _():
+        pltpu.make_async_copy(normed_hbm, normed_t, normed_sem).start()
+        for which, held_weights in enumerate((w_key, w_value)):
+            for k in range(shards):
+                pltpu.make_async_copy(
+                    weights.at[k, pl.ds(skipped + which * each, each)],
+                    held_weights.at[pl.ds(k * each, each)],
+                    weight_sem.at[which],
+                ).start()
+        for which, held_weights in enumerate((w_key, w_value)):
+            pltpu.make_async_copy(
+                held_weights, held_weights, weight_sem.at[which]
+            ).wait()
+
     key_rows[...] = jnp.dot(rows, w_key[...], preferred_element_type=F32).astype(BF16)
     value_rows[...] = jnp.dot(rows, w_value[...], preferred_element_type=F32).astype(
         BF16
@@ -222,19 +264,46 @@
     def _():
         across = jnp.concatenate([latents_t[c] for c in range(spans)], axis=1)
         of_v, of_p, of_r = (0, keep_v, send_v), (1, keep_p, send_p), (2, keep_r, send_r)
-        rows_k, rows_q = keep_v.shape[1], total_q.shape[0] // devices
+        rows_k, rows_q = keep_v.shape[1], normed_t.shape[0] // devices
         shared = keep_p.shape[1] - rows_k
+
+        def write(first):
+            for n in (first, first + 1):
+                pltpu.make_async_copy(staged[n], results[n], out_sem.at[n]).start()
+
         for total, grad, target in ((total_v, value_grad, of_v), (total_k, key_grad, of_p)):
             total[:latent, :] = dot(across, grad[...], nn)
             total[latent:, :] = jnp.zeros((total.shape[0] - latent, inner), F32)
             place_blocks(
-                total, latent // devices, place, turn, devices // 2, [target + (0, 0, rows_k)]
+                total, latent // devices, place, turn, range(devices // 2), [target + (0, 0, rows_k)]
             )
-        total_q[...] = dot(normed_t[...], query_grad[...], nn)
+            if target is of_v or not shared:
+                write(2 * target[0])
         targets = [of_r + (shared, 0, rows_q - shared)]
         if shared:
             targets.append(of_p + (0, rows_k, shared))
-        place_blocks(total_q, rows_q, place, turn, devices // 2, targets)
+        tile = total_q.shape[1]
+        pltpu.make_async_copy(normed_hbm, normed_t, normed_sem).wait()
+        for at in range(0, normed_t.shape[0], tile):
+            part = total_q.at[at // tile % 2]
+            part[...] = dot(normed_t[at : at + tile, :], query_grad[...], nn)
+            pairs = range(at // rows_q // 2, (at + tile) // rows_q // 2)
+            place_blocks(part, rows_q, place, turn, pairs, targets)
+        if shared:
+            write(2)
+        write(4)
+        for n in range(6):
+            pltpu.make_async_copy(staged[n], results[n], out_sem.at[n]).wait()
+
+
+def held(value, after):
+    return pl.pallas_call(
+        lambda *refs: None,
+        out_shape=jax.ShapeDtypeStruct(value.shape, value.dtype),
+        in_specs=[ANY] * (1 + len(after)),
+        out_specs=ANY,
+        input_output_aliases={0: 0},
+    )(value, *after)
 
 
 def swap(value, bit, devices):
@@ -269,74 +338,76 @@
         * lax.rsqrt(jnp.mean(as_float * as_float, axis=-1, keepdims=True) + 1e-06)
     ).astype(BF16)
 
-    pieces = []
-    cuts = lane_cuts(latent, (3, 3, 1))
-    before = []
-    for turn_at, (start, width) in enumerate(cuts):
-        served = pl.pallas_call(
-            functools.partial(serve_kernel, owners, slots, owned, start, len(before)),
-            out_shape=[jax.ShapeDtypeStruct((slots, slice_tokens, width), BF16)]
-            * owners,
-            in_specs=[SMEM, SMEM, ANY] + [ANY] * len(before),
-            out_specs=[VMEM] * owners,
+    heights = [w.shape[0] for w in (w_query, w_key, w_value)]
+
+    def serve(start, width, by_peer, lay=(), after=()):
+        lengths = [slots] * owners if by_peer else [owners * slots]
+        shapes = [
+            jax.ShapeDtypeStruct((n, slice_tokens, width), BF16) for n in lengths
+        ]
+        if lay:
+            shapes.append(jax.ShapeDtypeStruct((sum(heights), inner), BF16))
+        return pl.pallas_call(
+            functools.partial(
+                serve_kernel, owners, slots, owned, start, len(lay), len(after)
+            ),
+            out_shape=shapes,
+            in_specs=[SMEM, SMEM, HBM] + [HBM] * len(lay) + [ANY] * len(after),
+            out_specs=[VMEM] * len(shapes),
             scratch_shapes=[
                 pltpu.SMEM((owners * slots + 1,), jnp.int32),
                 pltpu.SemaphoreType.DMA,
             ],
-            compiler_params=pltpu.CompilerParams(vmem_limit_bytes=16 << 20),
-        )(ids, place, latent_cache, *before)
-        arrived = [
-            part if k == 0 else swap(part, k * shards, devices)
-            for k, part in enumerate(served)
-        ]
-        if turn_at == 0:
-            heights = [w.shape[0] for w in (w_query, w_key, w_value)]
-            weights = pl.pallas_call(
-                functools.partial(concat_kernel, 1),
-                out_shape=jax.ShapeDtypeStruct((sum(heights), inner), BF16),
-                in_specs=[VMEM] * 3 + [ANY],
-                out_specs=VMEM,
-                compiler_params=pltpu.CompilerParams(vmem_limit_bytes=16 << 20),
-            )(w_query, w_key, w_value, served[0])
-            before = [weights]
-            weights = lax.all_gather(weights, "shard", axis=0)
-            a, b = heights[0], heights[0] + heights[1]
-            query_full = weights[:, :a].reshape(-1, inner)
-            key_full = weights[:, a:b].reshape(-1, inner)
-            value_full = weights[:, b:].reshape(-1, inner)
-            query_sum = jnp.dot(normed, query_full, preferred_element_type=F32)
-            queries = (query_sum * scale).astype(BF16)
-            normed_t = normed.T
-        else:
-            before = [served[0]]
-        ready = []
-        if turn_at == len(cuts) - 1:
-            ready = [queries, key_full, value_full, normed_t]
+            compiler_params=pltpu.CompilerParams(vmem_limit_bytes=58 << 20),
+        )(ids, place, latent_cache, *lay, *after)
+
+    def send(rows):
+        return lax.all_to_all(rows, "dp", split_axis=0, concat_axis=0, tiled=True)
+
+    def pick(arrived, width, after=()):
         picked = pl.pallas_call(
-            functools.partial(pick_kernel, owners, shards, owned, len(ready)),
+            functools.partial(
+                pick_kernel, owners, slots, shards, owned, len(arrived), len(after)
+            ),
             out_shape=[jax.ShapeDtypeStruct((each, slice_tokens, width), BF16)]
             * shards,
-            in_specs=[SMEM, SMEM] + [ANY] * (owners + len(ready)),
+            in_specs=[SMEM, SMEM] + [ANY] * (len(arrived) + len(after)),
             out_specs=[VMEM] * shards,
             scratch_shapes=[
                 pltpu.SMEM((owners + group,), jnp.int32),
                 pltpu.SemaphoreType.DMA,
             ],
             compiler_params=pltpu.CompilerParams(vmem_limit_bytes=16 << 20),
-        )(ids, place, *arrived, *ready)
-        pieces += [
+        )(ids, place, *arrived, *after)
+        return [
             piece if k == 0 else swap(piece, k, devices)
             for k, piece in enumerate(picked)
         ]
 
+    cut_0, cut_1, cut_2 = lane_cuts(latent, (3, 3, 1))
+    rows_0, weights = serve(*cut_0, False, (w_query, w_key, w_value))
+    arrived_0 = send(rows_0)
+    weights = lax.all_gather(weights, "shard", axis=0)
+    rows_1 = serve(*cut_1, True, (), [rows_0])
+    arrived_1 = [
+        part if k == 0 else swap(part, k * shards, devices)
+        for k, part in enumerate(rows_1)
+    ]
+    pieces_0 = pick([arrived_0], cut_0[1])
+    query_full = weights[:, : heights[0]].reshape(-1, inner)
+    query_sum = jnp.dot(normed, query_full, preferred_element_type=F32)
+    queries = (query_sum * scale).astype(BF16)
+    normed_t = normed.T
+    (rows_2,) = serve(*cut_2, False, (), [rows_1[0]])
+    rows_2 = held(rows_2, [arrived_0, *arrived_1[1:], queries, pieces_0[0]])
+    arrived_2 = send(rows_2)
+    pieces_1 = pick(arrived_1, cut_1[1])
+    pieces_2 = pick([arrived_2], cut_2[1], pieces_1[:1])
+    pieces = pieces_0 + pieces_1 + pieces_2
+
     keys = nbr * shards * slice_tokens
     width_q = tokens.shape[1]
     by_span = pl.BlockSpec((span, inner), lambda c: (c, 0))
-
-    def fixed(*shape):
-        return pl.BlockSpec(
-            shape, lambda c: (0,) * len(shape), pipeline_mode=pl.Buffered(1)
-        )
 
     low = 1 << (owners.bit_length() - 1) // 2
     length = dict(z=owners // low, x=low, y=shards // 2)
@@ -354,13 +425,11 @@
 
     rows_k = -(-latent // devices // 16) * 16
     rows_q = width_q // devices
-    shared = max(0, (rows_k + rows_q) // 32 * 16 - rows_k)
-    blocks, block_specs = [], []
+    shared = rows_q // 64 * 16
+    blocks = []
     for rows in (rows_k, rows_k + shared, rows_q - shared):
-        for kind in (F32, BF16):
-            shape = (devices // 2, rows, inner)
-            blocks.append(jax.ShapeDtypeStruct(shape, kind))
-            block_specs.append(fixed(*shape))
+        shape = (devices // 2, rows, inner)
+        blocks += [jax.ShapeDtypeStruct(shape, BF16)] * 2
     spare = rows_k
     context, *blocks = pl.pallas_call(
         functools.partial(
@@ -379,9 +448,8 @@
             pl.BlockSpec((nbr, slice_tokens, piece.shape[2]), lambda c: (c, 0, 0))
             for piece in pieces
         ]
-        + [SMEM, by_span, by_span, fixed(width_q, spans * span)]
-        + [fixed(latent, inner)] * 2,
-        out_specs=[by_span] + block_specs,
+        + [SMEM, by_span, by_span, ANY, ANY],
+        out_specs=[by_span] + [ANY] * len(blocks),
         scratch_shapes=[pltpu.VMEM((keys, inner), BF16)] * 2
         + [pltpu.VMEM((heads * span, keys), F32)] * 2
         + [pltpu.VMEM((heads * span, keys), BF16)] * 2
@@ -391,29 +459,37 @@
         ]
         + [pltpu.VMEM((spans * keys, inner), BF16)] * 2
         + [pltpu.VMEM((latent + spare, inner), F32)] * 2
-        + [pltpu.VMEM((width_q, inner), F32)],
-        compiler_params=pltpu.CompilerParams(vmem_limit_bytes=VMEM_LIMIT),
+        + [pltpu.VMEM((2, 8 * width_q // devices, inner), F32)]
+        + [pltpu.VMEM(block.shape, BF16) for block in blocks]
+        + [pltpu.VMEM((latent, inner), BF16)] * 2
+        + [
+            pltpu.VMEM(normed_t.shape, BF16),
+            pltpu.SemaphoreType.DMA((2,)),
+            pltpu.SemaphoreType.DMA,
+            pltpu.SemaphoreType.DMA((6,)),
+        ],
+        compiler_params=pltpu.CompilerParams(vmem_limit_bytes=58 << 20),
         cost_estimate=pl.CostEstimate(
             flops=2 * inner * (4 * spans * keys * (latent + 2 * span) + tokens.size),
             bytes_accessed=12 * (2 * latent + width_q) * inner,
             transcendentals=spans * span * keys * heads,
         ),
-    )(*pieces, place, queries, ctx_cotangent, normed_t, key_full, value_full)
+    )(*pieces, place, queries, ctx_cotangent, normed_t, weights)
 
     def travel(sends, axis):
         return [swap(part, k * bit[axis], devices) for k, part in enumerate(sends, 1)]
 
     keep_v, send_v, keep_p, send_p, keep_r, send_r = blocks
-    came_v, came_p, came_r = (swap(s, 1, devices) for s in (send_v, send_p, send_r))
-    keep_v, sends = combine([[keep_v, came_v]], length["z"])
-    came_v = travel(sends, "z")
+    came_r, came_p, came_v = (swap(s, 1, devices) for s in (send_r, send_p, send_v))
+    keep_r, sends = combine([[keep_r, came_r]], length["x"])
+    came_r = travel(sends, "x")
     keep_p, sends = combine([[keep_p, came_p]], length["y"], sends[:1])
     came_p = travel(sends, "y")
-    keep_r, sends = combine([[keep_r, came_r]], length["x"], sends[:1])
-    came_r = travel(sends, "x")
-    keep_p, sends = combine([[keep_p, *came_p]], length["x"], sends[:1])
+    keep_v, sends = combine([[keep_v, came_v]], length["z"], sends[:1])
+    came_v = travel(sends, "z")
+    keep_p, sends = combine([[keep_p, *came_p]], length["x"], came_v[:1])
     came_p = travel(sends, "x")
-    keep_r, sends = combine([[keep_r, *came_r]], length["y"], sends[:1])
+    keep_r, sends = combine([[keep_r, *came_r]], length["y"], [*sends[:1], *came_v[:2]])
     came_r = travel(sends, "y")
     keep_v, sends = combine([[keep_v, *came_v]], length["y"], sends[:1])
     came_v = travel(sends, "y")
@@ -423,13 +499,18 @@
     came = travel(sends, "z")
     keep_v, sends = combine([[keep_v, *came_v]], length["x"], sends[:1])
     came_v = travel(sends, "x")
-
-    def whole_sum(parts):
-        return sum((part[0].astype(F32) for part in parts[1:]), parts[0][0])
-
-    grad_value = whole_sum([keep_v, *came_v])[: latent // devices]
-    rest = whole_sum([keep, *came])
-    grad_key, grad_query = rest[: latent // devices], rest[rows_k:]
+    ends = [keep_v, *came_v, keep, *came]
+    grad_query, grad_key, grad_value = pl.pallas_call(
+        functools.partial(finish_kernel, 1 + len(came_v), rows_k),
+        out_shape=[
+            jax.ShapeDtypeStruct((rows_q, inner), F32),
+            jax.ShapeDtypeStruct((latent // devices, inner), F32),
+            jax.ShapeDtypeStruct((latent // devices, inner), F32),
+        ],
+        in_specs=[VMEM] * len(ends),
+        out_specs=[VMEM] * 3,
+        compiler_params=pltpu.CompilerParams(vmem_limit_bytes=16 << 20),
+    )(*ends)
     return context, grad_query, grad_key, grad_value
 
 

time: 237 us -> 234 us (0.987)
  starting transfers between devices: 73.3 us -> 61.5 us
  local copies, waits for them, and re-layouts: 22.3 us -> 15 us
  Pallas kernels: 45 us -> 52 us
  waiting for transfers between devices: 78 us -> 84.3 us
    ppermute x45 -> x31, starting transfers between devices: 65.9 us -> 40.2 us  [swap(): return lax.ppermute(value, AXES, [(i, i ^ bit) for i in range(devices)])]
    all_to_all x0 -> x2, waiting for transfers between devices: none -> 21.3 us  [send(): return lax.all_to_all(rows, 'dp', split_axis=0, concat_axis=0, tiled=True)]
    ppermute x45 -> x31, waiting for transfers between devices: 71.1 us -> 50.9 us  [swap(): return lax.ppermute(value, AXES, [(i, i ^ bit) for i in range(devices)])]
    all_to_all x0 -> x2, starting transfers between devices: none -> 14 us  [send(): return lax.all_to_all(rows, 'dp', split_axis=0, concat_axis=0, tiled=True)]
    pallas_call x7 -> x8, Pallas kernels: 20.6 us -> 27.4 us  [the longest x3 18.4 us: serve(): pl.pallas_call(functools.partial(serve_kernel, owners, slots, owned, star...]
    all_gather x1, waiting for transfers between devices: 0.01 us -> 5.67 us  [body(): weights = lax.all_gather(weights, 'shard', axis=0)]
    slice x4 -> x1, local copies, waits for them, and re-layouts: 6.62 us -> 2.74 us  [body(): query_full = weights[:, :heights[0]].reshape(-1, inner)]
    unnamed x64 -> x78, local copies, waits for them, and re-layouts: 14.9 us -> 11.5 us
  transfers between devices with their start and end apart: 47 -> 35, of which waited for: 19 -> 19; matrix products, arithmetic and copies ran while one was open for 5% -> 4% of each run, Pallas kernels for 8% -> 9%
where the time goes in v3:
time: 234 us; the launch traced here: 233 us
  waiting for transfers between devices  84.3 us (36%)
  starting transfers between devices  61.5 us (26%)
  Pallas kernels  52 us (22%)
  local copies, waits for them, and re-layouts  15 us (6%)
  between operations  14.5 us (6%)
  other arithmetic  3.41 us (1%)
    ppermute x31, waiting for transfers between devices, swap(): return lax.ppermute(value, AXES, [(i, i ^ bit) for i in range(devices)])  50.9 us
    ppermute x31, starting transfers between devices, swap(): return lax.ppermute(value, AXES, [(i, i ^ bit) for i in range(devices)])  40.2 us
    pallas_call x1, Pallas kernels, body(): pl.pallas_call(functools.partial(attend_kernel, len(pieces) // shards, sh...  22.9 us
    all_to_all x2, waiting for transfers between devices, send(): return lax.all_to_all(rows, 'dp', split_axis=0, concat_axis=0, tiled=True)  21.3 us
    pallas_call x3, Pallas kernels, serve(): pl.pallas_call(functools.partial(serve_kernel, owners, slots, owned, star...  18.4 us
    all_to_all x2, starting transfers between devices, send(): return lax.all_to_all(rows, 'dp', split_axis=0, concat_axis=0, tiled=True)  14 us
    unnamed x78, local copies, waits for them, and re-layouts  11.5 us
    pallas_call x3, Pallas kernels, pick(): pl.pallas_call(functools.partial(pick_kernel, owners, slots, shards, owne...  8.18 us
  transfers between devices with their start and end apart: 35, of which 19 were waited for; matrix products, arithmetic and copies ran while one was open for 4% of the time, Pallas kernels for 9%

profile of v3, /device:TPU:0, one launch (start us, length us, event | category | flops | bytes accessed | tf_op | source)
XLA Modules:
  0.0 232.8 jit_solution(17965164042595340023)
XLA Ops:
  8.6 7.3 %all-to-all-start = ((s32[32,1,8]{2,1,0:T(1,128)}), s32[32,1,8]{2,1,0:T(1,128)S(1)}, u32[]{:S(2)}, u32[]{:S(2)}) async-start(s32[32,1,8]{2,1,0:T(1,128)} %broadcast_in_dim.9), calls=%async_computation | async-start | bytes 32768 | tf_op jit(solution)/shard_map/all_to_all | solution.py:328
  16.6 6.4 %all-to-all-done = s32[32,1,8]{2,1,0:T(1,128)S(1)} async-done(((s32[32,1,8]{2,1,0:T(1,128)}), s32[32,1,8]{2,1,0:T(1,128)S(1)}, u32[]{:S(2)}, u32[]{:S(2)}) %all-to-all-start) | async-done | bytes 1056 | tf_op jit(solution)/shard_map/all_to_all | solution.py:328
  23.6 6.8 %shard_map.102 = (bf16[64,32,384]{2,1,0:T(8,128)(2,1)}, bf16[960,1024]{1,0:T(8,128)(2,1)}) custom-call(s32[32,8]{1,0:T(8,128)} %bitcast.9, s32[3]{0:T(128)} %pad_add_fusion.place.refs_12_, bf16[128,32,896]{2,1,0:T(8,128)(2,1)} %cache.5, bf16[512,1024]{1,0:T(8,128)(2,1)} %rest_0_.1, bf16[224,1024]{1,0:T(8,128)(2,1)} %rest_1_.1, bf16[224,1024]{1,0:T(8,128)(2,1)} %rest_2_.1), custom_call_target="tpu_custom_call" | custom-call | tf_op jit(solution)/shard_map/pallas_call | solution.py:350
  30.5 3.6 %all-to-all-start.1 = ((bf16[64,32,384]{2,1,0:T(8,128)(2,1)}), bf16[64,32,384]{2,1,0:T(8,128)(2,1)S(1)}, u32[]{:S(2)}, u32[]{:S(2)}) async-start(bf16[64,32,384]{2,1,0:T(8,128)(2,1)} %get-tuple-element.56.rest_0_), calls=%async_computation.1 | async-start | bytes 3145728 | tf_op jit(solution)/shard_map/all_to_all | solution.py:365
  34.1 1.6 copy.17
  36.0 6.0 %shard_map.104 = (bf16[8,32,384]{2,1,0:T(8,128)(2,1)}, bf16[8,32,384]{2,1,0:T(8,128)(2,1)}, bf16[8,32,384]{2,1,0:T(8,128)(2,1)}, bf16[8,32,384]{2,1,0:T(8,128)(2...) custom-call(s32[32,8]{1,0:T(8,128)} %bitcast.10, ...), custom_call_target="tpu_custom_call" | custom-call | tf_op jit(solution)/shard_map/pallas_call | solution.py:350
  42.4 2.6 %collective-permute-start.4 = (bf16[8,32,384]{2,1,0:T(8,128)(2,1)}, bf16[8,32,384]{2,1,0:T(8,128)(2,1)S(1)}, u32[]{:S(2)}, u32[]{:S(2)}) collective-permute-start(bf16[8,32,384]{2,1,0:T(8,128)(2,1)} %get-tuple-element.63), channel_id=1, source_target_pairs={{0,8},{1,9},{2,10},{3,11},{4,12},{5,13},{6,14},{7,15},{8,0},{9,1},... | collective-permute-start | bytes 589832 | tf_op jit(solution)/shard_map/ppermute | solution.py:310
  45.6 2.4 %collective-permute-start.6 = (bf16[8,32,384]{2,1,0:T(8,128)(2,1)}, bf16[8,32,384]{2,1,0:T(8,128)(2,1)S(1)}, u32[]{:S(2)}, u32[]{:S(2)}) collective-permute-start(bf16[8,32,384]{2,1,0:T(8,128)(2,1)} %get-tuple-element.65), channel_id=1, source_target_pairs={{0,16},{1,17},{2,18},{3,19},{4,20},{5,21},{6,22},{7,23},{8,24},{9,... | collective-permute-start | bytes 589832 | tf_op jit(solution)/shard_map/ppermute | solution.py:310
  48.0 1.2 collective-permute-start.7
  49.2 5.6 %shard_map.106.refs_0_ = bf16[64,32,128]{2,1,0:T(8,128)(2,1)} custom-call(s32[32,8]{1,0:T(8,128)} %bitcast.11, s32[3]{0:T(128)} %pad_add_fusion.place.refs_12_, bf16[128,32,896]{2,1,0:T(8,128)(2,1)} %cache.5, bf16[8,32,384]{2,1,0:T(8,128)(2,1)} %get-tuple-element.61.rest_0_), custom_call_target="tpu_custom_call" | custom-call | tf_op jit(solution)/shard_map/pallas_call | solution.py:350
  54.8 18.7 %all-to-all-done.1.rest_0_.refs_1_ = bf16[64,32,384]{2,1,0:T(8,128)(2,1)S(1)} async-done(((bf16[64,32,384]{2,1,0:T(8,128)(2,1)}), bf16[64,32,384]{2,1,0:T(8,128)(2,1)S(1)}, u32[]{:S(2)}, u32[]{:S(2)}) %all-to-all-start.1) | async-done | bytes 1572896 | tf_op jit(solution)/shard_map/all_to_all | solution.py:365
  73.5 2.4 %shard_map.103 = (bf16[8,32,384]{2,1,0:T(8,128)(2,1)S(1)}, bf16[8,32,384]{2,1,0:T(8,128)(2,1)S(1)}, bf16[8,32,384]{2,1,0:T(8,128)(2,1)S(1)}, bf16[8,32,384]{2,1,0:T(8,128)(2,1)S(1)}) custom-call(s32[32,8]{1,0:T(8,128)S(1)} %bitcast.12, s32[3]{0:T(128)S(1)} %copy-done.23, bf16[64,32,384]{2,1,0:T(8,128)(2,1)S(1)} %all-to-all-done.1.rest_0_.refs_1_), custom_call_target="tpu_custom_call" | custom-call | tf_op jit(solution)/shard_map/pallas_call | solution.py:368
  76.6 5.7 %all-gather.3.cloned.1.call-done = bf16[3840,1024]{1,0:T(8,128)(2,1)} async-done(((bf16[960,1024]{1,0:T(8,128)(2,1)}), bf16[3840,1024]{1,0:T(8,128)(2,1)}) %all-gather.3.cloned.1.call-update) | async-done | bytes 7864336 | tf_op jit(solution)/shard_map/all_gather | solution.py:390
  82.3 2.7 %slice.4 = bf16[4,512,1024]{2,1,0:T(8,128)(2,1)S(1)} slice(bf16[4,960,1024]{2,1,0:T(8,128)(2,1)} %bitcast.16), slice={[0:4], [0:512], [0:1024]} | slice | bytes 8388608 | tf_op jit(solution)/shard_map/slice | solution.py:397
  85.0 3.4 %collective-permute-start.8 = (bf16[8,32,384]{2,1,0:T(8,128)(2,1)S(1)}, bf16[8,32,384]{2,1,0:T(8,128)(2,1)S(1)}, u32[]{:S(2)}, u32[]{:S(2)}) collective-permute-start(bf16[8,32,384]{2,1,0:T(8,128)(2,1)S(1)} %copy-done.33), channel_id=1, source_target_pairs={{0,24},{1,25},{2,26},{3,27},{4,28},{5,29},{6,30},{7,31},{8,16},{9,... | collective-permute-start | bytes 589832 | tf_op jit(solution)/shard_map/ppermute | solution.py:310
  88.4 1.5 collective-permute-start.9
  89.9 2.1 fusion.2.refs_9_.refs_13_
  92.1 2.2 collective-permute-done.8.rest_6_.refs_7_
  94.2 5.0 %collective-permute-done.9.rest_7_.refs_8_ = bf16[8,32,384]{2,1,0:T(8,128)(2,1)S(1)} collective-permute-done((bf16[8,32,384]{2,1,0:T(8,128)(2,1)S(1)}, bf16[8,32,384]{2,1,0:T(8,128)(2,1)S(1)}, u32[]{:S(2)}, u32[]{:S(2)}) %collective-permute-start.9) | collective-permute-done | bytes 196640 | tf_op jit(solution)/shard_map/ppermute | solution.py:310
  99.9 10.3 %all-to-all-start.2 = ((bf16[64,32,128]{2,1,0:T(8,128)(2,1)}), bf16[64,32,128]{2,1,0:T(8,128)(2,1)S(1)}, u32[]{:S(2)}, u32[]{:S(2)}) async-start(bf16[64,32,128]{2,1,0:T(8,128)(2,1)} %shard_map.107), calls=%async_computation.2 | async-start | bytes 1048576 | tf_op jit(solution)/shard_map/all_to_all | solution.py:365
  111.2 0.9 copy-done.13
  113.0 0.9 copy-done.17
  114.0 0.9 copy-done.19
  114.9 4.0 %shard_map.105 = (bf16[8,32,384]{2,1,0:T(8,128)(2,1)S(1)}, bf16[8,32,384]{2,1,0:T(8,128)(2,1)S(1)}, bf16[8,32,384]{2,1,0:T(8,128)(2,1)S(1)}, bf16[8,32,384]{2,1,0:T(8,128)(2,1)S(1)}) custom-call(s32[32,8]{1,0:T(8,128)S(1)} %bitcast.13, s32[3]{0:T(128)S(1)} %copy-done.23, bf16[8,32,384]{2,1,0:T(8,128)(2,1)S(1)} %copy-done.20, ...), custom_call_target="tpu_custom_call" | custom-call | tf_op jit(solution)/shard_map/pallas_call | solution.py:368
  119.6 1.2 collective-permute-start.12
  121.8 2.6 %all-to-all-done.2.rest_0_ = bf16[64,32,128]{2,1,0:T(8,128)(2,1)S(1)} async-done(((bf16[64,32,128]{2,1,0:T(8,128)(2,1)}), bf16[64,32,128]{2,1,0:T(8,128)(2,1)S(1)}, u32[]{:S(2)}, u32[]{:S(2)}) %all-to-all-start.2) | async-done | bytes 524320 | tf_op jit(solution)/shard_map/all_to_all | solution.py:365
  124.4 1.7 shard_map.108
  126.9 3.2 %collective-permute-done.12.refs_7_ = bf16[8,32,384]{2,1,0:T(8,128)(2,1)S(1)} collective-permute-done((bf16[8,32,384]{2,1,0:T(8,128)(2,1)S(1)}, bf16[8,32,384]{2,1,0:T(8,128)(2,1)S(1)}, u32[]{:S(2)}, u32[]{:S(2)}) %collective-permute-start.12) | collective-permute-done | bytes 196640 | tf_op jit(solution)/shard_map/ppermute | solution.py:310
  130.6 1.5 collective-permute-start.15
  132.2 2.4 %fusion.3.refs_15_ = bf16[2048,256]{1,0:T(8,128)(2,1)} fusion(f32[256]{0:T(256)S(1)} %add_rsqrt_fusion, bf16[256,2048]{0,1:T(8,128)(2,1)} %copy-done.25), kind=kLoop, calls=%fused_computation.6 | loop fusion | flops 1572864 | bytes 2098176 | tf_op jit(solution)/shard_map/transpose | solution.py:400
  135.2 3.3 %collective-permute-done.2.refs_3_ = bf16[8,32,384]{2,1,0:T(8,128)(2,1)S(1)} collective-permute-done((bf16[8,32,384]{2,1,0:T(8,128)(2,1)S(1)}, bf16[8,32,384]{2,1,0:T(8,128)(2,1)S(1)}, u32[]{:S(2)}, u32[]{:S(2)}) %collective-permute-start.2) | collective-permute-done | bytes 196640 | tf_op jit(solution)/shard_map/ppermute | solution.py:310
  138.5 2.3 collective-permute-done.14.refs_10_
  141.9 22.9 %shard_map.109 = (bf16[256,1024]{1,0:T(8,128)(2,1)}, bf16[16,32,1024]{2,1,0:T(8,128)(2,1)}, bf16[16,32,1024]{2,1,0:T(8,128)(2,1)}, bf16[16,48,1024]{2,1,0:T(8,12...) custom-call(bf16[8,32,384]{2,1,0:T(8,128)(2,1)} %copy-done.21, ...), custom_call_target="tpu_custom_call" | custom-call | flops 9663676416 | bytes 47185920 | tf_op jit(solution)/shard_map/pallas_call | solution.py:434
  165.7 2.8 %collective-permute-done.18.refs_1_ = bf16[16,48,1024]{2,1,0:T(8,128)(2,1)S(1)} collective-permute-done((bf16[16,48,1024]{2,1,0:T(8,128)(2,1)}, bf16[16,48,1024]{2,1,0:T(8,128)(2,1)S(1)}, u32[]{:S(2)}, u32[]{:S(2)}) %collective-permute-start.18) | collective-permute-done | bytes 1572896 | tf_op jit(solution)/shard_map/ppermute | solution.py:310
  168.6 1.4 copy-done.1
  172.4 2.0 collective-permute-start.22
  174.7 1.5 collective-permute-start.19
  176.3 2.4 %collective-permute-start.20 = (bf16[4,32,1024]{2,1,0:T(8,128)(2,1)S(1)}, bf16[4,32,1024]{2,1,0:T(8,128)(2,1)S(1)}, u32[]{:S(2)}, u32[]{:S(2)}) collective-permute-start(bf16[4,32,1024]{2,1,0:T(8,128)(2,1)S(1)} %get-tuple-element.89), channel_id=1, source_target_pairs={{0,16},{1,17},{2,18},{3,19},{4,20},{5,21},{6,22},{7,23},{8,24},{9,... | collective-permute-start | bytes 786440 | tf_op jit(solution)/shard_map/ppermute | solution.py:310
  178.6 9.5 %collective-permute-done.19.refs_2_.refs_3_.refs_1_ = bf16[4,32,1024]{2,1,0:T(8,128)(2,1)S(1)} collective-permute-done((bf16[4,32,1024]{2,1,0:T(8,128)(2,1)S(1)}, bf16[4,32,1024]{2,1,0:T(8,128)(2,1)S(1)}, u32[]{:S(2)}, u32[]{:S(2)}) %collective-permute-start.19) | collective-permute-done | bytes 262176 | tf_op jit(solution)/shard_map/ppermute | solution.py:310
  188.1 3.5 %collective-permute-done.23.refs_1_ = bf16[8,48,1024]{2,1,0:T(8,128)(2,1)S(1)} collective-permute-done((bf16[8,48,1024]{2,1,0:T(8,128)(2,1)S(1)}, bf16[8,48,1024]{2,1,0:T(8,128)(2,1)S(1)}, u32[]{:S(2)}, u32[]{:S(2)}) %collective-permute-start.23) | collective-permute-done | bytes 786464 | tf_op jit(solution)/shard_map/ppermute | solution.py:310
  191.8 2.1 collective-permute-start.25
  194.6 3.3 %collective-permute-start.21 = (bf16[4,32,1024]{2,1,0:T(8,128)(2,1)S(1)}, bf16[4,32,1024]{2,1,0:T(8,128)(2,1)S(1)}, u32[]{:S(2)}, u32[]{:S(2)}) collective-permute-start(bf16[4,32,1024]{2,1,0:T(8,128)(2,1)S(1)} %get-tuple-element.90), channel_id=1, source_target_pairs={{0,24},{1,25},{2,26},{3,27},{4,28},{5,29},{6,30},{7,31},{8,16},{9,... | collective-permute-start | bytes 786440 | tf_op jit(solution)/shard_map/ppermute | solution.py:310
  197.9 5.8 %collective-permute-done.21.refs_3_ = bf16[4,32,1024]{2,1,0:T(8,128)(2,1)S(1)} collective-permute-done((bf16[4,32,1024]{2,1,0:T(8,128)(2,1)S(1)}, bf16[4,32,1024]{2,1,0:T(8,128)(2,1)S(1)}, u32[]{:S(2)}, u32[]{:S(2)}) %collective-permute-start.21) | collective-permute-done | bytes 262176 | tf_op jit(solution)/shard_map/ppermute | solution.py:310
  203.8 1.5 collective-permute-start.24
  205.5 6.2 %collective-permute-start.29 = (bf16[1,96,1024]{2,1,0:T(8,128)(2,1)S(1)}, bf16[1,96,1024]{2,1,0:T(8,128)(2,1)S(1)}, u32[]{:S(2)}, u32[]{:S(2)}) collective-permute-start(bf16[1,96,1024]{2,1,0:T(8,128)(2,1)S(1)} %get-tuple-element.103), channel_id=1, source_target_pairs={{0,16},{1,17},{2,18},{3,19},{4,20},{5,21},{6,22},{7,23},{8,24},{9,... | collective-permute-start | bytes 589832 | tf_op jit(solution)/shard_map/ppermute | solution.py:310
  211.6 1.5 collective-permute-start.30
  213.7 3.7 %collective-permute-done.27.refs_1_ = bf16[1,32,1024]{2,1,0:T(8,128)(2,1)S(1)} collective-permute-done((bf16[1,32,1024]{2,1,0:T(8,128)(2,1)S(1)}, bf16[1,32,1024]{2,1,0:T(8,128)(2,1)S(1)}, u32[]{:S(2)}, u32[]{:S(2)}) %collective-permute-start.27) | collective-permute-done | bytes 65568 | tf_op jit(solution)/shard_map/ppermute | solution.py:310
  217.4 7.7 %collective-permute-done.29.refs_4_ = bf16[1,96,1024]{2,1,0:T(8,128)(2,1)S(1)} collective-permute-done((bf16[1,96,1024]{2,1,0:T(8,128)(2,1)S(1)}, bf16[1,96,1024]{2,1,0:T(8,128)(2,1)S(1)}, u32[]{:S(2)}, u32[]{:S(2)}) %collective-permute-start.29) | collective-permute-done | bytes 196640 | tf_op jit(solution)/shard_map/ppermute | solution.py:310
  (126 shorter events, 18.2 us)
Async XLA Ops:
  8.6 14.4 %all-to-all-start = ((s32[32,1,8]{2,1,0:T(1,128)}), s32[32,1,8]{2,1,0:T(1,128)S(1)}, u32[]{:S(2)}, u32[]{:S(2)}) async-start(s32[32,1,8]{2,1,0:T(1,128)} %broadcast_in_dim.9), calls=%async_computation | async-start | bytes 32768 | tf_op jit(solution)/shard_map/all_to_all | solution.py:328
  15.9 66.3 %all-gather.3.cloned.1.call-start = ((), (), s32[]{:S(2)}) async-start(), calls=%async_computation.3 | async-start | bytes 9830400 | tf_op jit(solution)/shard_map/all_gather | solution.py:390
  30.5 43.0 %all-to-all-start.1 = ((bf16[64,32,384]{2,1,0:T(8,128)(2,1)}), bf16[64,32,384]{2,1,0:T(8,128)(2,1)S(1)}, u32[]{:S(2)}, u32[]{:S(2)}) async-start(bf16[64,32,384]{2,1,0:T(8,128)(2,1)} %get-tuple-element.56.rest_0_), calls=%async_computation.1 | async-start | bytes 3145728 | tf_op jit(solution)/shard_map/all_to_all | solution.py:365
  42.0 43.0 %collective-permute-start.3 = (bf16[8,32,384]{2,1,0:T(8,128)(2,1)}, bf16[8,32,384]{2,1,0:T(8,128)(2,1)S(1)}, u32[]{:S(2)}, u32[]{:S(2)}) collective-permute-start(bf16[8,32,384]{2,1,0:T(8,128)(2,1)} %get-tuple-element.62), channel_id=1, source_target_pairs={{0,4},{1,5},{2,6},{3,7},{4,0},{5,1},{6,2},{7,3},{8,12},{9,13},{10,... | collective-permute-start | bytes 589832 | tf_op jit(solution)/shard_map/ppermute | solution.py:310
  42.4 46.0 %collective-permute-start.4 = (bf16[8,32,384]{2,1,0:T(8,128)(2,1)}, bf16[8,32,384]{2,1,0:T(8,128)(2,1)S(1)}, u32[]{:S(2)}, u32[]{:S(2)}) collective-permute-start(bf16[8,32,384]{2,1,0:T(8,128)(2,1)} %get-tuple-element.63), channel_id=1, source_target_pairs={{0,8},{1,9},{2,10},{3,11},{4,12},{5,13},{6,14},{7,15},{8,0},{9,1},... | collective-permute-start | bytes 589832 | tf_op jit(solution)/shard_map/ppermute | solution.py:310
  45.0 47.0 %collective-permute-start.5 = (bf16[8,32,384]{2,1,0:T(8,128)(2,1)}, bf16[8,32,384]{2,1,0:T(8,128)(2,1)S(1)}, u32[]{:S(2)}, u32[]{:S(2)}) collective-permute-start(bf16[8,32,384]{2,1,0:T(8,128)(2,1)} %get-tuple-element.64), channel_id=1, source_target_pairs={{0,12},{1,13},{2,14},{3,15},{4,8},{5,9},{6,10},{7,11},{8,4},{9,5},... | collective-permute-start | bytes 589832 | tf_op jit(solution)/shard_map/ppermute | solution.py:310
  45.6 46.4 %collective-permute-start.6 = (bf16[8,32,384]{2,1,0:T(8,128)(2,1)}, bf16[8,32,384]{2,1,0:T(8,128)(2,1)S(1)}, u32[]{:S(2)}, u32[]{:S(2)}) collective-permute-start(bf16[8,32,384]{2,1,0:T(8,128)(2,1)} %get-tuple-element.65), channel_id=1, source_target_pairs={{0,16},{1,17},{2,18},{3,19},{4,20},{5,21},{6,22},{7,23},{8,24},{9,... | collective-permute-start | bytes 589832 | tf_op jit(solution)/shard_map/ppermute | solution.py:310
  48.0 44.1 %collective-permute-start.7 = (bf16[8,32,384]{2,1,0:T(8,128)(2,1)}, bf16[8,32,384]{2,1,0:T(8,128)(2,1)S(1)}, u32[]{:S(2)}, u32[]{:S(2)}) collective-permute-start(bf16[8,32,384]{2,1,0:T(8,128)(2,1)} %get-tuple-element.66), channel_id=1, source_target_pairs={{0,20},{1,21},{2,22},{3,23},{4,16},{5,17},{6,18},{7,19},{8,28},{9,... | collective-permute-start | bytes 589832 | tf_op jit(solution)/shard_map/ppermute | solution.py:310
  49.2 24.3 %copy-start.5 = (s32[32,1,8]{2,1,0:T(1,128)S(1)}, s32[32,1,8]{2,1,0:T(1,128)}, u32[]{:S(2)}) copy-start(s32[32,1,8]{2,1,0:T(1,128)} %copy-done.4) | copy-start | bytes 3076
  49.2 24.3 %copy-start.23 = (s32[3]{0:T(128)S(1)}, s32[3]{0:T(128)}, u32[]{:S(2)}) copy-start(s32[3]{0:T(128)} %pad_add_fusion.place.refs_12_) | copy-start | bytes 40
  73.5 11.5 %copy-start = (bf16[64,32,384]{2,1,0:T(8,128)(2,1)}, bf16[64,32,384]{2,1,0:T(8,128)(2,1)S(1)}, u32[]{:S(2)}) copy-start(bf16[64,32,384]{2,1,0:T(8,128)(2,1)S(1)} %all-to-all-done.1.rest_0_.refs_1_) | copy-start | bytes 4718596
  82.3 7.7 %copy-start.26 = (bf16[256,2048]{0,1:T(8,128)(2,1)S(1)}, bf16[256,2048]{0,1:T(8,128)(2,1)}, u32[]{:S(2)}) copy-start(bf16[256,2048]{0,1:T(8,128)(2,1)} %copy-done.25) | copy-start | bytes 3145732
  85.0 9.2 %collective-permute-start.8 = (bf16[8,32,384]{2,1,0:T(8,128)(2,1)S(1)}, bf16[8,32,384]{2,1,0:T(8,128)(2,1)S(1)}, u32[]{:S(2)}, u32[]{:S(2)}) collective-permute-start(bf16[8,32,384]{2,1,0:T(8,128)(2,1)S(1)} %copy-done.33), channel_id=1, source_target_pairs={{0,24},{1,25},{2,26},{3,27},{4,28},{5,29},{6,30},{7,31},{8,16},{9,... | collective-permute-start | bytes 589832 | tf_op jit(solution)/shard_map/ppermute | solution.py:310
  88.4 10.8 %collective-permute-start.9 = (bf16[8,32,384]{2,1,0:T(8,128)(2,1)S(1)}, bf16[8,32,384]{2,1,0:T(8,128)(2,1)S(1)}, u32[]{:S(2)}, u32[]{:S(2)}) collective-permute-start(bf16[8,32,384]{2,1,0:T(8,128)(2,1)S(1)} %copy-done.32), channel_id=1, source_target_pairs={{0,28},{1,29},{2,30},{3,31},{4,24},{5,25},{6,26},{7,27},{8,20},{9,... | collective-permute-start | bytes 589832 | tf_op jit(solution)/shard_map/ppermute | solution.py:310
  99.9 10.3 %copy-start.7 = (bf16[8,32,384]{2,1,0:T(8,128)(2,1)S(1)}, bf16[8,32,384]{2,1,0:T(8,128)(2,1)}, u32[]{:S(2)}) copy-start(bf16[8,32,384]{2,1,0:T(8,128)(2,1)} %copy-done.6) | copy-start | bytes 589828
  99.9 10.4 %copy-start.9 = (bf16[8,32,384]{2,1,0:T(8,128)(2,1)S(1)}, bf16[8,32,384]{2,1,0:T(8,128)(2,1)}, u32[]{:S(2)}) copy-start(bf16[8,32,384]{2,1,0:T(8,128)(2,1)} %copy-done.8) | copy-start | bytes 589828
  99.9 10.4 %copy-start.20 = (bf16[8,32,384]{2,1,0:T(8,128)(2,1)S(1)}, bf16[8,32,384]{2,1,0:T(8,128)(2,1)}, u32[]{:S(2)}) copy-start(bf16[8,32,384]{2,1,0:T(8,128)(2,1)} %get-tuple-element.61.rest_0_) | copy-start | bytes 589828
  99.9 24.5 %all-to-all-start.2 = ((bf16[64,32,128]{2,1,0:T(8,128)(2,1)}), bf16[64,32,128]{2,1,0:T(8,128)(2,1)S(1)}, u32[]{:S(2)}, u32[]{:S(2)}) async-start(bf16[64,32,128]{2,1,0:T(8,128)(2,1)} %shard_map.107), calls=%async_computation.2 | async-start | bytes 1048576 | tf_op jit(solution)/shard_map/all_to_all | solution.py:365
  118.9 22.4 %copy-start.22 = (bf16[8,32,384]{2,1,0:T(8,128)(2,1)}, bf16[8,32,384]{2,1,0:T(8,128)(2,1)S(1)}, u32[]{:S(2)}) copy-start(bf16[8,32,384]{2,1,0:T(8,128)(2,1)S(1)} %get-tuple-element.69.rest_1_.refs_4_) | copy-start | bytes 589828
  118.9 7.2 %collective-permute-start.10 = (bf16[8,32,384]{2,1,0:T(8,128)(2,1)S(1)}, bf16[8,32,384]{2,1,0:T(8,128)(2,1)S(1)}, u32[]{:S(2)}, u32[]{:S(2)}) collective-permute-start(bf16[8,32,384]{2,1,0:T(8,128)(2,1)S(1)} %get-tuple-element.70), channel_id=1, source_target_pairs={{0,1},{1,0},{2,3},{3,2},{4,5},{5,4},{6,7},{7,6},{8,9},{9,8},{10,11... | collective-permute-start | bytes 589832 | tf_op jit(solution)/shard_map/ppermute | solution.py:310
  119.0 7.8 %collective-permute-start.11 = (bf16[8,32,384]{2,1,0:T(8,128)(2,1)S(1)}, bf16[8,32,384]{2,1,0:T(8,128)(2,1)S(1)}, u32[]{:S(2)}, u32[]{:S(2)}) collective-permute-start(bf16[8,32,384]{2,1,0:T(8,128)(2,1)S(1)} %get-tuple-element.71), channel_id=1, source_target_pairs={{0,2},{1,3},{2,0},{3,1},{4,6},{5,7},{6,4},{7,5},{8,10},{9,11},{10,... | collective-permute-start | bytes 589832 | tf_op jit(solution)/shard_map/ppermute | solution.py:310
  119.6 10.5 %collective-permute-start.12 = (bf16[8,32,384]{2,1,0:T(8,128)(2,1)S(1)}, bf16[8,32,384]{2,1,0:T(8,128)(2,1)S(1)}, u32[]{:S(2)}, u32[]{:S(2)}) collective-permute-start(bf16[8,32,384]{2,1,0:T(8,128)(2,1)S(1)} %get-tuple-element.72), channel_id=1, source_target_pairs={{0,3},{1,2},{2,1},{3,0},{4,7},{5,6},{6,5},{7,4},{8,11},{9,10},{10,... | collective-permute-start | bytes 589832 | tf_op jit(solution)/shard_map/ppermute | solution.py:310
  120.9 9.8 %collective-permute-start = (bf16[8,32,384]{2,1,0:T(8,128)(2,1)S(1)}, bf16[8,32,384]{2,1,0:T(8,128)(2,1)S(1)}, u32[]{:S(2)}, u32[]{:S(2)}) collective-permute-start(bf16[8,32,384]{2,1,0:T(8,128)(2,1)S(1)} %get-tuple-element.58), channel_id=1, source_target_pairs={{0,1},{1,0},{2,3},{3,2},{4,5},{5,4},{6,7},{7,6},{8,9},{9,8},{10,11... | collective-permute-start | bytes 589832 | tf_op jit(solution)/shard_map/ppermute | solution.py:310
  121.2 14.0 %collective-permute-start.1 = (bf16[8,32,384]{2,1,0:T(8,128)(2,1)S(1)}, bf16[8,32,384]{2,1,0:T(8,128)(2,1)S(1)}, u32[]{:S(2)}, u32[]{:S(2)}) collective-permute-start(bf16[8,32,384]{2,1,0:T(8,128)(2,1)S(1)} %get-tuple-element.59), channel_id=1, source_target_pairs={{0,2},{1,3},{2,0},{3,1},{4,6},{5,7},{6,4},{7,5},{8,10},{9,11},{10,... | collective-permute-start | bytes 589832 | tf_op jit(solution)/shard_map/ppermute | solution.py:310
  126.1 15.2 %copy-start.24 = (bf16[8,32,128]{2,1,0:T(8,128)(2,1)}, bf16[8,32,128]{2,1,0:T(8,128)(2,1)S(1)}, u32[]{:S(2)}) copy-start(bf16[8,32,128]{2,1,0:T(8,128)(2,1)S(1)} %get-tuple-element.74.refs_8_) | copy-start | bytes 196612
  126.1 15.2 %copy-start.27 = (bf16[8,32,384]{2,1,0:T(8,128)(2,1)}, bf16[8,32,384]{2,1,0:T(8,128)(2,1)S(1)}, u32[]{:S(2)}) copy-start(bf16[8,32,384]{2,1,0:T(8,128)(2,1)S(1)} %collective-permute-done.10.refs_5_) | copy-start | bytes 589828
  126.1 12.4 %collective-permute-start.2 = (bf16[8,32,384]{2,1,0:T(8,128)(2,1)S(1)}, bf16[8,32,384]{2,1,0:T(8,128)(2,1)S(1)}, u32[]{:S(2)}, u32[]{:S(2)}) collective-permute-start(bf16[8,32,384]{2,1,0:T(8,128)(2,1)S(1)} %get-tuple-element.60), channel_id=1, source_target_pairs={{0,3},{1,2},{2,1},{3,0},{4,7},{5,6},{6,5},{7,4},{8,11},{9,10},{10,... | collective-permute-start | bytes 589832 | tf_op jit(solution)/shard_map/ppermute | solution.py:310
  126.8 14.6 %copy-start.28 = (bf16[8,32,384]{2,1,0:T(8,128)(2,1)}, bf16[8,32,384]{2,1,0:T(8,128)(2,1)S(1)}, u32[]{:S(2)}) copy-start(bf16[8,32,384]{2,1,0:T(8,128)(2,1)S(1)} %collective-permute-done.11.refs_6_) | copy-start | bytes 589828
  126.8 11.7 %collective-permute-start.13 = (bf16[8,32,128]{2,1,0:T(8,128)(2,1)S(1)}, bf16[8,32,128]{2,1,0:T(8,128)(2,1)S(1)}, u32[]{:S(2)}, u32[]{:S(2)}) collective-permute-start(bf16[8,32,128]{2,1,0:T(8,128)(2,1)S(1)} %get-tuple-element.75), channel_id=1, source_target_pairs={{0,1},{1,0},{2,3},{3,2},{4,5},{5,4},{6,7},{7,6},{8,9},{9,8},{10,11... | collective-permute-start | bytes 196616 | tf_op jit(solution)/shard_map/ppermute | solution.py:310
  130.1 11.3 %copy-start.29 = (bf16[8,32,384]{2,1,0:T(8,128)(2,1)}, bf16[8,32,384]{2,1,0:T(8,128)(2,1)S(1)}, u32[]{:S(2)}) copy-start(bf16[8,32,384]{2,1,0:T(8,128)(2,1)S(1)} %collective-permute-done.12.refs_7_) | copy-start | bytes 589828
  130.1 10.7 %collective-permute-start.14 = (bf16[8,32,128]{2,1,0:T(8,128)(2,1)S(1)}, bf16[8,32,128]{2,1,0:T(8,128)(2,1)S(1)}, u32[]{:S(2)}, u32[]{:S(2)}) collective-permute-start(bf16[8,32,128]{2,1,0:T(8,128)(2,1)S(1)} %get-tuple-element.76), channel_id=1, source_target_pairs={{0,2},{1,3},{2,0},{3,1},{4,6},{5,7},{6,4},{7,5},{8,10},{9,11},{10,... | collective-permute-start | bytes 196616 | tf_op jit(solution)/shard_map/ppermute | solution.py:310
  130.6 10.7 %copy-start.30 = (bf16[8,32,384]{2,1,0:T(8,128)(2,1)}, bf16[8,32,384]{2,1,0:T(8,128)(2,1)S(1)}, u32[]{:S(2)}) copy-start(bf16[8,32,384]{2,1,0:T(8,128)(2,1)S(1)} %collective-permute-done.refs_1_) | copy-start | bytes 589828
  130.6 10.7 %collective-permute-start.15 = (bf16[8,32,128]{2,1,0:T(8,128)(2,1)S(1)}, bf16[8,32,128]{2,1,0:T(8,128)(2,1)S(1)}, u32[]{:S(2)}, u32[]{:S(2)}) collective-permute-start(bf16[8,32,128]{2,1,0:T(8,128)(2,1)S(1)} %get-tuple-element.77), channel_id=1, source_target_pairs={{0,3},{1,2},{2,1},{3,0},{4,7},{5,6},{6,5},{7,4},{8,11},{9,10},{10,... | collective-permute-start | bytes 196616 | tf_op jit(solution)/shard_map/ppermute | solution.py:310
  164.9 3.7 %collective-permute-start.18 = (bf16[16,48,1024]{2,1,0:T(8,128)(2,1)}, bf16[16,48,1024]{2,1,0:T(8,128)(2,1)S(1)}, u32[]{:S(2)}, u32[]{:S(2)}) collective-permute-start(bf16[16,48,1024]{2,1,0:T(8,128)(2,1)} %get-tuple-element.84), channel_id=1, source_target_pairs={{0,1},{1,0},{2,3},{3,2},{4,5},{5,4},{6,7},{7,6},{8,9},{9,8},{10,11... | collective-permute-start | bytes 4718600 | tf_op jit(solution)/shard_map/ppermute | solution.py:310
  165.2 5.6 %collective-permute-start.17 = (bf16[16,48,1024]{2,1,0:T(8,128)(2,1)}, bf16[16,48,1024]{2,1,0:T(8,128)(2,1)S(1)}, u32[]{:S(2)}, u32[]{:S(2)}) collective-permute-start(bf16[16,48,1024]{2,1,0:T(8,128)(2,1)} %get-tuple-element.82), channel_id=1, source_target_pairs={{0,1},{1,0},{2,3},{3,2},{4,5},{5,4},{6,7},{7,6},{8,9},{9,8},{10,11... | collective-permute-start | bytes 4718600 | tf_op jit(solution)/shard_map/ppermute | solution.py:310
  165.5 9.0 %collective-permute-start.16 = (bf16[16,32,1024]{2,1,0:T(8,128)(2,1)}, bf16[16,32,1024]{2,1,0:T(8,128)(2,1)S(1)}, u32[]{:S(2)}, u32[]{:S(2)}) collective-permute-start(bf16[16,32,1024]{2,1,0:T(8,128)(2,1)} %get-tuple-element.80), channel_id=1, source_target_pairs={{0,1},{1,0},{2,3},{3,2},{4,5},{5,4},{6,7},{7,6},{8,9},{9,8},{10,11... | collective-permute-start | bytes 3145736 | tf_op jit(solution)/shard_map/ppermute | solution.py:310
  171.8 19.8 %collective-permute-start.23 = (bf16[8,48,1024]{2,1,0:T(8,128)(2,1)S(1)}, bf16[8,48,1024]{2,1,0:T(8,128)(2,1)S(1)}, u32[]{:S(2)}, u32[]{:S(2)}) collective-permute-start(bf16[8,48,1024]{2,1,0:T(8,128)(2,1)S(1)} %get-tuple-element.86.refs_2_), channel_id=1, source_target_pairs={{0,2},{1,3},{2,0},{3,1},{4,6},{5,7},{6,4},{7,5},{8,10},{9,11},{10,... | collective-permute-start | bytes 2359304 | tf_op jit(solution)/shard_map/ppermute | solution.py:310
  172.4 21.4 %collective-permute-start.22 = (bf16[8,48,1024]{2,1,0:T(8,128)(2,1)S(1)}, bf16[8,48,1024]{2,1,0:T(8,128)(2,1)S(1)}, u32[]{:S(2)}, u32[]{:S(2)}) collective-permute-start(bf16[8,48,1024]{2,1,0:T(8,128)(2,1)S(1)} %get-tuple-element.85.refs_2_), channel_id=1, source_target_pairs={{0,4},{1,5},{2,6},{3,7},{4,0},{5,1},{6,2},{7,3},{8,12},{9,13},{10,... | collective-permute-start | bytes 2359304 | tf_op jit(solution)/shard_map/ppermute | solution.py:310
  174.7 13.4 %collective-permute-start.19 = (bf16[4,32,1024]{2,1,0:T(8,128)(2,1)S(1)}, bf16[4,32,1024]{2,1,0:T(8,128)(2,1)S(1)}, u32[]{:S(2)}, u32[]{:S(2)}) collective-permute-start(bf16[4,32,1024]{2,1,0:T(8,128)(2,1)S(1)} %get-tuple-element.88), channel_id=1, source_target_pairs={{0,8},{1,9},{2,10},{3,11},{4,12},{5,13},{6,14},{7,15},{8,0},{9,1},... | collective-permute-start | bytes 786440 | tf_op jit(solution)/shard_map/ppermute | solution.py:310
  176.3 17.6 %collective-permute-start.20 = (bf16[4,32,1024]{2,1,0:T(8,128)(2,1)S(1)}, bf16[4,32,1024]{2,1,0:T(8,128)(2,1)S(1)}, u32[]{:S(2)}, u32[]{:S(2)}) collective-permute-start(bf16[4,32,1024]{2,1,0:T(8,128)(2,1)S(1)} %get-tuple-element.89), channel_id=1, source_target_pairs={{0,16},{1,17},{2,18},{3,19},{4,20},{5,21},{6,22},{7,23},{8,24},{9,... | collective-permute-start | bytes 786440 | tf_op jit(solution)/shard_map/ppermute | solution.py:310
  191.8 13.6 %collective-permute-start.25 = (bf16[4,48,1024]{2,1,0:T(8,128)(2,1)S(1)}, bf16[4,48,1024]{2,1,0:T(8,128)(2,1)S(1)}, u32[]{:S(2)}, u32[]{:S(2)}) collective-permute-start(bf16[4,48,1024]{2,1,0:T(8,128)(2,1)S(1)} %get-tuple-element.93.refs_2_), channel_id=1, source_target_pairs={{0,4},{1,5},{2,6},{3,7},{4,0},{5,1},{6,2},{7,3},{8,12},{9,13},{10,... | collective-permute-start | bytes 1179656 | tf_op jit(solution)/shard_map/ppermute | solution.py:310
  194.0 11.3 %collective-permute-start.26 = (bf16[4,48,1024]{2,1,0:T(8,128)(2,1)S(1)}, bf16[4,48,1024]{2,1,0:T(8,128)(2,1)S(1)}, u32[]{:S(2)}, u32[]{:S(2)}) collective-permute-start(bf16[4,48,1024]{2,1,0:T(8,128)(2,1)S(1)} %get-tuple-element.94.refs_4_), channel_id=1, source_target_pairs={{0,2},{1,3},{2,0},{3,1},{4,6},{5,7},{6,4},{7,5},{8,10},{9,11},{10,... | collective-permute-start | bytes 1179656 | tf_op jit(solution)/shard_map/ppermute | solution.py:310
  194.6 9.0 %collective-permute-start.21 = (bf16[4,32,1024]{2,1,0:T(8,128)(2,1)S(1)}, bf16[4,32,1024]{2,1,0:T(8,128)(2,1)S(1)}, u32[]{:S(2)}, u32[]{:S(2)}) collective-permute-start(bf16[4,32,1024]{2,1,0:T(8,128)(2,1)S(1)} %get-tuple-element.90), channel_id=1, source_target_pairs={{0,24},{1,25},{2,26},{3,27},{4,28},{5,29},{6,30},{7,31},{8,16},{9,... | collective-permute-start | bytes 786440 | tf_op jit(solution)/shard_map/ppermute | solution.py:310
  203.8 9.3 %collective-permute-start.24 = (bf16[2,32,1024]{2,1,0:T(8,128)(2,1)S(1)}, bf16[2,32,1024]{2,1,0:T(8,128)(2,1)S(1)}, u32[]{:S(2)}, u32[]{:S(2)}) collective-permute-start(bf16[2,32,1024]{2,1,0:T(8,128)(2,1)S(1)} %get-tuple-element.96.refs_4_), channel_id=1, source_target_pairs={{0,2},{1,3},{2,0},{3,1},{4,6},{5,7},{6,4},{7,5},{8,10},{9,11},{10,... | collective-permute-start | bytes 393224 | tf_op jit(solution)/shard_map/ppermute | solution.py:310
  205.5 19.6 %collective-permute-start.29 = (bf16[1,96,1024]{2,1,0:T(8,128)(2,1)S(1)}, bf16[1,96,1024]{2,1,0:T(8,128)(2,1)S(1)}, u32[]{:S(2)}, u32[]{:S(2)}) collective-permute-start(bf16[1,96,1024]{2,1,0:T(8,128)(2,1)S(1)} %get-tuple-element.103), channel_id=1, source_target_pairs={{0,16},{1,17},{2,18},{3,19},{4,20},{5,21},{6,22},{7,23},{8,24},{9,... | collective-permute-start | bytes 589832 | tf_op jit(solution)/shard_map/ppermute | solution.py:310
  211.6 13.5 %collective-permute-start.30 = (bf16[1,96,1024]{2,1,0:T(8,128)(2,1)S(1)}, bf16[1,96,1024]{2,1,0:T(8,128)(2,1)S(1)}, u32[]{:S(2)}, u32[]{:S(2)}) collective-permute-start(bf16[1,96,1024]{2,1,0:T(8,128)(2,1)S(1)} %get-tuple-element.104), channel_id=1, source_target_pairs={{0,24},{1,25},{2,26},{3,27},{4,28},{5,29},{6,30},{7,31},{8,16},{9,... | collective-permute-start | bytes 589832 | tf_op jit(solution)/shard_map/ppermute | solution.py:310
  213.1 12.0 %collective-permute-start.28 = (bf16[1,96,1024]{2,1,0:T(8,128)(2,1)S(1)}, bf16[1,96,1024]{2,1,0:T(8,128)(2,1)S(1)}, u32[]{:S(2)}, u32[]{:S(2)}) collective-permute-start(bf16[1,96,1024]{2,1,0:T(8,128)(2,1)S(1)} %get-tuple-element.99.refs_2_), channel_id=1, source_target_pairs={{0,8},{1,9},{2,10},{3,11},{4,12},{5,13},{6,14},{7,15},{8,0},{9,1},... | collective-permute-start | bytes 589832 | tf_op jit(solution)/shard_map/ppermute | solution.py:310
  213.1 4.3 %collective-permute-start.27 = (bf16[1,32,1024]{2,1,0:T(8,128)(2,1)S(1)}, bf16[1,32,1024]{2,1,0:T(8,128)(2,1)S(1)}, u32[]{:S(2)}, u32[]{:S(2)}) collective-permute-start(bf16[1,32,1024]{2,1,0:T(8,128)(2,1)S(1)} %get-tuple-element.101), channel_id=1, source_target_pairs={{0,4},{1,5},{2,6},{3,7},{4,0},{5,1},{6,2},{7,3},{8,12},{9,13},{10,... | collective-permute-start | bytes 196616 | tf_op jit(solution)/shard_map/ppermute | solution.py:310
  (25 other events, 78.9 us)
Sparse Core Ops, SparseCore 0:
  30.6 51.6 all-gather.2

commit v4 on v3

--- a/solution.py
+++ b/solution.py
@@ -181,19 +181,52 @@
 
 def attend_kernel(parts, shards, heads, scale, devices, spans, turn, *refs):
     pieces, refs = refs[: parts * shards], refs[parts * shards :]
-    place, queries, cotangent, normed_hbm, weights, context = refs[:6]
-    results, refs = refs[6:12], refs[12:]
+    place, queries_hbm, cotangent_hbm, normed_hbm, weights = refs[:5]
+    context, keep_v, send_v, keep_p, send_p, keep_r, send_r = refs[5:12]
+    refs = refs[12:]
     key_rows, value_rows, scores, prob_grads, prob_rounds, score_grads = refs[:6]
     latents_t, query_grad, key_grad, value_grad, total_v, total_k, total_q = refs[6:13]
-    keep_v, send_v, keep_p, send_p, keep_r, send_r = staged = refs[13:19]
-    w_key, w_value, normed_t, weight_sem, normed_sem, out_sem = refs[19:]
-    nbr, tokens, _ = pieces[0].shape
+    w_key, w_value, normed_t, all_queries, all_cotangent = refs[13:18]
+    held_pieces, sems = refs[18 : 18 + parts], refs[18 + parts]
     step = pl.program_id(0)
+    _, nbr, tokens, _ = held_pieces[0].shape
+    nbr = nbr // spans
+    of_step = pl.ds(step * nbr, nbr)
+    span = all_queries.shape[0] // spans
+    of_span = pl.ds(pl.multiple_of(step * span, span), span)
+    queries, cotangent = all_queries.at[of_span], all_cotangent.at[of_span]
+    each = w_key.shape[0] // shards
+    skipped = weights.shape[1] - 2 * each
+
+    @pl.when(step == 0)
+    def _():
+        for j in range(parts):
+            for k in range(shards):
+                pltpu.make_async_copy(
+                    pieces[j * shards + k], held_pieces[j].at[k], sems.at[0]
+                ).start()
+        for which, held_weights in enumerate((w_key, w_value)):
+            for k in range(shards):
+                pltpu.make_async_copy(
+                    weights.at[k, pl.ds(skipped + which * each, each)],
+                    held_weights.at[pl.ds(k * each, each)],
+                    sems.at[1 + which],
+                ).start()
+        pltpu.make_async_copy(queries_hbm, all_queries, sems.at[3]).start()
+        pltpu.make_async_copy(cotangent_hbm, all_cotangent, sems.at[4]).start()
+        pltpu.make_async_copy(normed_hbm, normed_t, sems.at[5]).start()
+        for ref in held_pieces:
+            pltpu.make_async_copy(ref, ref, sems.at[0]).wait()
+        pltpu.make_async_copy(w_key, w_key, sems.at[1]).wait()
+        pltpu.make_async_copy(w_value, w_value, sems.at[2]).wait()
+        pltpu.make_async_copy(queries_hbm, all_queries, sems.at[3]).wait()
+        pltpu.make_async_copy(cotangent_hbm, all_cotangent, sems.at[4]).wait()
+
     rows = jnp.concatenate(
         [
             jnp.concatenate(
                 [
-                    pieces[j * shards + k][...].reshape(nbr * tokens, -1)
+                    held_pieces[j][k, of_step].reshape(nbr * tokens, -1)
                     for j in range(parts)
                 ],
                 axis=1,
@@ -203,26 +236,8 @@
         axis=0,
     )
     keys, latent = rows.shape
-    span, inner = queries.shape
+    inner = queries.shape[1]
     latents_t[step] = rows.T
-    each = w_key.shape[0] // shards
-    skipped = weights.shape[1] - 2 * each
-
-    @pl.when(step == 0)
-    def _():
-        pltpu.make_async_copy(normed_hbm, normed_t, normed_sem).start()
-        for which, held_weights in enumerate((w_key, w_value)):
-            for k in range(shards):
-                pltpu.make_async_copy(
-                    weights.at[k, pl.ds(skipped + which * each, each)],
-                    held_weights.at[pl.ds(k * each, each)],
-                    weight_sem.at[which],
-                ).start()
-        for which, held_weights in enumerate((w_key, w_value)):
-            pltpu.make_async_copy(
-                held_weights, held_weights, weight_sem.at[which]
-            ).wait()
-
     key_rows[...] = jnp.dot(rows, w_key[...], preferred_element_type=F32).astype(BF16)
     value_rows[...] = jnp.dot(rows, w_value[...], preferred_element_type=F32).astype(
         BF16
@@ -232,7 +247,6 @@
     nn = (((1,), (0,)), ((), ()))
     tn = (((0,), (0,)), ((), ()))
     of_keys = pl.ds(pl.multiple_of(step * keys, keys), keys)
-    of_span = pl.ds(pl.multiple_of(step * span, span), span)
 
     def at_head(h):
         return slice(h * span, (h + 1) * span), slice(h * HEAD_DIM, (h + 1) * HEAD_DIM)
@@ -266,44 +280,22 @@
         of_v, of_p, of_r = (0, keep_v, send_v), (1, keep_p, send_p), (2, keep_r, send_r)
         rows_k, rows_q = keep_v.shape[1], normed_t.shape[0] // devices
         shared = keep_p.shape[1] - rows_k
-
-        def write(first):
-            for n in (first, first + 1):
-                pltpu.make_async_copy(staged[n], results[n], out_sem.at[n]).start()
-
         for total, grad, target in ((total_v, value_grad, of_v), (total_k, key_grad, of_p)):
             total[:latent, :] = dot(across, grad[...], nn)
             total[latent:, :] = jnp.zeros((total.shape[0] - latent, inner), F32)
             place_blocks(
                 total, latent // devices, place, turn, range(devices // 2), [target + (0, 0, rows_k)]
             )
-            if target is of_v or not shared:
-                write(2 * target[0])
         targets = [of_r + (shared, 0, rows_q - shared)]
         if shared:
             targets.append(of_p + (0, rows_k, shared))
         tile = total_q.shape[1]
-        pltpu.make_async_copy(normed_hbm, normed_t, normed_sem).wait()
+        pltpu.make_async_copy(normed_hbm, normed_t, sems.at[5]).wait()
         for at in range(0, normed_t.shape[0], tile):
             part = total_q.at[at // tile % 2]
             part[...] = dot(normed_t[at : at + tile, :], query_grad[...], nn)
             pairs = range(at // rows_q // 2, (at + tile) // rows_q // 2)
             place_blocks(part, rows_q, place, turn, pairs, targets)
-        if shared:
-            write(2)
-        write(4)
-        for n in range(6):
-            pltpu.make_async_copy(staged[n], results[n], out_sem.at[n]).wait()
-
-
-def held(value, after):
-    return pl.pallas_call(
-        lambda *refs: None,
-        out_shape=jax.ShapeDtypeStruct(value.shape, value.dtype),
-        in_specs=[ANY] * (1 + len(after)),
-        out_specs=ANY,
-        input_output_aliases={0: 0},
-    )(value, *after)
 
 
 def swap(value, bit, devices):
@@ -361,9 +353,6 @@
             compiler_params=pltpu.CompilerParams(vmem_limit_bytes=58 << 20),
         )(ids, place, latent_cache, *lay, *after)
 
-    def send(rows):
-        return lax.all_to_all(rows, "dp", split_axis=0, concat_axis=0, tiled=True)
-
     def pick(arrived, width, after=()):
         picked = pl.pallas_call(
             functools.partial(
@@ -384,9 +373,9 @@
             for k, piece in enumerate(picked)
         ]
 
-    cut_0, cut_1, cut_2 = lane_cuts(latent, (3, 3, 1))
+    cut_0, cut_1 = lane_cuts(latent, (4, 3))
     rows_0, weights = serve(*cut_0, False, (w_query, w_key, w_value))
-    arrived_0 = send(rows_0)
+    arrived_0 = lax.all_to_all(rows_0, "dp", split_axis=0, concat_axis=0, tiled=True)
     weights = lax.all_gather(weights, "shard", axis=0)
     rows_1 = serve(*cut_1, True, (), [rows_0])
     arrived_1 = [
@@ -398,12 +387,8 @@
     query_sum = jnp.dot(normed, query_full, preferred_element_type=F32)
     queries = (query_sum * scale).astype(BF16)
     normed_t = normed.T
-    (rows_2,) = serve(*cut_2, False, (), [rows_1[0]])
-    rows_2 = held(rows_2, [arrived_0, *arrived_1[1:], queries, pieces_0[0]])
-    arrived_2 = send(rows_2)
-    pieces_1 = pick(arrived_1, cut_1[1])
-    pieces_2 = pick([arrived_2], cut_2[1], pieces_1[:1])
-    pieces = pieces_0 + pieces_1 + pieces_2
+    pieces_1 = pick(arrived_1, cut_1[1], [queries, normed_t, pieces_0[0]])
+    pieces = pieces_0 + pieces_1
 
     keys = nbr * shards * slice_tokens
     width_q = tokens.shape[1]
@@ -444,12 +429,8 @@
         ),
         grid=(spans,),
         out_shape=[jax.ShapeDtypeStruct((spans * span, inner), BF16)] + blocks,
-        in_specs=[
-            pl.BlockSpec((nbr, slice_tokens, piece.shape[2]), lambda c: (c, 0, 0))
-            for piece in pieces
-        ]
-        + [SMEM, by_span, by_span, ANY, ANY],
-        out_specs=[by_span] + [ANY] * len(blocks),
+        in_specs=[HBM] * len(pieces) + [SMEM] + [HBM] * 4,
+        out_specs=[by_span] + [VMEM] * len(blocks),
         scratch_shapes=[pltpu.VMEM((keys, inner), BF16)] * 2
         + [pltpu.VMEM((heads * span, keys), F32)] * 2
         + [pltpu.VMEM((heads * span, keys), BF16)] * 2
@@ -460,15 +441,15 @@
         + [pltpu.VMEM((spans * keys, inner), BF16)] * 2
         + [pltpu.VMEM((latent + spare, inner), F32)] * 2
         + [pltpu.VMEM((2, 8 * width_q // devices, inner), F32)]
-        + [pltpu.VMEM(block.shape, BF16) for block in blocks]
         + [pltpu.VMEM((latent, inner), BF16)] * 2
+        + [pltpu.VMEM(normed_t.shape, BF16)]
+        + [pltpu.VMEM(queries.shape, BF16)] * 2
         + [
-            pltpu.VMEM(normed_t.shape, BF16),
-            pltpu.SemaphoreType.DMA((2,)),
-            pltpu.SemaphoreType.DMA,
-            pltpu.SemaphoreType.DMA((6,)),
-        ],
-        compiler_params=pltpu.CompilerParams(vmem_limit_bytes=58 << 20),
+            pltpu.VMEM((shards, *piece.shape), BF16)
+            for piece in pieces[:: shards]
+        ]
+        + [pltpu.SemaphoreType.DMA((6,))],
+        compiler_params=pltpu.CompilerParams(vmem_limit_bytes=40 << 20),
         cost_estimate=pl.CostEstimate(
             flops=2 * inner * (4 * spans * keys * (latent + 2 * span) + tokens.size),
             bytes_accessed=12 * (2 * latent + width_q) * inner,

time: 234 us -> 215 us (0.919)
  waiting for transfers between devices: 84.3 us -> 97.8 us
  starting transfers between devices: 61.5 us -> 48.8 us
  Pallas kernels: 52 us -> 40 us
  local copies, waits for them, and re-layouts: 15 us -> 9.29 us
    all_to_all x2 -> x1, waiting for transfers between devices: 21.3 us -> 40.3 us  [body(): lax.all_to_all(rows_0, 'dp', split_axis=0, concat_axis=0, tiled=True)]
    all_to_all x2 -> x1, starting transfers between devices: 14 us -> 3.61 us  [body(): lax.all_to_all(rows_0, 'dp', split_axis=0, concat_axis=0, tiled=True)]
    pallas_call x3 -> x2, Pallas kernels: 18.4 us -> 11.6 us  [serve(): pl.pallas_call(functools.partial(serve_kernel, owners, slots, owned, star...]
    unnamed x78 -> x32, local copies, waits for them, and re-layouts: 11.5 us -> 5.8 us
    all_gather x1, waiting for transfers between devices: 5.67 us -> 0.01 us  [body(): weights = lax.all_gather(weights, 'shard', axis=0)]
    pallas_call x1, Pallas kernels: 22.9 us -> 19.8 us  [body(): pl.pallas_call(functools.partial(attend_kernel, len(pieces) // shards, sh...]
    ppermute x31 -> x28, starting transfers between devices: 40.2 us -> 37.9 us  [swap(): return lax.ppermute(value, AXES, [(i, i ^ bit) for i in range(devices)])]
    pallas_call x3 -> x2, Pallas kernels: 8.18 us -> 6.12 us  [pick(): pl.pallas_call(functools.partial(pick_kernel, owners, slots, shards, owne...]
  transfers between devices with their start and end apart: 35 -> 31, of which waited for: 19 -> 17; matrix products, arithmetic and copies ran while one was open for 4% -> 4% of each run, Pallas kernels for 9% -> 6%
where the time goes in v4:
time: 215 us; the launch traced here: 214 us
  waiting for transfers between devices  97.8 us (45%)
  starting transfers between devices  48.8 us (23%)
  Pallas kernels  40 us (19%)
  between operations  14.3 us (7%)
  local copies, waits for them, and re-layouts  9.29 us (4%)
  other arithmetic  2.44 us (1%)
    ppermute x28, waiting for transfers between devices, swap(): return lax.ppermute(value, AXES, [(i, i ^ bit) for i in range(devices)])  51.1 us
    all_to_all x1, waiting for transfers between devices, body(): lax.all_to_all(rows_0, 'dp', split_axis=0, concat_axis=0, tiled=True)  40.3 us
    ppermute x28, starting transfers between devices, swap(): return lax.ppermute(value, AXES, [(i, i ^ bit) for i in range(devices)])  37.9 us
    pallas_call x1, Pallas kernels, body(): pl.pallas_call(functools.partial(attend_kernel, len(pieces) // shards, sh...  19.8 us
    pallas_call x2, Pallas kernels, serve(): pl.pallas_call(functools.partial(serve_kernel, owners, slots, owned, star...  11.6 us
    all_to_all x1, starting transfers between devices, body(): lax.all_to_all(jnp.broadcast_to(nbr_ids.reshape(1, each), (devices, each)...  7.3 us
    all_to_all x1, waiting for transfers between devices, body(): lax.all_to_all(jnp.broadcast_to(nbr_ids.reshape(1, each), (devices, each)...  6.38 us
    pallas_call x2, Pallas kernels, pick(): pl.pallas_call(functools.partial(pick_kernel, owners, slots, shards, owne...  6.12 us
  transfers between devices with their start and end apart: 31, of which 17 were waited for; matrix products, arithmetic and copies ran while one was open for 4% of the time, Pallas kernels for 6%

profile of v4, /device:TPU:0, one launch (start us, length us, event | category | flops | bytes accessed | tf_op | source)
XLA Modules:
  0.0 213.9 jit_solution(17262862922743053375)
XLA Ops:
  7.2 0.8 copy.15
  8.0 0.6 broadcast_in_dim.9
  8.6 7.3 %all-to-all-start = ((s32[32,1,8]{2,1,0:T(1,128)}), s32[32,1,8]{2,1,0:T(1,128)S(1)}, u32[]{:S(2)}, u32[]{:S(2)}) async-start(s32[32,1,8]{2,1,0:T(1,128)} %broadcast_in_dim.9), calls=%async_computation | async-start | bytes 32768 | tf_op jit(solution)/shard_map/all_to_all | solution.py:320
  16.0 0.6 pad_add_fusion.place.refs_8_
  16.6 6.4 %all-to-all-done = s32[32,1,8]{2,1,0:T(1,128)S(1)} async-done(((s32[32,1,8]{2,1,0:T(1,128)}), s32[32,1,8]{2,1,0:T(1,128)S(1)}, u32[]{:S(2)}, u32[]{:S(2)}) %all-to-all-start) | async-done | bytes 1056 | tf_op jit(solution)/shard_map/all_to_all | solution.py:320
  23.6 6.3 %shard_map.102 = (bf16[64,32,512]{2,1,0:T(8,128)(2,1)}, bf16[960,1024]{1,0:T(8,128)(2,1)}) custom-call(s32[32,8]{1,0:T(8,128)} %bitcast.9, s32[3]{0:T(128)} %pad_add_fusion.place.refs_8_, bf16[128,32,896]{2,1,0:T(8,128)(2,1)} %cache.3, bf16[512,1024]{1,0:T(8,128)(2,1)} %rest_0_.1, bf16[224,1024]{1,0:T(8,128)(2,1)} %rest_1_.1, bf16[224,1024]{1,0:T(8,128)(2,1)} %rest_2_.1), custom_call_target="tpu_custom_call" | custom-call | tf_op jit(solution)/shard_map/pallas_call | solution.py:342
  30.0 3.6 %all-to-all-start.1 = ((bf16[64,32,512]{2,1,0:T(8,128)(2,1)}), bf16[64,32,512]{2,1,0:T(8,128)(2,1)S(1)}, u32[]{:S(2)}, u32[]{:S(2)}) async-start(bf16[64,32,512]{2,1,0:T(8,128)(2,1)} %get-tuple-element.52.rest_0_), calls=%async_computation.1 | async-start | bytes 4194304 | tf_op jit(solution)/shard_map/all_to_all | solution.py:378
  33.6 1.6 copy.16
  35.5 0.7 copy-done.11
  36.2 5.3 %shard_map.104 = (bf16[8,32,384]{2,1,0:T(8,128)(2,1)}, bf16[8,32,384]{2,1,0:T(8,128)(2,1)}, bf16[8,32,384]{2,1,0:T(8,128)(2,1)}, bf16[8,32,384]{2,1,0:T(8,128)(2...) custom-call(s32[32,8]{1,0:T(8,128)} %bitcast.10, ...), custom_call_target="tpu_custom_call" | custom-call | tf_op jit(solution)/shard_map/pallas_call | solution.py:342
  41.5 2.5 %collective-permute-start.3 = (bf16[8,32,384]{2,1,0:T(8,128)(2,1)}, bf16[8,32,384]{2,1,0:T(8,128)(2,1)}, u32[]{:S(2)}, u32[]{:S(2)}) collective-permute-start(bf16[8,32,384]{2,1,0:T(8,128)(2,1)} %get-tuple-element.58), channel_id=1, source_target_pairs={{0,4},{1,5},{2,6},{3,7},{4,0},{5,1},{6,2},{7,3},{8,12},{9,13},{10,... | collective-permute-start | bytes 589832 | tf_op jit(solution)/shard_map/ppermute | solution.py:302
  43.9 1.4 collective-permute-start.4
  45.8 2.7 %collective-permute-start.6 = (bf16[8,32,384]{2,1,0:T(8,128)(2,1)}, bf16[8,32,384]{2,1,0:T(8,128)(2,1)}, u32[]{:S(2)}, u32[]{:S(2)}) collective-permute-start(bf16[8,32,384]{2,1,0:T(8,128)(2,1)} %get-tuple-element.61), channel_id=1, source_target_pairs={{0,16},{1,17},{2,18},{3,19},{4,20},{5,21},{6,22},{7,23},{8,24},{9,... | collective-permute-start | bytes 589832 | tf_op jit(solution)/shard_map/ppermute | solution.py:302
  48.5 1.3 collective-permute-start.7
  49.8 1.5 fusion.3.rest_9_.refs_11_
  51.3 40.3 %all-to-all-done.1.rest_0_ = bf16[64,32,512]{2,1,0:T(8,128)(2,1)S(1)} async-done(((bf16[64,32,512]{2,1,0:T(8,128)(2,1)}), bf16[64,32,512]{2,1,0:T(8,128)(2,1)S(1)}, u32[]{:S(2)}, u32[]{:S(2)}) %all-to-all-start.1) | async-done | bytes 2097184 | tf_op jit(solution)/shard_map/all_to_all | solution.py:378
  91.6 2.7 %shard_map.103 = (bf16[8,32,512]{2,1,0:T(8,128)(2,1)S(1)}, bf16[8,32,512]{2,1,0:T(8,128)(2,1)S(1)}, bf16[8,32,512]{2,1,0:T(8,128)(2,1)S(1)}, bf16[8,32,512]{2,1,0:T(8,128)(2,1)S(1)}) custom-call(s32[32,8]{1,0:T(8,128)S(1)} %bitcast.11, s32[3]{0:T(128)S(1)} %copy-done.3, bf16[64,32,512]{2,1,0:T(8,128)(2,1)S(1)} %all-to-all-done.1.rest_0_), custom_call_target="tpu_custom_call" | custom-call | tf_op jit(solution)/shard_map/pallas_call | solution.py:357
  94.3 0.7 copy-done.5
  95.0 0.7 copy-done.7
  95.7 0.7 copy-done.9
  96.5 2.8 %slice.4 = bf16[4,512,1024]{2,1,0:T(8,128)(2,1)S(1)} slice(bf16[4,960,1024]{2,1,0:T(8,128)(2,1)} %bitcast.14), slice={[0:4], [0:512], [0:1024]} | slice | bytes 8388608 | tf_op jit(solution)/shard_map/slice | solution.py:386
  99.3 1.4 collective-permute-start.8
  100.7 3.8 %collective-permute-start.9 = (bf16[8,32,384]{2,1,0:T(8,128)(2,1)S(1)}, bf16[8,32,384]{2,1,0:T(8,128)(2,1)S(1)}, u32[]{:S(2)}, u32[]{:S(2)}) collective-permute-start(bf16[8,32,384]{2,1,0:T(8,128)(2,1)S(1)} %copy-done.13), channel_id=1, source_target_pairs={{0,28},{1,29},{2,30},{3,31},{4,24},{5,25},{6,26},{7,27},{8,20},{9,... | collective-permute-start | bytes 589832 | tf_op jit(solution)/shard_map/ppermute | solution.py:302
  105.1 1.3 collective-permute-start.2
  106.3 1.3 fusion.2.rest_8_.refs_9_
  107.6 1.1 collective-permute-done.8.rest_6_
  108.8 3.2 %collective-permute-done.9.rest_7_ = bf16[8,32,384]{2,1,0:T(8,128)(2,1)S(1)} collective-permute-done((bf16[8,32,384]{2,1,0:T(8,128)(2,1)S(1)}, bf16[8,32,384]{2,1,0:T(8,128)(2,1)S(1)}, u32[]{:S(2)}, u32[]{:S(2)}) %collective-permute-start.9) | collective-permute-done | bytes 196640 | tf_op jit(solution)/shard_map/ppermute | solution.py:302
  111.9 3.4 %shard_map.105 = (bf16[8,32,384]{2,1,0:T(8,128)(2,1)S(1)}, bf16[8,32,384]{2,1,0:T(8,128)(2,1)S(1)}, bf16[8,32,384]{2,1,0:T(8,128)(2,1)S(1)}, bf16[8,32,384]{2,1,0:T(8,128)(2,1)S(1)}) custom-call(s32[32,8]{1,0:T(8,128)S(1)} %bitcast.12, s32[3]{0:T(128)S(1)} %copy-done.3, bf16[8,32,384]{2,1,0:T(8,128)(2,1)S(1)} %copy-done.2, ...), custom_call_target="tpu_custom_call" | custom-call | tf_op jit(solution)/shard_map/pallas_call | solution.py:357
  115.9 1.3 collective-permute-start.12
  117.3 1.1 collective-permute-done.2.refs_3_
  118.3 4.9 %collective-permute-done.11.refs_6_ = bf16[8,32,384]{2,1,0:T(8,128)(2,1)S(1)} collective-permute-done((bf16[8,32,384]{2,1,0:T(8,128)(2,1)S(1)}, bf16[8,32,384]{2,1,0:T(8,128)(2,1)S(1)}, u32[]{:S(2)}, u32[]{:S(2)}) %collective-permute-start.11) | collective-permute-done | bytes 196640 | tf_op jit(solution)/shard_map/ppermute | solution.py:302
  123.2 3.7 %collective-permute-done.12.refs_7_ = bf16[8,32,384]{2,1,0:T(8,128)(2,1)S(1)} collective-permute-done((bf16[8,32,384]{2,1,0:T(8,128)(2,1)S(1)}, bf16[8,32,384]{2,1,0:T(8,128)(2,1)S(1)}, u32[]{:S(2)}, u32[]{:S(2)}) %collective-permute-start.12) | collective-permute-done | bytes 196640 | tf_op jit(solution)/shard_map/ppermute | solution.py:302
  127.0 19.8 %shard_map.106 = (bf16[256,1024]{1,0:T(8,128)(2,1)}, bf16[16,32,1024]{2,1,0:T(8,128)(2,1)S(1)}, bf16[16,32,1024]{2,1,0:T(8,128)(2,1)S(1)}, bf16[16,48,1024]{2,1,...) custom-call(bf16[8,32,512]{2,1,0:T(8,128)(2,1)S(1)} %get-tuple-eleme, ...), custom_call_target="tpu_custom_call" | custom-call | flops 9663676416 | bytes 47185920 | tf_op jit(solution)/shard_map/pallas_call | solution.py:419
  147.5 2.8 %collective-permute-done.15.refs_1_ = bf16[16,48,1024]{2,1,0:T(8,128)(2,1)S(1)} collective-permute-done((bf16[16,48,1024]{2,1,0:T(8,128)(2,1)S(1)}, bf16[16,48,1024]{2,1,0:T(8,128)(2,1)S(1)}, u32[]{:S(2)}, u32[]{:S(2)}) %collective-permute-start.15) | collective-permute-done | bytes 1572896 | tf_op jit(solution)/shard_map/ppermute | solution.py:302
  150.7 1.8 collective-permute-done.14.refs_1_
  154.3 5.7 %collective-permute-start.16 = (bf16[4,32,1024]{2,1,0:T(8,128)(2,1)S(1)}, bf16[4,32,1024]{2,1,0:T(8,128)(2,1)S(1)}, u32[]{:S(2)}, u32[]{:S(2)}) collective-permute-start(bf16[4,32,1024]{2,1,0:T(8,128)(2,1)S(1)} %get-tuple-element.80), channel_id=1, source_target_pairs={{0,8},{1,9},{2,10},{3,11},{4,12},{5,13},{6,14},{7,15},{8,0},{9,1},... | collective-permute-start | bytes 786440 | tf_op jit(solution)/shard_map/ppermute | solution.py:302
  160.0 10.6 %collective-permute-done.16.refs_2_.refs_3_.refs_1_ = bf16[4,32,1024]{2,1,0:T(8,128)(2,1)S(1)} collective-permute-done((bf16[4,32,1024]{2,1,0:T(8,128)(2,1)S(1)}, bf16[4,32,1024]{2,1,0:T(8,128)(2,1)S(1)}, u32[]{:S(2)}, u32[]{:S(2)}) %collective-permute-start.16) | collective-permute-done | bytes 262176 | tf_op jit(solution)/shard_map/ppermute | solution.py:302
  170.6 2.0 collective-permute-done.20.refs_1_
  173.1 1.1 collective-permute-done.17.refs_4_.refs_2_
  174.4 1.5 collective-permute-start.23
  175.9 1.2 collective-permute-start.18
  177.2 7.0 %collective-permute-done.18.refs_3_ = bf16[4,32,1024]{2,1,0:T(8,128)(2,1)S(1)} collective-permute-done((bf16[4,32,1024]{2,1,0:T(8,128)(2,1)S(1)}, bf16[4,32,1024]{2,1,0:T(8,128)(2,1)S(1)}, u32[]{:S(2)}, u32[]{:S(2)}) %collective-permute-start.18) | collective-permute-done | bytes 262176 | tf_op jit(solution)/shard_map/ppermute | solution.py:302
  185.1 6.6 %collective-permute-start.26 = (bf16[1,96,1024]{2,1,0:T(8,128)(2,1)S(1)}, bf16[1,96,1024]{2,1,0:T(8,128)(2,1)S(1)}, u32[]{:S(2)}, u32[]{:S(2)}) collective-permute-start(bf16[1,96,1024]{2,1,0:T(8,128)(2,1)S(1)} %get-tuple-element.95), channel_id=1, source_target_pairs={{0,16},{1,17},{2,18},{3,19},{4,20},{5,21},{6,22},{7,23},{8,24},{9,... | collective-permute-start | bytes 589832 | tf_op jit(solution)/shard_map/ppermute | solution.py:302
  191.6 1.9 collective-permute-start.27
  193.6 1.3 collective-permute-start.24
  194.9 3.0 %collective-permute-done.24.refs_1_ = bf16[1,32,1024]{2,1,0:T(8,128)(2,1)S(1)} collective-permute-done((bf16[1,32,1024]{2,1,0:T(8,128)(2,1)S(1)}, bf16[1,32,1024]{2,1,0:T(8,128)(2,1)S(1)}, u32[]{:S(2)}, u32[]{:S(2)}) %collective-permute-start.24) | collective-permute-done | bytes 65568 | tf_op jit(solution)/shard_map/ppermute | solution.py:302
  197.9 7.9 %collective-permute-done.26.refs_4_ = bf16[1,96,1024]{2,1,0:T(8,128)(2,1)S(1)} collective-permute-done((bf16[1,96,1024]{2,1,0:T(8,128)(2,1)S(1)}, bf16[1,96,1024]{2,1,0:T(8,128)(2,1)S(1)}, u32[]{:S(2)}, u32[]{:S(2)}) %collective-permute-start.26) | collective-permute-done | bytes 196640 | tf_op jit(solution)/shard_map/ppermute | solution.py:302
  206.2 0.8 shard_map.115
  (69 shorter events, 7.7 us)
Async XLA Ops:
  8.6 14.4 %all-to-all-start = ((s32[32,1,8]{2,1,0:T(1,128)}), s32[32,1,8]{2,1,0:T(1,128)S(1)}, u32[]{:S(2)}, u32[]{:S(2)}) async-start(s32[32,1,8]{2,1,0:T(1,128)} %broadcast_in_dim.9), calls=%async_computation | async-start | bytes 32768 | tf_op jit(solution)/shard_map/all_to_all | solution.py:320
  15.9 80.5 %all-gather.3.cloned.1.call-start = ((), (), s32[]{:S(2)}) async-start(), calls=%async_computation.2 | async-start | bytes 9830400 | tf_op jit(solution)/shard_map/all_gather | solution.py:379
  23.0 0.6 copy-start
  30.0 61.6 %all-to-all-start.1 = ((bf16[64,32,512]{2,1,0:T(8,128)(2,1)}), bf16[64,32,512]{2,1,0:T(8,128)(2,1)S(1)}, u32[]{:S(2)}, u32[]{:S(2)}) async-start(bf16[64,32,512]{2,1,0:T(8,128)(2,1)} %get-tuple-element.52.rest_0_), calls=%async_computation.1 | async-start | bytes 4194304 | tf_op jit(solution)/shard_map/all_to_all | solution.py:378
  35.2 1.0 copy-start.11
  41.5 50.1 %copy-start.1 = (s32[32,1,8]{2,1,0:T(1,128)S(1)}, s32[32,1,8]{2,1,0:T(1,128)}, u32[]{:S(2)}) copy-start(s32[32,1,8]{2,1,0:T(1,128)} %copy-done) | copy-start | bytes 3076
  41.5 50.1 %copy-start.3 = (s32[3]{0:T(128)S(1)}, s32[3]{0:T(128)}, u32[]{:S(2)}) copy-start(s32[3]{0:T(128)} %pad_add_fusion.place.refs_8_) | copy-start | bytes 40
  41.5 57.8 %collective-permute-start.3 = (bf16[8,32,384]{2,1,0:T(8,128)(2,1)}, bf16[8,32,384]{2,1,0:T(8,128)(2,1)}, u32[]{:S(2)}, u32[]{:S(2)}) collective-permute-start(bf16[8,32,384]{2,1,0:T(8,128)(2,1)} %get-tuple-element.58), channel_id=1, source_target_pairs={{0,4},{1,5},{2,6},{3,7},{4,0},{5,1},{6,2},{7,3},{8,12},{9,13},{10,... | collective-permute-start | bytes 589832 | tf_op jit(solution)/shard_map/ppermute | solution.py:302
  43.9 56.7 %collective-permute-start.4 = (bf16[8,32,384]{2,1,0:T(8,128)(2,1)}, bf16[8,32,384]{2,1,0:T(8,128)(2,1)}, u32[]{:S(2)}, u32[]{:S(2)}) collective-permute-start(bf16[8,32,384]{2,1,0:T(8,128)(2,1)} %get-tuple-element.59), channel_id=1, source_target_pairs={{0,8},{1,9},{2,10},{3,11},{4,12},{5,13},{6,14},{7,15},{8,0},{9,1},... | collective-permute-start | bytes 589832 | tf_op jit(solution)/shard_map/ppermute | solution.py:302
  45.3 59.1 %collective-permute-start.5 = (bf16[8,32,384]{2,1,0:T(8,128)(2,1)}, bf16[8,32,384]{2,1,0:T(8,128)(2,1)}, u32[]{:S(2)}, u32[]{:S(2)}) collective-permute-start(bf16[8,32,384]{2,1,0:T(8,128)(2,1)} %get-tuple-element.60), channel_id=1, source_target_pairs={{0,12},{1,13},{2,14},{3,15},{4,8},{5,9},{6,10},{7,11},{8,4},{9,5},... | collective-permute-start | bytes 589832 | tf_op jit(solution)/shard_map/ppermute | solution.py:302
  45.8 58.6 %collective-permute-start.6 = (bf16[8,32,384]{2,1,0:T(8,128)(2,1)}, bf16[8,32,384]{2,1,0:T(8,128)(2,1)}, u32[]{:S(2)}, u32[]{:S(2)}) collective-permute-start(bf16[8,32,384]{2,1,0:T(8,128)(2,1)} %get-tuple-element.61), channel_id=1, source_target_pairs={{0,16},{1,17},{2,18},{3,19},{4,20},{5,21},{6,22},{7,23},{8,24},{9,... | collective-permute-start | bytes 589832 | tf_op jit(solution)/shard_map/ppermute | solution.py:302
  48.5 56.6 %collective-permute-start.7 = (bf16[8,32,384]{2,1,0:T(8,128)(2,1)}, bf16[8,32,384]{2,1,0:T(8,128)(2,1)}, u32[]{:S(2)}, u32[]{:S(2)}) collective-permute-start(bf16[8,32,384]{2,1,0:T(8,128)(2,1)} %get-tuple-element.62), channel_id=1, source_target_pairs={{0,20},{1,21},{2,22},{3,23},{4,16},{5,17},{6,18},{7,19},{8,28},{9,... | collective-permute-start | bytes 589832 | tf_op jit(solution)/shard_map/ppermute | solution.py:302
  94.3 0.7 copy-start.5
  95.0 0.7 copy-start.7
  95.7 0.7 copy-start.9
  96.4 2.8 %copy-start.14 = (bf16[8,32,384]{2,1,0:T(8,128)(2,1)S(1)}, bf16[8,32,384]{2,1,0:T(8,128)(2,1)}, u32[]{:S(2)}) copy-start(bf16[8,32,384]{2,1,0:T(8,128)(2,1)} %get-tuple-element.63) | copy-start | bytes 589828
  96.4 4.2 %copy-start.13 = (bf16[8,32,384]{2,1,0:T(8,128)(2,1)S(1)}, bf16[8,32,384]{2,1,0:T(8,128)(2,1)}, u32[]{:S(2)}) copy-start(bf16[8,32,384]{2,1,0:T(8,128)(2,1)} %get-tuple-element.64) | copy-start | bytes 589828
  96.4 8.0 %copy-start.10 = (bf16[8,32,512]{2,1,0:T(8,128)(2,1)S(1)}, bf16[8,32,512]{2,1,0:T(8,128)(2,1)}, u32[]{:S(2)}) copy-start(bf16[8,32,512]{2,1,0:T(8,128)(2,1)} %copy-done.9) | copy-start | bytes 786436
  96.4 8.0 %copy-start.8 = (bf16[8,32,512]{2,1,0:T(8,128)(2,1)S(1)}, bf16[8,32,512]{2,1,0:T(8,128)(2,1)}, u32[]{:S(2)}) copy-start(bf16[8,32,512]{2,1,0:T(8,128)(2,1)} %copy-done.7) | copy-start | bytes 786436
  96.5 8.6 %copy-start.6 = (bf16[8,32,512]{2,1,0:T(8,128)(2,1)S(1)}, bf16[8,32,512]{2,1,0:T(8,128)(2,1)}, u32[]{:S(2)}) copy-start(bf16[8,32,512]{2,1,0:T(8,128)(2,1)} %copy-done.5) | copy-start | bytes 786436
  96.5 9.9 %copy-start.12 = (bf16[256,2048]{0,1:T(8,128)(2,1)S(1)}, bf16[256,2048]{0,1:T(8,128)(2,1)}, u32[]{:S(2)}) copy-start(bf16[256,2048]{0,1:T(8,128)(2,1)} %copy-done.11) | copy-start | bytes 3145732
  99.3 9.5 %collective-permute-start.8 = (bf16[8,32,384]{2,1,0:T(8,128)(2,1)S(1)}, bf16[8,32,384]{2,1,0:T(8,128)(2,1)S(1)}, u32[]{:S(2)}, u32[]{:S(2)}) collective-permute-start(bf16[8,32,384]{2,1,0:T(8,128)(2,1)S(1)} %copy-done.14), channel_id=1, source_target_pairs={{0,24},{1,25},{2,26},{3,27},{4,28},{5,29},{6,30},{7,31},{8,16},{9,... | collective-permute-start | bytes 589832 | tf_op jit(solution)/shard_map/ppermute | solution.py:302
  100.7 11.3 %collective-permute-start.9 = (bf16[8,32,384]{2,1,0:T(8,128)(2,1)S(1)}, bf16[8,32,384]{2,1,0:T(8,128)(2,1)S(1)}, u32[]{:S(2)}, u32[]{:S(2)}) collective-permute-start(bf16[8,32,384]{2,1,0:T(8,128)(2,1)S(1)} %copy-done.13), channel_id=1, source_target_pairs={{0,28},{1,29},{2,30},{3,31},{4,24},{5,25},{6,26},{7,27},{8,20},{9,... | collective-permute-start | bytes 589832 | tf_op jit(solution)/shard_map/ppermute | solution.py:302
  104.4 11.5 %collective-permute-start = (bf16[8,32,512]{2,1,0:T(8,128)(2,1)S(1)}, bf16[8,32,512]{2,1,0:T(8,128)(2,1)S(1)}, u32[]{:S(2)}, u32[]{:S(2)}) collective-permute-start(bf16[8,32,512]{2,1,0:T(8,128)(2,1)S(1)} %copy-done.10), channel_id=1, source_target_pairs={{0,1},{1,0},{2,3},{3,2},{4,5},{5,4},{6,7},{7,6},{8,9},{9,8},{10,11... | collective-permute-start | bytes 786440 | tf_op jit(solution)/shard_map/ppermute | solution.py:302
  104.5 12.8 %collective-permute-start.1 = (bf16[8,32,512]{2,1,0:T(8,128)(2,1)S(1)}, bf16[8,32,512]{2,1,0:T(8,128)(2,1)S(1)}, u32[]{:S(2)}, u32[]{:S(2)}) collective-permute-start(bf16[8,32,512]{2,1,0:T(8,128)(2,1)S(1)} %copy-done.8), channel_id=1, source_target_pairs={{0,2},{1,3},{2,0},{3,1},{4,6},{5,7},{6,4},{7,5},{8,10},{9,11},{10,... | collective-permute-start | bytes 786440 | tf_op jit(solution)/shard_map/ppermute | solution.py:302
  105.1 13.3 %collective-permute-start.2 = (bf16[8,32,512]{2,1,0:T(8,128)(2,1)S(1)}, bf16[8,32,512]{2,1,0:T(8,128)(2,1)S(1)}, u32[]{:S(2)}, u32[]{:S(2)}) collective-permute-start(bf16[8,32,512]{2,1,0:T(8,128)(2,1)S(1)} %copy-done.6), channel_id=1, source_target_pairs={{0,3},{1,2},{2,1},{3,0},{4,7},{5,6},{6,5},{7,4},{8,11},{9,10},{10,... | collective-permute-start | bytes 786440 | tf_op jit(solution)/shard_map/ppermute | solution.py:302
  106.3 5.6 %copy-start.2 = (bf16[8,32,384]{2,1,0:T(8,128)(2,1)S(1)}, bf16[8,32,384]{2,1,0:T(8,128)(2,1)}, u32[]{:S(2)}) copy-start(bf16[8,32,384]{2,1,0:T(8,128)(2,1)} %get-tuple-element.57.rest_0_) | copy-start | bytes 589828
  107.6 19.4 %copy-start.4 = (bf16[256,1024]{1,0:T(8,128)(2,1)S(1)}, bf16[256,1024]{1,0:T(8,128)(2,1)}, u32[]{:S(2)}) copy-start(bf16[256,1024]{1,0:T(8,128)(2,1)} %refs_10_.1) | copy-start | bytes 1572868
  115.3 3.0 %collective-permute-start.10 = (bf16[8,32,384]{2,1,0:T(8,128)(2,1)S(1)}, bf16[8,32,384]{2,1,0:T(8,128)(2,1)S(1)}, u32[]{:S(2)}, u32[]{:S(2)}) collective-permute-start(bf16[8,32,384]{2,1,0:T(8,128)(2,1)S(1)} %get-tuple-element.67), channel_id=1, source_target_pairs={{0,1},{1,0},{2,3},{3,2},{4,5},{5,4},{6,7},{7,6},{8,9},{9,8},{10,11... | collective-permute-start | bytes 589832 | tf_op jit(solution)/shard_map/ppermute | solution.py:302
  115.4 7.9 %collective-permute-start.11 = (bf16[8,32,384]{2,1,0:T(8,128)(2,1)S(1)}, bf16[8,32,384]{2,1,0:T(8,128)(2,1)S(1)}, u32[]{:S(2)}, u32[]{:S(2)}) collective-permute-start(bf16[8,32,384]{2,1,0:T(8,128)(2,1)S(1)} %get-tuple-element.68), channel_id=1, source_target_pairs={{0,2},{1,3},{2,0},{3,1},{4,6},{5,7},{6,4},{7,5},{8,10},{9,11},{10,... | collective-permute-start | bytes 589832 | tf_op jit(solution)/shard_map/ppermute | solution.py:302
  115.9 11.1 %collective-permute-start.12 = (bf16[8,32,384]{2,1,0:T(8,128)(2,1)S(1)}, bf16[8,32,384]{2,1,0:T(8,128)(2,1)S(1)}, u32[]{:S(2)}, u32[]{:S(2)}) collective-permute-start(bf16[8,32,384]{2,1,0:T(8,128)(2,1)S(1)} %get-tuple-element.69), channel_id=1, source_target_pairs={{0,3},{1,2},{2,1},{3,0},{4,7},{5,6},{6,5},{7,4},{8,11},{9,10},{10,... | collective-permute-start | bytes 589832 | tf_op jit(solution)/shard_map/ppermute | solution.py:302
  146.8 3.5 %collective-permute-start.15 = (bf16[16,48,1024]{2,1,0:T(8,128)(2,1)S(1)}, bf16[16,48,1024]{2,1,0:T(8,128)(2,1)S(1)}, u32[]{:S(2)}, u32[]{:S(2)}) collective-permute-start(bf16[16,48,1024]{2,1,0:T(8,128)(2,1)S(1)} %get-tuple-element.76), channel_id=1, source_target_pairs={{0,1},{1,0},{2,3},{3,2},{4,5},{5,4},{6,7},{7,6},{8,9},{9,8},{10,11... | collective-permute-start | bytes 4718600 | tf_op jit(solution)/shard_map/ppermute | solution.py:302
  147.0 5.5 %collective-permute-start.14 = (bf16[16,48,1024]{2,1,0:T(8,128)(2,1)S(1)}, bf16[16,48,1024]{2,1,0:T(8,128)(2,1)S(1)}, u32[]{:S(2)}, u32[]{:S(2)}) collective-permute-start(bf16[16,48,1024]{2,1,0:T(8,128)(2,1)S(1)} %get-tuple-element.74), channel_id=1, source_target_pairs={{0,1},{1,0},{2,3},{3,2},{4,5},{5,4},{6,7},{7,6},{8,9},{9,8},{10,11... | collective-permute-start | bytes 4718600 | tf_op jit(solution)/shard_map/ppermute | solution.py:302
  147.4 6.6 %collective-permute-start.13 = (bf16[16,32,1024]{2,1,0:T(8,128)(2,1)S(1)}, bf16[16,32,1024]{2,1,0:T(8,128)(2,1)S(1)}, u32[]{:S(2)}, u32[]{:S(2)}) collective-permute-start(bf16[16,32,1024]{2,1,0:T(8,128)(2,1)S(1)} %get-tuple-element.72), channel_id=1, source_target_pairs={{0,1},{1,0},{2,3},{3,2},{4,5},{5,4},{6,7},{7,6},{8,9},{9,8},{10,11... | collective-permute-start | bytes 3145736 | tf_op jit(solution)/shard_map/ppermute | solution.py:302
  152.9 19.6 %collective-permute-start.20 = (bf16[8,48,1024]{2,1,0:T(8,128)(2,1)S(1)}, bf16[8,48,1024]{2,1,0:T(8,128)(2,1)S(1)}, u32[]{:S(2)}, u32[]{:S(2)}) collective-permute-start(bf16[8,48,1024]{2,1,0:T(8,128)(2,1)S(1)} %get-tuple-element.78.refs_2_), channel_id=1, source_target_pairs={{0,2},{1,3},{2,0},{3,1},{4,6},{5,7},{6,4},{7,5},{8,10},{9,11},{10,... | collective-permute-start | bytes 2359304 | tf_op jit(solution)/shard_map/ppermute | solution.py:302
  153.5 20.7 %collective-permute-start.19 = (bf16[8,48,1024]{2,1,0:T(8,128)(2,1)S(1)}, bf16[8,48,1024]{2,1,0:T(8,128)(2,1)S(1)}, u32[]{:S(2)}, u32[]{:S(2)}) collective-permute-start(bf16[8,48,1024]{2,1,0:T(8,128)(2,1)S(1)} %get-tuple-element.77.refs_2_), channel_id=1, source_target_pairs={{0,4},{1,5},{2,6},{3,7},{4,0},{5,1},{6,2},{7,3},{8,12},{9,13},{10,... | collective-permute-start | bytes 2359304 | tf_op jit(solution)/shard_map/ppermute | solution.py:302
  154.3 16.2 %collective-permute-start.16 = (bf16[4,32,1024]{2,1,0:T(8,128)(2,1)S(1)}, bf16[4,32,1024]{2,1,0:T(8,128)(2,1)S(1)}, u32[]{:S(2)}, u32[]{:S(2)}) collective-permute-start(bf16[4,32,1024]{2,1,0:T(8,128)(2,1)S(1)} %get-tuple-element.80), channel_id=1, source_target_pairs={{0,8},{1,9},{2,10},{3,11},{4,12},{5,13},{6,14},{7,15},{8,0},{9,1},... | collective-permute-start | bytes 786440 | tf_op jit(solution)/shard_map/ppermute | solution.py:302
  160.0 14.2 %collective-permute-start.17 = (bf16[4,32,1024]{2,1,0:T(8,128)(2,1)S(1)}, bf16[4,32,1024]{2,1,0:T(8,128)(2,1)S(1)}, u32[]{:S(2)}, u32[]{:S(2)}) collective-permute-start(bf16[4,32,1024]{2,1,0:T(8,128)(2,1)S(1)} %get-tuple-element.81), channel_id=1, source_target_pairs={{0,16},{1,17},{2,18},{3,19},{4,20},{5,21},{6,22},{7,23},{8,24},{9,... | collective-permute-start | bytes 786440 | tf_op jit(solution)/shard_map/ppermute | solution.py:302
  172.7 12.2 %collective-permute-start.22 = (bf16[4,48,1024]{2,1,0:T(8,128)(2,1)S(1)}, bf16[4,48,1024]{2,1,0:T(8,128)(2,1)S(1)}, u32[]{:S(2)}, u32[]{:S(2)}) collective-permute-start(bf16[4,48,1024]{2,1,0:T(8,128)(2,1)S(1)} %get-tuple-element.85.refs_2_), channel_id=1, source_target_pairs={{0,4},{1,5},{2,6},{3,7},{4,0},{5,1},{6,2},{7,3},{8,12},{9,13},{10,... | collective-permute-start | bytes 1179656 | tf_op jit(solution)/shard_map/ppermute | solution.py:302
  174.4 10.6 %collective-permute-start.23 = (bf16[4,48,1024]{2,1,0:T(8,128)(2,1)S(1)}, bf16[4,48,1024]{2,1,0:T(8,128)(2,1)S(1)}, u32[]{:S(2)}, u32[]{:S(2)}) collective-permute-start(bf16[4,48,1024]{2,1,0:T(8,128)(2,1)S(1)} %get-tuple-element.86.refs_4_), channel_id=1, source_target_pairs={{0,2},{1,3},{2,0},{3,1},{4,6},{5,7},{6,4},{7,5},{8,10},{9,11},{10,... | collective-permute-start | bytes 1179656 | tf_op jit(solution)/shard_map/ppermute | solution.py:302
  175.9 8.3 %collective-permute-start.18 = (bf16[4,32,1024]{2,1,0:T(8,128)(2,1)S(1)}, bf16[4,32,1024]{2,1,0:T(8,128)(2,1)S(1)}, u32[]{:S(2)}, u32[]{:S(2)}) collective-permute-start(bf16[4,32,1024]{2,1,0:T(8,128)(2,1)S(1)} %get-tuple-element.82), channel_id=1, source_target_pairs={{0,24},{1,25},{2,26},{3,27},{4,28},{5,29},{6,30},{7,31},{8,16},{9,... | collective-permute-start | bytes 786440 | tf_op jit(solution)/shard_map/ppermute | solution.py:302
  184.3 9.3 %collective-permute-start.21 = (bf16[2,32,1024]{2,1,0:T(8,128)(2,1)S(1)}, bf16[2,32,1024]{2,1,0:T(8,128)(2,1)S(1)}, u32[]{:S(2)}, u32[]{:S(2)}) collective-permute-start(bf16[2,32,1024]{2,1,0:T(8,128)(2,1)S(1)} %get-tuple-element.88.refs_4_), channel_id=1, source_target_pairs={{0,2},{1,3},{2,0},{3,1},{4,6},{5,7},{6,4},{7,5},{8,10},{9,11},{10,... | collective-permute-start | bytes 393224 | tf_op jit(solution)/shard_map/ppermute | solution.py:302
  185.1 20.8 %collective-permute-start.26 = (bf16[1,96,1024]{2,1,0:T(8,128)(2,1)S(1)}, bf16[1,96,1024]{2,1,0:T(8,128)(2,1)S(1)}, u32[]{:S(2)}, u32[]{:S(2)}) collective-permute-start(bf16[1,96,1024]{2,1,0:T(8,128)(2,1)S(1)} %get-tuple-element.95), channel_id=1, source_target_pairs={{0,16},{1,17},{2,18},{3,19},{4,20},{5,21},{6,22},{7,23},{8,24},{9,... | collective-permute-start | bytes 589832 | tf_op jit(solution)/shard_map/ppermute | solution.py:302
  191.6 14.2 %collective-permute-start.27 = (bf16[1,96,1024]{2,1,0:T(8,128)(2,1)S(1)}, bf16[1,96,1024]{2,1,0:T(8,128)(2,1)S(1)}, u32[]{:S(2)}, u32[]{:S(2)}) collective-permute-start(bf16[1,96,1024]{2,1,0:T(8,128)(2,1)S(1)} %get-tuple-element.96), channel_id=1, source_target_pairs={{0,24},{1,25},{2,26},{3,27},{4,28},{5,29},{6,30},{7,31},{8,16},{9,... | collective-permute-start | bytes 589832 | tf_op jit(solution)/shard_map/ppermute | solution.py:302
  193.6 12.7 %collective-permute-start.25 = (bf16[1,96,1024]{2,1,0:T(8,128)(2,1)S(1)}, bf16[1,96,1024]{2,1,0:T(8,128)(2,1)S(1)}, u32[]{:S(2)}, u32[]{:S(2)}) collective-permute-start(bf16[1,96,1024]{2,1,0:T(8,128)(2,1)S(1)} %get-tuple-element.91.refs_2_), channel_id=1, source_target_pairs={{0,8},{1,9},{2,10},{3,11},{4,12},{5,13},{6,14},{7,15},{8,0},{9,1},... | collective-permute-start | bytes 589832 | tf_op jit(solution)/shard_map/ppermute | solution.py:302
  193.6 4.3 %collective-permute-start.24 = (bf16[1,32,1024]{2,1,0:T(8,128)(2,1)S(1)}, bf16[1,32,1024]{2,1,0:T(8,128)(2,1)S(1)}, u32[]{:S(2)}, u32[]{:S(2)}) collective-permute-start(bf16[1,32,1024]{2,1,0:T(8,128)(2,1)S(1)} %get-tuple-element.93), channel_id=1, source_target_pairs={{0,4},{1,5},{2,6},{3,7},{4,0},{5,1},{6,2},{7,3},{8,12},{9,13},{10,... | collective-permute-start | bytes 196616 | tf_op jit(solution)/shard_map/ppermute | solution.py:302
Sparse Core Ops, SparseCore 0:
  30.1 52.5 all-gather.2

commit v5 on v4

--- a/solution.py
+++ b/solution.py
@@ -100,6 +100,18 @@
 
     for out in outs:
         pltpu.make_async_copy(out, out, sem).wait()
+
+
+def project_kernel(scale, normed, weights, out, held, sem):
+    parts = weights.shape[0]
+    rows = held.shape[0] // parts
+    for k in range(parts):
+        pltpu.make_async_copy(
+            weights.at[k, pl.ds(0, rows)], held.at[pl.ds(k * rows, rows)], sem
+        ).start()
+    pltpu.make_async_copy(held, held, sem).wait()
+    total = jnp.dot(normed[...], held[...], preferred_element_type=F32)
+    out[...] = (total * scale).astype(BF16)
 
 
 def place_blocks(total, rows, place, turn, pairs, targets):
@@ -383,9 +395,17 @@
         for k, part in enumerate(rows_1)
     ]
     pieces_0 = pick([arrived_0], cut_0[1])
-    query_full = weights[:, : heights[0]].reshape(-1, inner)
-    query_sum = jnp.dot(normed, query_full, preferred_element_type=F32)
-    queries = (query_sum * scale).astype(BF16)
+    queries = pl.pallas_call(
+        functools.partial(project_kernel, scale),
+        out_shape=jax.ShapeDtypeStruct((spans * span, inner), BF16),
+        in_specs=[VMEM, HBM],
+        out_specs=VMEM,
+        scratch_shapes=[
+            pltpu.VMEM((tokens.shape[1], inner), BF16),
+            pltpu.SemaphoreType.DMA,
+        ],
+        compiler_params=pltpu.CompilerParams(vmem_limit_bytes=16 << 20),
+    )(normed, weights)
     normed_t = normed.T
     pieces_1 = pick(arrived_1, cut_1[1], [queries, normed_t, pieces_0[0]])
     pieces = pieces_0 + pieces_1

time: 215 us -> 217 us (level)
  starting transfers between devices: 48.8 us -> 42.7 us
  waiting for transfers between devices: 97.8 us -> 103 us
  Pallas kernels: 40 us -> 42.9 us
    ppermute x28, starting transfers between devices: 37.9 us -> 31.7 us  [swap(): return lax.ppermute(value, AXES, [(i, i ^ bit) for i in range(devices)])]
    ppermute x28, waiting for transfers between devices: 51.1 us -> 55.8 us  [swap(): return lax.ppermute(value, AXES, [(i, i ^ bit) for i in range(devices)])]
    slice x1 -> x0, local copies, waits for them, and re-layouts: 2.78 us -> none  [body(): query_full = weights[:, :heights[0]].reshape(-1, inner)]
    unnamed x32 -> x18, local copies, waits for them, and re-layouts: 5.8 us -> 6.93 us
  transfers between devices with their start and end apart: 31 -> 31, of which waited for: 17 -> 14; matrix products, arithmetic and copies ran while one was open for 4% -> 3% of each run, Pallas kernels for 6% -> 7%
where the time goes in v5:
time: 217 us; the launch traced here: 215 us
  waiting for transfers between devices  103 us (47%)
  Pallas kernels  42.9 us (20%)
  starting transfers between devices  42.7 us (20%)
  between operations  14.3 us (7%)
  local copies, waits for them, and re-layouts  9.11 us (4%)
  other arithmetic  3.7 us (2%)
    ppermute x28, waiting for transfers between devices, swap(): return lax.ppermute(value, AXES, [(i, i ^ bit) for i in range(devices)])  55.8 us
    all_to_all x1, waiting for transfers between devices, body(): lax.all_to_all(rows_0, 'dp', split_axis=0, concat_axis=0, tiled=True)  40.6 us
    ppermute x28, starting transfers between devices, swap(): return lax.ppermute(value, AXES, [(i, i ^ bit) for i in range(devices)])  31.7 us
    pallas_call x1, Pallas kernels, body(): pl.pallas_call(functools.partial(attend_kernel, len(pieces) // shards, sh...  19.8 us
    pallas_call x2, Pallas kernels, serve(): pl.pallas_call(functools.partial(serve_kernel, owners, slots, owned, star...  12.3 us
    all_to_all x1, starting transfers between devices, body(): lax.all_to_all(jnp.broadcast_to(nbr_ids.reshape(1, each), (devices, each)...  7.3 us
    unnamed x18, local copies, waits for them, and re-layouts  6.93 us
    pallas_call x2, Pallas kernels, pick(): pl.pallas_call(functools.partial(pick_kernel, owners, slots, shards, owne...  6.67 us
  transfers between devices with their start and end apart: 31, of which 14 were waited for; matrix products, arithmetic and copies ran while one was open for 3% of the time, Pallas kernels for 7%

profile of v5, /device:TPU:0, one launch (start us, length us, event | category | flops | bytes accessed | tf_op | source)
XLA Modules:
  0.0 215.5 jit_solution(2406390060944397822)
XLA Ops:
  7.2 0.8 copy.17
  8.0 0.6 broadcast_in_dim.9
  8.6 7.3 %all-to-all-start = ((s32[32,1,8]{2,1,0:T(1,128)}), s32[32,1,8]{2,1,0:T(1,128)S(1)}, u32[]{:S(2)}, u32[]{:S(2)}) async-start(s32[32,1,8]{2,1,0:T(1,128)} %broadcast_in_dim.9), calls=%async_computation | async-start | bytes 32768 | tf_op jit(solution)/shard_map/all_to_all | solution.py:332
  16.0 0.6 pad_add_fusion.place.refs_8_
  16.6 6.4 %all-to-all-done = s32[32,1,8]{2,1,0:T(1,128)S(1)} async-done(((s32[32,1,8]{2,1,0:T(1,128)}), s32[32,1,8]{2,1,0:T(1,128)S(1)}, u32[]{:S(2)}, u32[]{:S(2)}) %all-to-all-start) | async-done | bytes 1056 | tf_op jit(solution)/shard_map/all_to_all | solution.py:332
  23.0 0.6 copy-done.1
  23.6 6.7 %shard_map.102 = (bf16[64,32,512]{2,1,0:T(8,128)(2,1)}, bf16[960,1024]{1,0:T(8,128)(2,1)}) custom-call(s32[32,8]{1,0:T(8,128)} %bitcast.9, s32[3]{0:T(128)} %pad_add_fusion.place.refs_8_, bf16[128,32,896]{2,1,0:T(8,128)(2,1)} %cache.3, bf16[512,1024]{1,0:T(8,128)(2,1)} %rest_0_.1, bf16[224,1024]{1,0:T(8,128)(2,1)} %rest_1_.1, bf16[224,1024]{1,0:T(8,128)(2,1)} %rest_2_.1), custom_call_target="tpu_custom_call" | custom-call | tf_op jit(solution)/shard_map/pallas_call | solution.py:354
  30.4 3.6 %all-to-all-start.1 = ((bf16[64,32,512]{2,1,0:T(8,128)(2,1)}), bf16[64,32,512]{2,1,0:T(8,128)(2,1)S(1)}, u32[]{:S(2)}, u32[]{:S(2)}) async-start(bf16[64,32,512]{2,1,0:T(8,128)(2,1)} %get-tuple-element.52.rest_0_), calls=%async_computation.1 | async-start | bytes 4194304 | tf_op jit(solution)/shard_map/all_to_all | solution.py:390
  34.0 1.6 copy.18
  35.9 0.7 copy-done.6
  36.7 5.6 %shard_map.104 = (bf16[8,32,384]{2,1,0:T(8,128)(2,1)}, bf16[8,32,384]{2,1,0:T(8,128)(2,1)}, bf16[8,32,384]{2,1,0:T(8,128)(2,1)}, bf16[8,32,384]{2,1,0:T(8,128)(2...) custom-call(s32[32,8]{1,0:T(8,128)} %bitcast.10, ...), custom_call_target="tpu_custom_call" | custom-call | tf_op jit(solution)/shard_map/pallas_call | solution.py:354
  42.3 0.8 collective-permute-start.3
  43.1 3.0 %collective-permute-start.4 = (bf16[8,32,384]{2,1,0:T(8,128)(2,1)}, bf16[8,32,384]{2,1,0:T(8,128)(2,1)}, u32[]{:S(2)}, u32[]{:S(2)}) collective-permute-start(bf16[8,32,384]{2,1,0:T(8,128)(2,1)} %get-tuple-element.59), channel_id=1, source_target_pairs={{0,8},{1,9},{2,10},{3,11},{4,12},{5,13},{6,14},{7,15},{8,0},{9,1},... | collective-permute-start | bytes 589832 | tf_op jit(solution)/shard_map/ppermute | solution.py:314
  46.1 2.6 %collective-permute-start.6 = (bf16[8,32,384]{2,1,0:T(8,128)(2,1)}, bf16[8,32,384]{2,1,0:T(8,128)(2,1)}, u32[]{:S(2)}, u32[]{:S(2)}) collective-permute-start(bf16[8,32,384]{2,1,0:T(8,128)(2,1)} %get-tuple-element.61), channel_id=1, source_target_pairs={{0,16},{1,17},{2,18},{3,19},{4,20},{5,21},{6,22},{7,23},{8,24},{9,... | collective-permute-start | bytes 589832 | tf_op jit(solution)/shard_map/ppermute | solution.py:314
  48.7 1.2 collective-permute-start.7
  49.9 1.5 fusion.2.rest_9_.refs_11_
  51.4 40.6 %all-to-all-done.1.rest_0_ = bf16[64,32,512]{2,1,0:T(8,128)(2,1)S(1)} async-done(((bf16[64,32,512]{2,1,0:T(8,128)(2,1)}), bf16[64,32,512]{2,1,0:T(8,128)(2,1)S(1)}, u32[]{:S(2)}, u32[]{:S(2)}) %all-to-all-start.1) | async-done | bytes 2097184 | tf_op jit(solution)/shard_map/all_to_all | solution.py:390
  92.0 3.6 %shard_map.103 = (bf16[8,32,512]{2,1,0:T(8,128)(2,1)S(1)}, bf16[8,32,512]{2,1,0:T(8,128)(2,1)}, bf16[8,32,512]{2,1,0:T(8,128)(2,1)}, bf16[8,32,512]{2,1,0:T(8,128)(2,1)}) custom-call(s32[32,8]{1,0:T(8,128)S(1)} %bitcast.11, s32[3]{0:T(128)S(1)} %copy-done.4, bf16[64,32,512]{2,1,0:T(8,128)(2,1)S(1)} %all-to-all-done.1.rest_0_), custom_call_target="tpu_custom_call" | custom-call | tf_op jit(solution)/shard_map/pallas_call | solution.py:369
  95.6 1.3 collective-permute-start.8
  97.0 3.8 %collective-permute-start.9 = (bf16[8,32,384]{2,1,0:T(8,128)(2,1)}, bf16[8,32,384]{2,1,0:T(8,128)(2,1)S(1)}, u32[]{:S(2)}, u32[]{:S(2)}) collective-permute-start(bf16[8,32,384]{2,1,0:T(8,128)(2,1)} %get-tuple-element.64), channel_id=1, source_target_pairs={{0,28},{1,29},{2,30},{3,31},{4,24},{5,25},{6,26},{7,27},{8,20},{9,... | collective-permute-start | bytes 589832 | tf_op jit(solution)/shard_map/ppermute | solution.py:314
  101.3 8.8 %collective-permute-done.7.rest_5_ = bf16[8,32,384]{2,1,0:T(8,128)(2,1)} collective-permute-done((bf16[8,32,384]{2,1,0:T(8,128)(2,1)}, bf16[8,32,384]{2,1,0:T(8,128)(2,1)}, u32[]{:S(2)}, u32[]{:S(2)}) %collective-permute-start.7) | collective-permute-done | bytes 196640 | tf_op jit(solution)/shard_map/ppermute | solution.py:314
  110.2 1.3 fusion.1
  111.5 1.5 copy.19.normed
  113.0 3.2 %copy-done = bf16[3840,1024]{1,0:T(8,128)(2,1)S(1)} copy-done((bf16[3840,1024]{1,0:T(8,128)(2,1)S(1)}, bf16[3840,1024]{1,0:T(8,128)(2,1)}, u32[]{:S(2)}) %copy-start) | copy-done | bytes 7864344
  116.2 1.5 shard_map.105.rest_8_.refs_9_
  117.8 3.1 %shard_map.106 = (bf16[8,32,384]{2,1,0:T(8,128)(2,1)S(1)}, bf16[8,32,384]{2,1,0:T(8,128)(2,1)S(1)}, bf16[8,32,384]{2,1,0:T(8,128)(2,1)S(1)}, bf16[8,32,384]{2,1,0:T(8,128)(2,1)S(1)}) custom-call(s32[32,8]{1,0:T(8,128)S(1)} %bitcast.12, s32[3]{0:T(128)S(1)} %copy-done.4, bf16[8,32,384]{2,1,0:T(8,128)(2,1)S(1)} %copy-done.3, ...), custom_call_target="tpu_custom_call" | custom-call | tf_op jit(solution)/shard_map/pallas_call | solution.py:369
  120.9 0.8 collective-permute-start.10
  121.7 1.4 collective-permute-start.11
  123.2 6.3 %collective-permute-done.11.refs_6_ = bf16[8,32,384]{2,1,0:T(8,128)(2,1)S(1)} collective-permute-done((bf16[8,32,384]{2,1,0:T(8,128)(2,1)S(1)}, bf16[8,32,384]{2,1,0:T(8,128)(2,1)S(1)}, u32[]{:S(2)}, u32[]{:S(2)}) %collective-permute-start.11) | collective-permute-done | bytes 196640 | tf_op jit(solution)/shard_map/ppermute | solution.py:314
  129.5 2.5 %collective-permute-done.12.refs_7_ = bf16[8,32,384]{2,1,0:T(8,128)(2,1)S(1)} collective-permute-done((bf16[8,32,384]{2,1,0:T(8,128)(2,1)S(1)}, bf16[8,32,384]{2,1,0:T(8,128)(2,1)S(1)}, u32[]{:S(2)}, u32[]{:S(2)}) %collective-permute-start.12) | collective-permute-done | bytes 196640 | tf_op jit(solution)/shard_map/ppermute | solution.py:314
  131.9 19.8 %shard_map.107 = (bf16[256,1024]{1,0:T(8,128)(2,1)}, bf16[16,32,1024]{2,1,0:T(8,128)(2,1)S(1)}, bf16[16,32,1024]{2,1,0:T(8,128)(2,1)S(1)}, bf16[16,48,1024]{2,1,...) custom-call(bf16[8,32,512]{2,1,0:T(8,128)(2,1)S(1)} %get-tuple-eleme, ...), custom_call_target="tpu_custom_call" | custom-call | flops 9663676416 | bytes 47185920 | tf_op jit(solution)/shard_map/pallas_call | solution.py:439
  151.7 0.8 collective-permute-start.15
  153.0 2.5 %collective-permute-done.15.refs_1_ = bf16[16,48,1024]{2,1,0:T(8,128)(2,1)S(1)} collective-permute-done((bf16[16,48,1024]{2,1,0:T(8,128)(2,1)S(1)}, bf16[16,48,1024]{2,1,0:T(8,128)(2,1)S(1)}, u32[]{:S(2)}, u32[]{:S(2)}) %collective-permute-start.15) | collective-permute-done | bytes 1572896 | tf_op jit(solution)/shard_map/ppermute | solution.py:314
  155.9 1.8 collective-permute-done.14.refs_1_
  158.2 1.4 collective-permute-start.20
  160.4 1.9 collective-permute-start.17
  162.3 10.4 %collective-permute-done.16.refs_2_.refs_3_.refs_1_ = bf16[4,32,1024]{2,1,0:T(8,128)(2,1)S(1)} collective-permute-done((bf16[4,32,1024]{2,1,0:T(8,128)(2,1)S(1)}, bf16[4,32,1024]{2,1,0:T(8,128)(2,1)S(1)}, u32[]{:S(2)}, u32[]{:S(2)}) %collective-permute-start.16) | collective-permute-done | bytes 262176 | tf_op jit(solution)/shard_map/ppermute | solution.py:314
  172.7 5.4 %collective-permute-done.20.refs_1_ = bf16[8,48,1024]{2,1,0:T(8,128)(2,1)S(1)} collective-permute-done((bf16[8,48,1024]{2,1,0:T(8,128)(2,1)S(1)}, bf16[8,48,1024]{2,1,0:T(8,128)(2,1)S(1)}, u32[]{:S(2)}, u32[]{:S(2)}) %collective-permute-start.20) | collective-permute-done | bytes 786464 | tf_op jit(solution)/shard_map/ppermute | solution.py:314
  179.3 1.0 collective-permute-start.23
  180.3 1.3 collective-permute-start.18
  181.7 7.8 %collective-permute-done.18.refs_3_ = bf16[4,32,1024]{2,1,0:T(8,128)(2,1)S(1)} collective-permute-done((bf16[4,32,1024]{2,1,0:T(8,128)(2,1)S(1)}, bf16[4,32,1024]{2,1,0:T(8,128)(2,1)S(1)}, u32[]{:S(2)}, u32[]{:S(2)}) %collective-permute-start.18) | collective-permute-done | bytes 262176 | tf_op jit(solution)/shard_map/ppermute | solution.py:314
  189.6 1.1 collective-permute-start.21
  190.8 3.9 %collective-permute-start.26 = (bf16[1,96,1024]{2,1,0:T(8,128)(2,1)S(1)}, bf16[1,96,1024]{2,1,0:T(8,128)(2,1)S(1)}, u32[]{:S(2)}, u32[]{:S(2)}) collective-permute-start(bf16[1,96,1024]{2,1,0:T(8,128)(2,1)S(1)} %get-tuple-element.95), channel_id=1, source_target_pairs={{0,16},{1,17},{2,18},{3,19},{4,20},{5,21},{6,22},{7,23},{8,24},{9,... | collective-permute-start | bytes 589832 | tf_op jit(solution)/shard_map/ppermute | solution.py:314
  194.8 1.5 collective-permute-start.27
  196.3 1.8 collective-permute-start.24
  198.1 2.6 %collective-permute-done.24.refs_1_ = bf16[1,32,1024]{2,1,0:T(8,128)(2,1)S(1)} collective-permute-done((bf16[1,32,1024]{2,1,0:T(8,128)(2,1)S(1)}, bf16[1,32,1024]{2,1,0:T(8,128)(2,1)S(1)}, u32[]{:S(2)}, u32[]{:S(2)}) %collective-permute-start.24) | collective-permute-done | bytes 65568 | tf_op jit(solution)/shard_map/ppermute | solution.py:314
  200.7 6.8 %collective-permute-done.26.refs_4_ = bf16[1,96,1024]{2,1,0:T(8,128)(2,1)S(1)} collective-permute-done((bf16[1,96,1024]{2,1,0:T(8,128)(2,1)S(1)}, bf16[1,96,1024]{2,1,0:T(8,128)(2,1)S(1)}, u32[]{:S(2)}, u32[]{:S(2)}) %collective-permute-start.26) | collective-permute-done | bytes 196640 | tf_op jit(solution)/shard_map/ppermute | solution.py:314
  207.8 0.8 shard_map.116
  (56 shorter events, 5.1 us)
Async XLA Ops:
  8.6 14.4 %all-to-all-start = ((s32[32,1,8]{2,1,0:T(1,128)}), s32[32,1,8]{2,1,0:T(1,128)S(1)}, u32[]{:S(2)}, u32[]{:S(2)}) async-start(s32[32,1,8]{2,1,0:T(1,128)} %broadcast_in_dim.9), calls=%async_computation | async-start | bytes 32768 | tf_op jit(solution)/shard_map/all_to_all | solution.py:332
  15.9 97.0 %all-gather.3.cloned.1.call-start = ((), (), s32[]{:S(2)}) async-start(), calls=%async_computation.2 | async-start | bytes 9830400 | tf_op jit(solution)/shard_map/all_gather | solution.py:391
  23.0 0.6 copy-start.1
  30.4 61.6 %all-to-all-start.1 = ((bf16[64,32,512]{2,1,0:T(8,128)(2,1)}), bf16[64,32,512]{2,1,0:T(8,128)(2,1)S(1)}, u32[]{:S(2)}, u32[]{:S(2)}) async-start(bf16[64,32,512]{2,1,0:T(8,128)(2,1)} %get-tuple-element.52.rest_0_), calls=%async_computation.1 | async-start | bytes 4194304 | tf_op jit(solution)/shard_map/all_to_all | solution.py:390
  35.6 1.1 copy-start.6
  42.3 49.7 %copy-start.2 = (s32[32,1,8]{2,1,0:T(1,128)S(1)}, s32[32,1,8]{2,1,0:T(1,128)}, u32[]{:S(2)}) copy-start(s32[32,1,8]{2,1,0:T(1,128)} %copy-done.1) | copy-start | bytes 3076
  42.3 49.7 %copy-start.4 = (s32[3]{0:T(128)S(1)}, s32[3]{0:T(128)}, u32[]{:S(2)}) copy-start(s32[3]{0:T(128)} %pad_add_fusion.place.refs_8_) | copy-start | bytes 40
  42.3 53.3 %collective-permute-start.3 = (bf16[8,32,384]{2,1,0:T(8,128)(2,1)}, bf16[8,32,384]{2,1,0:T(8,128)(2,1)}, u32[]{:S(2)}, u32[]{:S(2)}) collective-permute-start(bf16[8,32,384]{2,1,0:T(8,128)(2,1)} %get-tuple-element.58), channel_id=1, source_target_pairs={{0,4},{1,5},{2,6},{3,7},{4,0},{5,1},{6,2},{7,3},{8,12},{9,13},{10,... | collective-permute-start | bytes 589832 | tf_op jit(solution)/shard_map/ppermute | solution.py:314
  43.1 53.9 %collective-permute-start.4 = (bf16[8,32,384]{2,1,0:T(8,128)(2,1)}, bf16[8,32,384]{2,1,0:T(8,128)(2,1)}, u32[]{:S(2)}, u32[]{:S(2)}) collective-permute-start(bf16[8,32,384]{2,1,0:T(8,128)(2,1)} %get-tuple-element.59), channel_id=1, source_target_pairs={{0,8},{1,9},{2,10},{3,11},{4,12},{5,13},{6,14},{7,15},{8,0},{9,1},... | collective-permute-start | bytes 589832 | tf_op jit(solution)/shard_map/ppermute | solution.py:314
  46.1 54.7 %collective-permute-start.5 = (bf16[8,32,384]{2,1,0:T(8,128)(2,1)}, bf16[8,32,384]{2,1,0:T(8,128)(2,1)}, u32[]{:S(2)}, u32[]{:S(2)}) collective-permute-start(bf16[8,32,384]{2,1,0:T(8,128)(2,1)} %get-tuple-element.60), channel_id=1, source_target_pairs={{0,12},{1,13},{2,14},{3,15},{4,8},{5,9},{6,10},{7,11},{8,4},{9,5},... | collective-permute-start | bytes 589832 | tf_op jit(solution)/shard_map/ppermute | solution.py:314
  46.1 54.7 %collective-permute-start.6 = (bf16[8,32,384]{2,1,0:T(8,128)(2,1)}, bf16[8,32,384]{2,1,0:T(8,128)(2,1)}, u32[]{:S(2)}, u32[]{:S(2)}) collective-permute-start(bf16[8,32,384]{2,1,0:T(8,128)(2,1)} %get-tuple-element.61), channel_id=1, source_target_pairs={{0,16},{1,17},{2,18},{3,19},{4,20},{5,21},{6,22},{7,23},{8,24},{9,... | collective-permute-start | bytes 589832 | tf_op jit(solution)/shard_map/ppermute | solution.py:314
  48.7 61.5 %collective-permute-start.7 = (bf16[8,32,384]{2,1,0:T(8,128)(2,1)}, bf16[8,32,384]{2,1,0:T(8,128)(2,1)}, u32[]{:S(2)}, u32[]{:S(2)}) collective-permute-start(bf16[8,32,384]{2,1,0:T(8,128)(2,1)} %get-tuple-element.62), channel_id=1, source_target_pairs={{0,20},{1,21},{2,22},{3,23},{4,16},{5,17},{6,18},{7,19},{8,28},{9,... | collective-permute-start | bytes 589832 | tf_op jit(solution)/shard_map/ppermute | solution.py:314
  92.0 18.2 %copy-start.7 = (bf16[256,2048]{0,1:T(8,128)(2,1)S(1)}, bf16[256,2048]{0,1:T(8,128)(2,1)}, u32[]{:S(2)}) copy-start(bf16[256,2048]{0,1:T(8,128)(2,1)} %copy-done.6) | copy-start | bytes 3145732
  95.6 22.2 %collective-permute-start.8 = (bf16[8,32,384]{2,1,0:T(8,128)(2,1)}, bf16[8,32,384]{2,1,0:T(8,128)(2,1)S(1)}, u32[]{:S(2)}, u32[]{:S(2)}) collective-permute-start(bf16[8,32,384]{2,1,0:T(8,128)(2,1)} %get-tuple-element.63), channel_id=1, source_target_pairs={{0,24},{1,25},{2,26},{3,27},{4,28},{5,29},{6,30},{7,31},{8,16},{9,... | collective-permute-start | bytes 589832 | tf_op jit(solution)/shard_map/ppermute | solution.py:314
  97.0 20.8 %collective-permute-start.9 = (bf16[8,32,384]{2,1,0:T(8,128)(2,1)}, bf16[8,32,384]{2,1,0:T(8,128)(2,1)S(1)}, u32[]{:S(2)}, u32[]{:S(2)}) collective-permute-start(bf16[8,32,384]{2,1,0:T(8,128)(2,1)} %get-tuple-element.64), channel_id=1, source_target_pairs={{0,28},{1,29},{2,30},{3,31},{4,24},{5,25},{6,26},{7,27},{8,20},{9,... | collective-permute-start | bytes 589832 | tf_op jit(solution)/shard_map/ppermute | solution.py:314
  100.8 22.3 %collective-permute-start = (bf16[8,32,512]{2,1,0:T(8,128)(2,1)}, bf16[8,32,512]{2,1,0:T(8,128)(2,1)S(1)}, u32[]{:S(2)}, u32[]{:S(2)}) collective-permute-start(bf16[8,32,512]{2,1,0:T(8,128)(2,1)} %get-tuple-element.54), channel_id=1, source_target_pairs={{0,1},{1,0},{2,3},{3,2},{4,5},{5,4},{6,7},{7,6},{8,9},{9,8},{10,11... | collective-permute-start | bytes 786440 | tf_op jit(solution)/shard_map/ppermute | solution.py:314
  100.8 22.4 %collective-permute-start.1 = (bf16[8,32,512]{2,1,0:T(8,128)(2,1)}, bf16[8,32,512]{2,1,0:T(8,128)(2,1)S(1)}, u32[]{:S(2)}, u32[]{:S(2)}) collective-permute-start(bf16[8,32,512]{2,1,0:T(8,128)(2,1)} %get-tuple-element.55), channel_id=1, source_target_pairs={{0,2},{1,3},{2,0},{3,1},{4,6},{5,7},{6,4},{7,5},{8,10},{9,11},{10,... | collective-permute-start | bytes 786440 | tf_op jit(solution)/shard_map/ppermute | solution.py:314
  110.2 13.0 %collective-permute-start.2 = (bf16[8,32,512]{2,1,0:T(8,128)(2,1)}, bf16[8,32,512]{2,1,0:T(8,128)(2,1)}, u32[]{:S(2)}, u32[]{:S(2)}) collective-permute-start(bf16[8,32,512]{2,1,0:T(8,128)(2,1)} %get-tuple-element.56), channel_id=1, source_target_pairs={{0,3},{1,2},{2,1},{3,0},{4,7},{5,6},{6,5},{7,4},{8,11},{9,10},{10,... | collective-permute-start | bytes 786440 | tf_op jit(solution)/shard_map/ppermute | solution.py:314
  113.0 3.2 %copy-start = (bf16[3840,1024]{1,0:T(8,128)(2,1)S(1)}, bf16[3840,1024]{1,0:T(8,128)(2,1)}, u32[]{:S(2)}) copy-start(bf16[3840,1024]{1,0:T(8,128)(2,1)} %all-gather.3.cloned.1.call-done) | copy-start | bytes 23592964
  116.2 1.6 copy-start.3
  117.8 14.2 %copy-start.5 = (bf16[256,1024]{1,0:T(8,128)(2,1)S(1)}, bf16[256,1024]{1,0:T(8,128)(2,1)}, u32[]{:S(2)}) copy-start(bf16[256,1024]{1,0:T(8,128)(2,1)} %refs_10_.1) | copy-start | bytes 1572868
  120.9 2.3 %collective-permute-start.10 = (bf16[8,32,384]{2,1,0:T(8,128)(2,1)S(1)}, bf16[8,32,384]{2,1,0:T(8,128)(2,1)S(1)}, u32[]{:S(2)}, u32[]{:S(2)}) collective-permute-start(bf16[8,32,384]{2,1,0:T(8,128)(2,1)S(1)} %get-tuple-element.67), channel_id=1, source_target_pairs={{0,1},{1,0},{2,3},{3,2},{4,5},{5,4},{6,7},{7,6},{8,9},{9,8},{10,11... | collective-permute-start | bytes 589832 | tf_op jit(solution)/shard_map/ppermute | solution.py:314
  121.7 7.8 %collective-permute-start.11 = (bf16[8,32,384]{2,1,0:T(8,128)(2,1)S(1)}, bf16[8,32,384]{2,1,0:T(8,128)(2,1)S(1)}, u32[]{:S(2)}, u32[]{:S(2)}) collective-permute-start(bf16[8,32,384]{2,1,0:T(8,128)(2,1)S(1)} %get-tuple-element.68), channel_id=1, source_target_pairs={{0,2},{1,3},{2,0},{3,1},{4,6},{5,7},{6,4},{7,5},{8,10},{9,11},{10,... | collective-permute-start | bytes 589832 | tf_op jit(solution)/shard_map/ppermute | solution.py:314
  123.1 8.9 %collective-permute-start.12 = (bf16[8,32,384]{2,1,0:T(8,128)(2,1)S(1)}, bf16[8,32,384]{2,1,0:T(8,128)(2,1)S(1)}, u32[]{:S(2)}, u32[]{:S(2)}) collective-permute-start(bf16[8,32,384]{2,1,0:T(8,128)(2,1)S(1)} %get-tuple-element.69), channel_id=1, source_target_pairs={{0,3},{1,2},{2,1},{3,0},{4,7},{5,6},{6,5},{7,4},{8,11},{9,10},{10,... | collective-permute-start | bytes 589832 | tf_op jit(solution)/shard_map/ppermute | solution.py:314
  151.7 3.8 %collective-permute-start.15 = (bf16[16,48,1024]{2,1,0:T(8,128)(2,1)S(1)}, bf16[16,48,1024]{2,1,0:T(8,128)(2,1)S(1)}, u32[]{:S(2)}, u32[]{:S(2)}) collective-permute-start(bf16[16,48,1024]{2,1,0:T(8,128)(2,1)S(1)} %get-tuple-element.76), channel_id=1, source_target_pairs={{0,1},{1,0},{2,3},{3,2},{4,5},{5,4},{6,7},{7,6},{8,9},{9,8},{10,11... | collective-permute-start | bytes 4718600 | tf_op jit(solution)/shard_map/ppermute | solution.py:314
  152.5 5.3 %collective-permute-start.14 = (bf16[16,48,1024]{2,1,0:T(8,128)(2,1)S(1)}, bf16[16,48,1024]{2,1,0:T(8,128)(2,1)S(1)}, u32[]{:S(2)}, u32[]{:S(2)}) collective-permute-start(bf16[16,48,1024]{2,1,0:T(8,128)(2,1)S(1)} %get-tuple-element.74), channel_id=1, source_target_pairs={{0,1},{1,0},{2,3},{3,2},{4,5},{5,4},{6,7},{7,6},{8,9},{9,8},{10,11... | collective-permute-start | bytes 4718600 | tf_op jit(solution)/shard_map/ppermute | solution.py:314
  152.6 7.5 %collective-permute-start.13 = (bf16[16,32,1024]{2,1,0:T(8,128)(2,1)S(1)}, bf16[16,32,1024]{2,1,0:T(8,128)(2,1)S(1)}, u32[]{:S(2)}, u32[]{:S(2)}) collective-permute-start(bf16[16,32,1024]{2,1,0:T(8,128)(2,1)S(1)} %get-tuple-element.72), channel_id=1, source_target_pairs={{0,1},{1,0},{2,3},{3,2},{4,5},{5,4},{6,7},{7,6},{8,9},{9,8},{10,11... | collective-permute-start | bytes 3145736 | tf_op jit(solution)/shard_map/ppermute | solution.py:314
  158.2 19.9 %collective-permute-start.20 = (bf16[8,48,1024]{2,1,0:T(8,128)(2,1)S(1)}, bf16[8,48,1024]{2,1,0:T(8,128)(2,1)S(1)}, u32[]{:S(2)}, u32[]{:S(2)}) collective-permute-start(bf16[8,48,1024]{2,1,0:T(8,128)(2,1)S(1)} %get-tuple-element.78.refs_2_), channel_id=1, source_target_pairs={{0,2},{1,3},{2,0},{3,1},{4,6},{5,7},{6,4},{7,5},{8,10},{9,11},{10,... | collective-permute-start | bytes 2359304 | tf_op jit(solution)/shard_map/ppermute | solution.py:314
  159.6 19.5 %collective-permute-start.19 = (bf16[8,48,1024]{2,1,0:T(8,128)(2,1)S(1)}, bf16[8,48,1024]{2,1,0:T(8,128)(2,1)S(1)}, u32[]{:S(2)}, u32[]{:S(2)}) collective-permute-start(bf16[8,48,1024]{2,1,0:T(8,128)(2,1)S(1)} %get-tuple-element.77.refs_2_), channel_id=1, source_target_pairs={{0,4},{1,5},{2,6},{3,7},{4,0},{5,1},{6,2},{7,3},{8,12},{9,13},{10,... | collective-permute-start | bytes 2359304 | tf_op jit(solution)/shard_map/ppermute | solution.py:314
  160.3 12.4 %collective-permute-start.16 = (bf16[4,32,1024]{2,1,0:T(8,128)(2,1)S(1)}, bf16[4,32,1024]{2,1,0:T(8,128)(2,1)S(1)}, u32[]{:S(2)}, u32[]{:S(2)}) collective-permute-start(bf16[4,32,1024]{2,1,0:T(8,128)(2,1)S(1)} %get-tuple-element.80), channel_id=1, source_target_pairs={{0,8},{1,9},{2,10},{3,11},{4,12},{5,13},{6,14},{7,15},{8,0},{9,1},... | collective-permute-start | bytes 786440 | tf_op jit(solution)/shard_map/ppermute | solution.py:314
  160.4 18.1 %collective-permute-start.17 = (bf16[4,32,1024]{2,1,0:T(8,128)(2,1)S(1)}, bf16[4,32,1024]{2,1,0:T(8,128)(2,1)S(1)}, u32[]{:S(2)}, u32[]{:S(2)}) collective-permute-start(bf16[4,32,1024]{2,1,0:T(8,128)(2,1)S(1)} %get-tuple-element.81), channel_id=1, source_target_pairs={{0,16},{1,17},{2,18},{3,19},{4,20},{5,21},{6,22},{7,23},{8,24},{9,... | collective-permute-start | bytes 786440 | tf_op jit(solution)/shard_map/ppermute | solution.py:314
  178.2 12.4 %collective-permute-start.22 = (bf16[4,48,1024]{2,1,0:T(8,128)(2,1)S(1)}, bf16[4,48,1024]{2,1,0:T(8,128)(2,1)S(1)}, u32[]{:S(2)}, u32[]{:S(2)}) collective-permute-start(bf16[4,48,1024]{2,1,0:T(8,128)(2,1)S(1)} %get-tuple-element.85.refs_2_), channel_id=1, source_target_pairs={{0,4},{1,5},{2,6},{3,7},{4,0},{5,1},{6,2},{7,3},{8,12},{9,13},{10,... | collective-permute-start | bytes 1179656 | tf_op jit(solution)/shard_map/ppermute | solution.py:314
  179.3 11.4 %collective-permute-start.23 = (bf16[4,48,1024]{2,1,0:T(8,128)(2,1)S(1)}, bf16[4,48,1024]{2,1,0:T(8,128)(2,1)S(1)}, u32[]{:S(2)}, u32[]{:S(2)}) collective-permute-start(bf16[4,48,1024]{2,1,0:T(8,128)(2,1)S(1)} %get-tuple-element.86.refs_4_), channel_id=1, source_target_pairs={{0,2},{1,3},{2,0},{3,1},{4,6},{5,7},{6,4},{7,5},{8,10},{9,11},{10,... | collective-permute-start | bytes 1179656 | tf_op jit(solution)/shard_map/ppermute | solution.py:314
  180.3 9.1 %collective-permute-start.18 = (bf16[4,32,1024]{2,1,0:T(8,128)(2,1)S(1)}, bf16[4,32,1024]{2,1,0:T(8,128)(2,1)S(1)}, u32[]{:S(2)}, u32[]{:S(2)}) collective-permute-start(bf16[4,32,1024]{2,1,0:T(8,128)(2,1)S(1)} %get-tuple-element.82), channel_id=1, source_target_pairs={{0,24},{1,25},{2,26},{3,27},{4,28},{5,29},{6,30},{7,31},{8,16},{9,... | collective-permute-start | bytes 786440 | tf_op jit(solution)/shard_map/ppermute | solution.py:314
  189.6 6.8 %collective-permute-start.21 = (bf16[2,32,1024]{2,1,0:T(8,128)(2,1)S(1)}, bf16[2,32,1024]{2,1,0:T(8,128)(2,1)S(1)}, u32[]{:S(2)}, u32[]{:S(2)}) collective-permute-start(bf16[2,32,1024]{2,1,0:T(8,128)(2,1)S(1)} %get-tuple-element.88.refs_4_), channel_id=1, source_target_pairs={{0,2},{1,3},{2,0},{3,1},{4,6},{5,7},{6,4},{7,5},{8,10},{9,11},{10,... | collective-permute-start | bytes 393224 | tf_op jit(solution)/shard_map/ppermute | solution.py:314
  190.8 16.7 %collective-permute-start.26 = (bf16[1,96,1024]{2,1,0:T(8,128)(2,1)S(1)}, bf16[1,96,1024]{2,1,0:T(8,128)(2,1)S(1)}, u32[]{:S(2)}, u32[]{:S(2)}) collective-permute-start(bf16[1,96,1024]{2,1,0:T(8,128)(2,1)S(1)} %get-tuple-element.95), channel_id=1, source_target_pairs={{0,16},{1,17},{2,18},{3,19},{4,20},{5,21},{6,22},{7,23},{8,24},{9,... | collective-permute-start | bytes 589832 | tf_op jit(solution)/shard_map/ppermute | solution.py:314
  194.8 12.8 %collective-permute-start.27 = (bf16[1,96,1024]{2,1,0:T(8,128)(2,1)S(1)}, bf16[1,96,1024]{2,1,0:T(8,128)(2,1)S(1)}, u32[]{:S(2)}, u32[]{:S(2)}) collective-permute-start(bf16[1,96,1024]{2,1,0:T(8,128)(2,1)S(1)} %get-tuple-element.96), channel_id=1, source_target_pairs={{0,24},{1,25},{2,26},{3,27},{4,28},{5,29},{6,30},{7,31},{8,16},{9,... | collective-permute-start | bytes 589832 | tf_op jit(solution)/shard_map/ppermute | solution.py:314
  196.3 11.5 %collective-permute-start.25 = (bf16[1,96,1024]{2,1,0:T(8,128)(2,1)S(1)}, bf16[1,96,1024]{2,1,0:T(8,128)(2,1)S(1)}, u32[]{:S(2)}, u32[]{:S(2)}) collective-permute-start(bf16[1,96,1024]{2,1,0:T(8,128)(2,1)S(1)} %get-tuple-element.91.refs_2_), channel_id=1, source_target_pairs={{0,8},{1,9},{2,10},{3,11},{4,12},{5,13},{6,14},{7,15},{8,0},{9,1},... | collective-permute-start | bytes 589832 | tf_op jit(solution)/shard_map/ppermute | solution.py:314
  196.3 4.3 %collective-permute-start.24 = (bf16[1,32,1024]{2,1,0:T(8,128)(2,1)S(1)}, bf16[1,32,1024]{2,1,0:T(8,128)(2,1)S(1)}, u32[]{:S(2)}, u32[]{:S(2)}) collective-permute-start(bf16[1,32,1024]{2,1,0:T(8,128)(2,1)S(1)} %get-tuple-element.93), channel_id=1, source_target_pairs={{0,4},{1,5},{2,6},{3,7},{4,0},{5,1},{6,2},{7,3},{8,12},{9,13},{10,... | collective-permute-start | bytes 196616 | tf_op jit(solution)/shard_map/ppermute | solution.py:314
Sparse Core Ops, SparseCore 0:
  30.5 52.0 all-gather.2
